TPU v7x, 32 devices: a whole 2x2x4 slice. The times are simulated.
32 devices in a mesh: ens: 8 (over z, y), mp: 4 (over x, core).
Axes of the slice: x: 2, y: 2, z: 4, core: 2. Of those that a mesh axis runs over, the one named last changes fastest.
Arguments:
- tokens: bfloat16 [8, 2048, 1024], P('ens', 'mp'), may hold values from -6 to 6
- ln_gain: float32 [1024], replicated, may hold values from 0.5 to 1.5
- w_qkv: bfloat16 [1024, 3072], replicated, may hold values from -1 to 1
- w_out: bfloat16 [1024, 1024], replicated, may hold values from -0.75 to 0.75
- neighbours: int32 [4, 8192], P(None, 'mp'), may hold values from 0 to 2047, as said below
- edge_weights: float32 [4, 8192], P(None, 'mp'), may hold values from 0.2 to 1
- w_dec: bfloat16 [100, 1024], replicated, may hold values from -0.1875 to 0.1875
- truth: float32 [100, 8192], P(None, ('mp', 'ens')), may hold values from -6 to 6
Outputs:
- crps_score: float32 [100, 8192], P(None, ('mp', 'ens'))
Inputs may be any that keep to these rules, and one draw needn't show every extreme that they name: `neighbours`: the tokens of point g are among tokens g // 2048 * 512 to g // 2048 * 512 + 511 of its member.
All inputs are finite; a program needn't handle non-finite values.
Results may differ from a plain program's by a relative error of at most 0.0028.
The roundings to bfloat16 on the way count: a program that leaves them out, or rounds other values in their place, can miss the bound.
Values may be sent and summed in bfloat16 or wider, within the bound.
No kernel may reach another device: no remote copies, remote signals or barrier semaphores. Data moves between devices by JAX's collectives and lax.ppermute only.
A program may use at most 128 MiB of HBM per device.

v0:
```python
import jax
import jax.numpy as jnp
from jax import lax
from jax.sharding import PartitionSpec as P

HEADS = 16
NEIGH = 4
HALF = 512


ALPHA = 0.95


def padded_2(value, sides, width):
    for axis, dim in sides:
        count, length = (lax.axis_size(axis), value.shape[dim])
        up = [(i, (i + 1) % count) for i in range(count - 1)]
        down = [(j, i) for i, j in up]
        last = lax.slice_in_dim(value, length - width, length, axis=dim)
        initial = lax.slice_in_dim(value, 0, width, axis=dim)
        before = lax.ppermute(last, axis, up)
        after = lax.ppermute(initial, axis, down)
        value = jnp.concatenate([before, value, after], axis=dim)
    return value


def layer_norm(inputs, ln_gain):
    values = inputs.astype(jnp.float32)
    average = jnp.mean(values, axis=-1, keepdims=True)
    centred = values - average
    variance = jnp.mean(centred * centred, axis=-1, keepdims=True)
    return (centred * lax.rsqrt(variance + 1e-05) * ln_gain).astype(jnp.bfloat16)


def attend(queries, key_rows, value_rows, first_row, seq_tokens):
    count = queries.shape[1]
    head_dim = queries.shape[-1]
    scores = jnp.einsum(
        "mqhe,mkhe->mhqk", queries, key_rows, preferred_element_type=jnp.float32
    ) / jnp.sqrt(jnp.float32(head_dim))
    query_pos = first_row + jnp.arange(count, dtype=jnp.int32)
    key_pos = first_row - HALF + jnp.arange(count + 2 * HALF, dtype=jnp.int32)
    allowed = (
        (key_pos[None, :] >= 0)
        & (key_pos[None, :] < seq_tokens)
        & (jnp.abs(key_pos[None, :] - query_pos[:, None]) <= HALF)
    )
    scores = jnp.where(allowed[None, None], scores, -1e30)
    top = jnp.max(scores, axis=-1, keepdims=True)
    expo = jnp.exp(scores - top)
    weights = (expo / jnp.sum(expo, axis=-1, keepdims=True)).astype(jnp.bfloat16)
    context = jnp.einsum("mhqk,mkhe->mqhe", weights, value_rows, preferred_element_type=jnp.float32)
    return context.astype(jnp.bfloat16)


def grouped_attend(queries, key_rows, value_rows, first_row, seq_tokens):
    members_here, tok_rows, head_count, head_dim = queries.shape
    group_size = 4
    group_count = head_count // group_size

    def split_heads(rows):
        shaped = rows.reshape(rows.shape[0], rows.shape[1], group_count, group_size, head_dim)
        return jnp.moveaxis(shaped, 2, 0)

    def one_group(trio):
        return attend(trio[0], trio[1], trio[2], first_row, seq_tokens)

    outs = lax.map(
        one_group, (split_heads(queries), split_heads(key_rows), split_heads(value_rows))
    )
    return jnp.moveaxis(outs, 0, 2).reshape(members_here, tok_rows, head_count, head_dim)


def shards(tokens, ln_gain, w_qkv, w_out, neighbours, edge_weights, w_dec, truth):
    members_here, tok_rows, model_width = tokens.shape
    lane_count = lax.axis_size("mp")
    lane_index = lax.axis_index("mp")
    seq_tokens = tok_rows * lane_count
    head_count = HEADS
    head_dim = model_width // head_count
    normed = layer_norm(tokens, ln_gain)
    projected = jnp.einsum("mtd,de->mte", normed, w_qkv, preferred_element_type=jnp.float32).astype(
        jnp.bfloat16
    )
    queries = projected[..., :model_width].reshape(members_here, tok_rows, head_count, head_dim)
    padded = padded_2(projected[..., model_width:], (("mp", 1),), HALF)
    key_rows = padded[..., :model_width].reshape(
        members_here, tok_rows + 2 * HALF, head_count, head_dim
    )
    value_rows = padded[..., model_width:].reshape(
        members_here, tok_rows + 2 * HALF, head_count, head_dim
    )
    context = grouped_attend(queries, key_rows, value_rows, lane_index * tok_rows, seq_tokens)
    context = context.reshape(members_here, tok_rows, model_width)
    proj_out = jnp.einsum("mtd,de->mte", context, w_out, preferred_element_type=jnp.float32)
    processed = (tokens.astype(jnp.float32) + proj_out).astype(jnp.bfloat16)
    local_index = neighbours - lane_index * tok_rows
    hidden = jnp.zeros((members_here, neighbours.shape[1], model_width), jnp.float32)
    for slot_index in range(NEIGH):
        picked = jnp.take(processed, local_index[slot_index], axis=1)
        hidden = hidden + edge_weights[slot_index][None, :, None] * picked.astype(jnp.float32)
    decoded = jnp.einsum(
        "vd,mgd->mvg", w_dec, hidden.astype(jnp.bfloat16), preferred_element_type=jnp.float32
    ).astype(jnp.bfloat16)
    gathered = lax.all_to_all(decoded, "ens", split_axis=2, concat_axis=0, tiled=True).astype(
        jnp.float32
    )
    member_total = gathered.shape[0]
    skill_term = jnp.mean(jnp.abs(gathered - truth[None]), axis=0)
    spread = jnp.sum(jnp.abs(gathered[:, None] - gathered[None, :]), axis=(0, 1))
    coeff = ALPHA / (2.0 * member_total * (member_total - 1)) + (1.0 - ALPHA) / (
        2.0 * member_total * member_total
    )
    return skill_term - coeff * spread


def solution(mesh):
    in_specs = (
        P("ens", "mp", None),
        P(),
        P(),
        P(),
        P(None, "mp"),
        P(None, "mp"),
        P(),
        P(None, ("mp", "ens")),
    )
    out_specs = P(None, ("mp", "ens"))
    return jax.shard_map(shards, mesh=mesh, in_specs=in_specs, out_specs=out_specs, check_vma=False)
```

profile of v0, /device:TPU:1, one launch (start us, length us, event | category | flops | bytes accessed | tf_op | source)
XLA Modules:
  0.0 286.4 jit_solution(13690178693507065198)
XLA Ops:
  0.0 1.6 convert_reduce_fusion
  1.6 1.6 fusion.33
  3.2 6.6 %fusion.24 = bf16[1,512,3072]{2,1,0:T(8,128)(2,1)S(1)} fusion(bf16[1024,3072]{1,0:T(8,128)(2,1)} %param.14, bf16[1,512,1024]{2,1,0:T(8,128)(2,1)} %param.12, f32[1024]{0:T(1024)} %param.13, f32[512]{0:T(512)S(1)} %add_rsqrt_fusion, f32[512]{0:T(512)S(1)} %broadcast_multiply_fusion), kind=kOutput, calls=%fused_computation.42 | convolution fusion | flops 3225419776 | bytes 10493952 | tf_op jit(solution)/shard_map/mtd,de->mte/dot_general | solution.py:82
  9.9 1.5 slice.57
  11.4 4.5 %collective-permute-start = (bf16[1,512,2048]{2,1,0:T(8,128)(2,1)}, bf16[1,512,2048]{2,1,0:T(8,128)(2,1)}, u32[]{:S(2)}, u32[]{:S(2)}) collective-permute-start(bf16[1,512,2048]{2,1,0:T(8,128)(2,1)} %slice.57), channel_id=1, source_target_pairs={{0,1},{1,2},{2,3},{4,5},{5,6},{6,7},{8,9},{9,10},{10,11},{12,13},{... | collective-permute-start | bytes 6291464 | tf_op jit(solution)/shard_map/ppermute | solution.py:21
  15.9 2.1 collective-permute-start.1
  18.1 1.1 slice.59
  19.1 1.5 copy.42
  21.9 0.6 fusion.47
  23.6 0.6 fusion.51
  24.3 15.0 %collective-permute-done = bf16[1,512,2048]{2,1,0:T(8,128)(2,1)} collective-permute-done((bf16[1,512,2048]{2,1,0:T(8,128)(2,1)}, bf16[1,512,2048]{2,1,0:T(8,128)(2,1)}, u32[]{:S(2)}, u32[]{:S(2)}) %collective-permute-start) | collective-permute-done | bytes 2097184 | tf_op jit(solution)/shard_map/ppermute | solution.py:21
  39.2 4.4 %collective-permute-done.1 = bf16[1,512,2048]{2,1,0:T(8,128)(2,1)} collective-permute-done((bf16[1,512,2048]{2,1,0:T(8,128)(2,1)}, bf16[1,512,2048]{2,1,0:T(8,128)(2,1)}, u32[]{:S(2)}, u32[]{:S(2)}) %collective-permute-start.1) | collective-permute-done | bytes 2097184 | tf_op jit(solution)/shard_map/ppermute | solution.py:22
  43.6 3.8 %pad_maximum_fusion = bf16[1,1536,2048]{2,1,0:T(8,128)(2,1)S(1)} fusion(bf16[1,512,2048]{2,1,0:T(8,128)(2,1)} %collective-permute-done.1, bf16[1,512,2048]{2,1,0:T(8,128)(2,1)} %slice.57, bf16[1,512,2048]{2,1,0:T(8,128)(2,1)} %collective-permute-done), kind=kLoop, calls=%fused_computation.34 | loop fusion | flops 18874368 | bytes 12582912 | tf_op jit(solution)/shard_map/concatenate | solution.py:23
  47.4 3.5 %fusion.50 = (bf16[1,1536,1024]{2,1,0:T(8,128)(2,1)}, bf16[1,1536,1024]{2,1,0:T(8,128)(2,1)}) fusion(bf16[1,1536,2048]{2,1,0:T(8,128)(2,1)S(1)} %pad_maximum_fusion), kind=kLoop, calls=%fused_computation.81 | loop fusion | bytes 12582912 | tf_op jit(solution)/shard_map/slice | solution.py:87
  51.0 4.7 %copy.41 = bf16[1,1536,1024]{1,2,0:T(8,128)(2,1)} copy(bf16[1,1536,1024]{2,1,0:T(8,128)(2,1)} %get-tuple-element.129) | data formatting | bytes 6291456 | tf_op jit(solution)/shard_map/slice | solution.py:90
  55.7 4.6 %copy.43 = bf16[1,1536,1024]{1,2,0:T(8,128)(2,1)} copy(bf16[1,1536,1024]{2,1,0:T(8,128)(2,1)} %get-tuple-element.128) | data formatting | bytes 6291456 | tf_op jit(solution)/shard_map/slice | solution.py:87
  60.3 130.3 %while.12 = (s32[]{:T(128)}, bf16[4,1,512,4,64]{2,4,3,1,0:T(8,128)(2,1)}, bf16[4,1,1536,4,64]{2,4,3,1,0:T(8,128)(2,1)}, s32[]{:T(128)}, s32[]{:T(128)}, /*index=...) while((s32[]{:T(128)}, bf16[4,1,512,4,64]{2,4,3,1,0:T(8,128)(2,1)}, ...), condition=%wide.region_5.6_spmd, body=%wide.region_2.5_spmd.sunk | while | flops 833758720 | bytes 54039648 | solution.py:68
  60.3 1.0 fusion.68
  61.3 7.4 %fusion.67 = f32[4,512,1536]{2,1,0:T(8,128)} fusion(bf16[4,1,1536,4,64]{2,4,3,1,0:T(8,128)(2,1)} %get-tuple-element.211, s32[]{:T(128)} %get-tuple-element.197, bf16[4,1,512,4,64]{2,4,3,1,0:T(8,128)(2,1)S(1)} %get-tuple-element.210), kind=kOutput, calls=%fused_computation.18.clone.1 | convolution fusion | flops 402653184 | bytes 13632512 | tf_op jit(solution)/shard_map/while/body/eval_jaxpr/mqhe,mkhe->mhqk/dot_general | solution.py:38
  68.7 16.5 %fusion.69 = (f32[4,512]{1,0:T(4,128)S(1)}, f32[4,512,1536]{2,1,0:T(8,128)}) fusion(f32[4,512,1536]{2,1,0:T(8,128)} %fusion.67, pred[512,1536]{1,0:T(8,128)(4,1)S(1)} %fusion.68), kind=kOutput, calls=%fused_computation.80.clone.1 | output fusion | flops 18875904 | bytes 25960448 | tf_op jit(solution)/shard_map/while/body/eval_jaxpr/sub | solution.py:50
  85.2 7.6 %fusion.70 = bf16[4,1,512,4,64]{2,4,3,1,0:T(8,128)(2,1)} fusion(bf16[4,1,512,4,64]{2,4,3,1,0:T(8,128)(2,1)} %get-tuple-element.198, s32[]{:T(128)} %get-tuple-element.197, f32[4,512,1536]{2,1,0:T(8,128)} %get-tuple-element.187, f32[4,512]{1,0:T(4,128)S(1)} %get-tuple-element.188, bf16[4,1,1536,4,64]{2,4,3,1,0:T(8,128)(2,1)} %get-tuple-element.207), kind=kOutput, calls=%fused_computation.17.clone.1 | convolution fusion | flops 409075712 | bytes 13640704 | tf_op jit(solution)/shard_map/while/body/eval_jaxpr/mhqk,mkhe->mqhe/dot_general | solution.py:52
  92.9 1.0 fusion.68
  93.9 7.4 %fusion.67 = f32[4,512,1536]{2,1,0:T(8,128)} fusion(bf16[4,1,1536,4,64]{2,4,3,1,0:T(8,128)(2,1)} %get-tuple-element.211, s32[]{:T(128)} %get-tuple-element.197, bf16[4,1,512,4,64]{2,4,3,1,0:T(8,128)(2,1)S(1)} %get-tuple-element.210), kind=kOutput, calls=%fused_computation.18.clone.1 | convolution fusion | flops 402653184 | bytes 13632512 | tf_op jit(solution)/shard_map/while/body/eval_jaxpr/mqhe,mkhe->mhqk/dot_general | solution.py:38
  101.3 16.5 %fusion.69 = (f32[4,512]{1,0:T(4,128)S(1)}, f32[4,512,1536]{2,1,0:T(8,128)}) fusion(f32[4,512,1536]{2,1,0:T(8,128)} %fusion.67, pred[512,1536]{1,0:T(8,128)(4,1)S(1)} %fusion.68), kind=kOutput, calls=%fused_computation.80.clone.1 | output fusion | flops 18875904 | bytes 25960448 | tf_op jit(solution)/shard_map/while/body/eval_jaxpr/sub | solution.py:50
  117.8 7.6 %fusion.70 = bf16[4,1,512,4,64]{2,4,3,1,0:T(8,128)(2,1)} fusion(bf16[4,1,512,4,64]{2,4,3,1,0:T(8,128)(2,1)} %get-tuple-element.198, s32[]{:T(128)} %get-tuple-element.197, f32[4,512,1536]{2,1,0:T(8,128)} %get-tuple-element.187, f32[4,512]{1,0:T(4,128)S(1)} %get-tuple-element.188, bf16[4,1,1536,4,64]{2,4,3,1,0:T(8,128)(2,1)} %get-tuple-element.207), kind=kOutput, calls=%fused_computation.17.clone.1 | convolution fusion | flops 409075712 | bytes 13640704 | tf_op jit(solution)/shard_map/while/body/eval_jaxpr/mhqk,mkhe->mqhe/dot_general | solution.py:52
  125.5 1.0 fusion.68
  126.4 7.4 %fusion.67 = f32[4,512,1536]{2,1,0:T(8,128)} fusion(bf16[4,1,1536,4,64]{2,4,3,1,0:T(8,128)(2,1)} %get-tuple-element.211, s32[]{:T(128)} %get-tuple-element.197, bf16[4,1,512,4,64]{2,4,3,1,0:T(8,128)(2,1)S(1)} %get-tuple-element.210), kind=kOutput, calls=%fused_computation.18.clone.1 | convolution fusion | flops 402653184 | bytes 13632512 | tf_op jit(solution)/shard_map/while/body/eval_jaxpr/mqhe,mkhe->mhqk/dot_general | solution.py:38
  133.9 16.5 %fusion.69 = (f32[4,512]{1,0:T(4,128)S(1)}, f32[4,512,1536]{2,1,0:T(8,128)}) fusion(f32[4,512,1536]{2,1,0:T(8,128)} %fusion.67, pred[512,1536]{1,0:T(8,128)(4,1)S(1)} %fusion.68), kind=kOutput, calls=%fused_computation.80.clone.1 | output fusion | flops 18875904 | bytes 25960448 | tf_op jit(solution)/shard_map/while/body/eval_jaxpr/sub | solution.py:50
  150.4 7.7 %fusion.70 = bf16[4,1,512,4,64]{2,4,3,1,0:T(8,128)(2,1)} fusion(bf16[4,1,512,4,64]{2,4,3,1,0:T(8,128)(2,1)} %get-tuple-element.198, s32[]{:T(128)} %get-tuple-element.197, f32[4,512,1536]{2,1,0:T(8,128)} %get-tuple-element.187, f32[4,512]{1,0:T(4,128)S(1)} %get-tuple-element.188, bf16[4,1,1536,4,64]{2,4,3,1,0:T(8,128)(2,1)} %get-tuple-element.207), kind=kOutput, calls=%fused_computation.17.clone.1 | convolution fusion | flops 409075712 | bytes 13640704 | tf_op jit(solution)/shard_map/while/body/eval_jaxpr/mhqk,mkhe->mqhe/dot_general | solution.py:52
  158.0 1.0 fusion.68
  159.0 7.4 %fusion.67 = f32[4,512,1536]{2,1,0:T(8,128)} fusion(bf16[4,1,1536,4,64]{2,4,3,1,0:T(8,128)(2,1)} %get-tuple-element.211, s32[]{:T(128)} %get-tuple-element.197, bf16[4,1,512,4,64]{2,4,3,1,0:T(8,128)(2,1)S(1)} %get-tuple-element.210), kind=kOutput, calls=%fused_computation.18.clone.1 | convolution fusion | flops 402653184 | bytes 13632512 | tf_op jit(solution)/shard_map/while/body/eval_jaxpr/mqhe,mkhe->mhqk/dot_general | solution.py:38
  166.5 16.5 %fusion.69 = (f32[4,512]{1,0:T(4,128)S(1)}, f32[4,512,1536]{2,1,0:T(8,128)}) fusion(f32[4,512,1536]{2,1,0:T(8,128)} %fusion.67, pred[512,1536]{1,0:T(8,128)(4,1)S(1)} %fusion.68), kind=kOutput, calls=%fused_computation.80.clone.1 | output fusion | flops 18875904 | bytes 25960448 | tf_op jit(solution)/shard_map/while/body/eval_jaxpr/sub | solution.py:50
  182.9 7.6 %fusion.70 = bf16[4,1,512,4,64]{2,4,3,1,0:T(8,128)(2,1)} fusion(bf16[4,1,512,4,64]{2,4,3,1,0:T(8,128)(2,1)} %get-tuple-element.198, s32[]{:T(128)} %get-tuple-element.197, f32[4,512,1536]{2,1,0:T(8,128)} %get-tuple-element.187, f32[4,512]{1,0:T(4,128)S(1)} %get-tuple-element.188, bf16[4,1,1536,4,64]{2,4,3,1,0:T(8,128)(2,1)} %get-tuple-element.207), kind=kOutput, calls=%fused_computation.17.clone.1 | convolution fusion | flops 409075712 | bytes 13640704 | tf_op jit(solution)/shard_map/while/body/eval_jaxpr/mhqk,mkhe->mqhe/dot_general | solution.py:52
  190.6 2.8 fusion.38
  193.4 9.7 %gather_fusion = bf16[2048,1024]{1,0:T(8,128)(2,1)} fusion(bf16[512,1024]{1,0:T(8,128)(2,1)S(1)} %fusion.38, s32[2048]{0:T(1024)S(1)} %fusion.44), kind=kCustom, calls=%fused_computation.clone | custom fusion | bytes 8396800 | tf_op jit(solution)/shard_map/jit(_take)/gather | solution.py:100
  203.1 9.7 %gather_fusion.1 = bf16[2048,1024]{1,0:T(8,128)(2,1)} fusion(bf16[512,1024]{1,0:T(8,128)(2,1)S(1)} %fusion.38, s32[2048]{0:T(1024)S(1)} %copy-done.4), kind=kCustom, calls=%fused_computation.1.clone | custom fusion | bytes 8396800 | tf_op jit(solution)/shard_map/jit(_take)/gather | solution.py:100
  212.7 9.7 %gather_fusion.2 = bf16[2048,1024]{1,0:T(8,128)(2,1)} fusion(bf16[512,1024]{1,0:T(8,128)(2,1)S(1)} %fusion.38, s32[2048]{0:T(1024)S(1)} %copy-done.2), kind=kCustom, calls=%fused_computation.2.clone | custom fusion | bytes 8396800 | tf_op jit(solution)/shard_map/jit(_take)/gather | solution.py:100
  222.5 9.7 %gather_fusion.3 = bf16[2048,1024]{1,0:T(8,128)(2,1)} fusion(bf16[512,1024]{1,0:T(8,128)(2,1)S(1)} %fusion.38, s32[2048]{0:T(1024)S(1)} %copy-done.3), kind=kCustom, calls=%fused_computation.3.clone | custom fusion | bytes 8396800 | tf_op jit(solution)/shard_map/jit(_take)/gather | solution.py:100
  232.3 10.6 %fusion.30 = bf16[1,100,2048]{2,1,0:T(8,128)(2,1)} fusion(bf16[100,1024]{1,0:T(8,128)(2,1)S(1)} %copy-done.15, bf16[2048,1024]{1,0:T(8,128)(2,1)} %gather_fusion.3, bf16[2048,1024]{1,0:T(8,128)(2,1)} %gather_fusion.2, bf16[2048,1024]{1,0:T(8,128)(2,1)} %gather_fusion.1, bf16[2048,1024]{1,0:T(8,128)(2,1)} %gather_fusion, f32[2048]{0:T(1024)S(1)} %bitcast.149, ...), kind=kOutput, calls=%fused_computation.49 | convolution fusion | flops 453189632 | bytes 17432576 | tf_op jit(solution)/shard_map/vd,mgd->mvg/dot_general | solution.py:102
  242.9 2.3 copy.47
  245.8 12.3 %reduce.12 = bf16[2048,100]{1,0:T(8,128)(2,1)} reduce(bf16[2048,1,100]{2,1,0:T(2,128)(2,1)S(1)} %bitcast.136, bf16[]{:T(256)} %broadcast.191), dimensions={1}, to_apply=%bitcast.117.reduce_sub_computation | reduce | bytes 819202
  258.1 2.6 reshape.267
  260.7 13.8 %all_to_all.4 = bf16[8,2,12800]{2,1,0:T(2,128)(2,1)S(1)} all-to-all(bf16[8,2,12800]{2,1,0:T(2,128)(2,1)S(1)} %reshape.267), channel_id=1, replica_groups=mesh['ens'=8,'mp'=4] {'ens'}, dimensions={0} | all-to-all | bytes 819200 | tf_op jit(solution)/shard_map/all_to_all | solution.py:105
  274.4 2.2 reshape.268
  276.6 3.8 %copy.48 = bf16[1,100,2048]{2,0,1:T(2,128)(2,1)} copy(bf16[1,100,2048]{1,0,2:T(2,128)(2,1)S(1)} %bitcast.135) | data formatting | bytes 819200 | tf_op jit(solution)/shard_map/all_to_all | solution.py:105
  280.4 3.5 %convert_reduce_fusion.1 = f32[100,2048]{1,0:T(8,128)S(1)} fusion(bf16[1,100,2048]{2,0,1:T(2,128)(2,1)} %copy.48), kind=kLoop, calls=%fused_computation.61 | loop fusion | flops 204800 | bytes 1228800 | tf_op jit(solution)/shard_map/convert_element_type | solution.py:105
  284.5 0.8 abs_reduce_fusion
  285.7 0.7 multiply_subtract_fusion
  (59 shorter events, 4.0 us)
Async XLA Ops:
  0.0 190.6 %copy-start = (bf16[1024,1024]{1,0:T(8,128)(2,1)S(1)}, bf16[1024,1024]{1,0:T(8,128)(2,1)}, u32[]{:S(2)}) copy-start(bf16[1024,1024]{1,0:T(8,128)(2,1)} %param.15) | copy-start | bytes 6291460
  9.9 10.7 %copy-start.5 = (s32[4,2048]{1,0:T(4,128)S(1)}, s32[4,2048]{1,0:T(4,128)}, u32[]{:S(2)}) copy-start(s32[4,2048]{1,0:T(4,128)} %param.16) | copy-start | bytes 98308
  9.9 13.7 %copy-start.6 = (f32[4,2048]{1,0:T(4,128)S(1)}, f32[4,2048]{1,0:T(4,128)}, u32[]{:S(2)}) copy-start(f32[4,2048]{1,0:T(4,128)} %param.17) | copy-start | bytes 98308
  11.4 27.8 %collective-permute-start = (bf16[1,512,2048]{2,1,0:T(8,128)(2,1)}, bf16[1,512,2048]{2,1,0:T(8,128)(2,1)}, u32[]{:S(2)}, u32[]{:S(2)}) collective-permute-start(bf16[1,512,2048]{2,1,0:T(8,128)(2,1)} %slice.57), channel_id=1, source_target_pairs={{0,1},{1,2},{2,3},{4,5},{5,6},{6,7},{8,9},{9,10},{10,11},{12,13},{... | collective-permute-start | bytes 6291464 | tf_op jit(solution)/shard_map/ppermute | solution.py:21
  15.9 27.7 %collective-permute-start.1 = (bf16[1,512,2048]{2,1,0:T(8,128)(2,1)}, bf16[1,512,2048]{2,1,0:T(8,128)(2,1)}, u32[]{:S(2)}, u32[]{:S(2)}) collective-permute-start(bf16[1,512,2048]{2,1,0:T(8,128)(2,1)} %slice.57), channel_id=1, source_target_pairs={{1,0},{2,1},{3,2},{5,4},{6,5},{7,6},{9,8},{10,9},{11,10},{13,12},{... | collective-permute-start | bytes 6291464 | tf_op jit(solution)/shard_map/ppermute | solution.py:22
  193.4 9.7 %copy-start.4 = (s32[2048]{0:T(1024)S(1)}, s32[2048]{0:T(1024)}, u32[]{:S(2)}) copy-start(s32[2048]{0:T(1024)} %fusion.45) | copy-start | bytes 24580
  203.1 9.7 %copy-start.2 = (s32[2048]{0:T(1024)S(1)}, s32[2048]{0:T(1024)}, u32[]{:S(2)}) copy-start(s32[2048]{0:T(1024)} %fusion.46) | copy-start | bytes 24580
  212.7 9.7 %copy-start.3 = (s32[2048]{0:T(1024)S(1)}, s32[2048]{0:T(1024)}, u32[]{:S(2)}) copy-start(s32[2048]{0:T(1024)} %fusion.47) | copy-start | bytes 24580
  222.4 9.8 %copy-start.7 = (f32[1,2048]{1,0:T(1,128)S(1)}, f32[1,2048]{1,0:T(1,128)}, u32[]{:S(2)}) copy-start(f32[1,2048]{1,0:T(1,128)} %get-tuple-element.130) | copy-start | bytes 24580
  222.4 9.8 %copy-start.8 = (f32[1,2048]{1,0:T(1,128)S(1)}, f32[1,2048]{1,0:T(1,128)}, u32[]{:S(2)}) copy-start(f32[1,2048]{1,0:T(1,128)} %get-tuple-element.131) | copy-start | bytes 24580
  222.4 9.8 %copy-start.9 = (f32[1,2048]{1,0:T(1,128)S(1)}, f32[1,2048]{1,0:T(1,128)}, u32[]{:S(2)}) copy-start(f32[1,2048]{1,0:T(1,128)} %get-tuple-element.132) | copy-start | bytes 24580
  222.4 9.8 %copy-start.10 = (f32[1,2048]{1,0:T(1,128)S(1)}, f32[1,2048]{1,0:T(1,128)}, u32[]{:S(2)}) copy-start(f32[1,2048]{1,0:T(1,128)} %get-tuple-element.133) | copy-start | bytes 24580
  222.4 9.8 %copy-start.11 = (pred[2048]{0:T(1024)(128)(4,1)S(1)}, pred[2048]{0:T(1024)(128)(4,1)}, u32[]{:S(2)}) copy-start(pred[2048]{0:T(1024)(128)(4,1)} %get-tuple-element.138) | copy-start | bytes 6148
  222.5 9.8 %copy-start.12 = (pred[2048]{0:T(1024)(128)(4,1)S(1)}, pred[2048]{0:T(1024)(128)(4,1)}, u32[]{:S(2)}) copy-start(pred[2048]{0:T(1024)(128)(4,1)} %get-tuple-element.139) | copy-start | bytes 6148
  222.5 9.8 %copy-start.13 = (pred[2048]{0:T(1024)(128)(4,1)S(1)}, pred[2048]{0:T(1024)(128)(4,1)}, u32[]{:S(2)}) copy-start(pred[2048]{0:T(1024)(128)(4,1)} %get-tuple-element.140) | copy-start | bytes 6148
  222.5 9.8 %copy-start.14 = (pred[2048]{0:T(1024)(128)(4,1)S(1)}, pred[2048]{0:T(1024)(128)(4,1)}, u32[]{:S(2)}) copy-start(pred[2048]{0:T(1024)(128)(4,1)} %get-tuple-element.141) | copy-start | bytes 6148
  222.5 9.8 %copy-start.15 = (bf16[100,1024]{1,0:T(8,128)(2,1)S(1)}, bf16[100,1024]{1,0:T(8,128)(2,1)}, u32[]{:S(2)}) copy-start(bf16[100,1024]{1,0:T(8,128)(2,1)} %param.18) | copy-start | bytes 614404
  280.4 5.0 %copy-start.1 = (f32[100,256]{1,0:T(8,128)S(1)}, f32[100,256]{1,0:T(8,128)}, u32[]{:S(2)}) copy-start(f32[100,256]{1,0:T(8,128)} %param.19) | copy-start | bytes 307204
where the time goes:
time: 287 us; the launch traced here: 286 us
  other arithmetic  97.6 us (34%)
  matrix products  80.4 us (28%)
  local copies, waits for them, and re-layouts  68.3 us (24%)
  waiting for transfers between devices  19.3 us (7%)
  blocking collectives  13.8 us (5%)
  starting transfers between devices  6.6 us (2%)
    sub x4, other arithmetic, attend(): expo = jnp.exp(scores - top)  65.9 us
    gather x4, local copies, waits for them, and re-layouts, shards(): picked = jnp.take(processed, local_index[slot_index], axis=1)  38.7 us
    dot_general x4, matrix products, attend(): jnp.einsum('mhqk,mkhe->mqhe', weights, value_rows, preferred_element_type...  30.6 us
    dot_general x4, matrix products, attend(): jnp.einsum('mqhe,mkhe->mhqk', queries, key_rows, preferred_element_type=j...  29.7 us
    ppermute x1, waiting for transfers between devices, padded_2(): before = lax.ppermute(last, axis, up)  15 us
    all_to_all x1, blocking collectives, shards(): lax.all_to_all(decoded, 'ens', split_axis=2, concat_axis=0, tiled=True)  13.8 us
    unnamed x1, other arithmetic  12.3 us
    dot_general x1, matrix products, shards(): jnp.einsum('vd,mgd->mvg', w_dec, hidden.astype(jnp.bfloat16), preferred_e...  10.6 us
  transfers between devices with their start and end apart: 2, of which 2 were waited for; matrix products, arithmetic and copies ran while one was open for 2% of the time, Pallas kernels for 0%

commit v1 on v0

v1 whole, which is shorter than its diff:
```python
import functools

import jax
import jax.numpy as jnp
from jax import lax
from jax.experimental import pallas as pl
from jax.experimental.pallas import tpu as pltpu
from jax.sharding import PartitionSpec as P

HEADS = 16
NEIGH = 4
HALF = 512
ALPHA = 0.95
EPS = 1e-05
MASKED = -1e30
GROUPS = 4
PAIR = 2

BF16 = jnp.bfloat16
F32 = jnp.float32
MIB = 1024 * 1024


def dot(a, b):
    return lax.dot_general(a, b, (((1,), (0,)), ((), ())), preferred_element_type=F32)


def dot_nt(a, b):
    return lax.dot_general(a, b, (((1,), (1,)), ((), ())), preferred_element_type=F32)


def layer_norm(inputs, ln_gain):
    values = inputs.astype(F32)
    average = jnp.mean(values, axis=-1, keepdims=True)
    centred = values - average
    variance = jnp.mean(centred * centred, axis=-1, keepdims=True)
    return (centred * lax.rsqrt(variance + EPS) * ln_gain).astype(BF16)


def halves(width):
    lane = lax.broadcasted_iota(jnp.int32, (1, width), 1)
    first = (lane < width // 2).astype(F32).astype(BF16)
    return first, (1.0 - first.astype(F32)).astype(BF16)


def value_side(values, masks):
    rows = values.shape[0]
    parts = []
    for mask in masks:
        ones = jnp.broadcast_to(mask, (rows, mask.shape[1]))
        parts.append(jnp.concatenate([values * mask, ones], axis=1))
    return jnp.concatenate(parts, axis=0)


def pair_attend(queries, keys, values_ext, masks, bias):
    width = queries.shape[1]
    tops, weights = [], []
    for mask in masks:
        scores = dot_nt(queries, keys * mask)
        if bias is not None:
            scores = scores + bias
        top = jnp.max(scores, axis=-1, keepdims=True)
        weights.append(jnp.exp(scores - top).astype(BF16))
        tops.append(top)
    both = dot(jnp.concatenate(weights, axis=1), values_ext)
    lane = lax.broadcasted_iota(jnp.int32, (queries.shape[0], width), 1)
    top = jnp.where(lane < width // 2, tops[0], tops[1])
    return both[:, :width], both[:, width:], top


def own_kernel(head_dim, x_ref, gain_ref, wq_ref, wk_ref, wv_ref, q_ref, sum_ref, total_ref, top_ref, normed_ref):
    @pl.when(pl.program_id(0) == 0)
    def _():
        normed_ref[...] = layer_norm(x_ref[...], gain_ref[...])

    rows, width = q_ref.shape
    normed = normed_ref[...]
    q_ref[...] = (dot(normed, wq_ref[...]).astype(BF16).astype(F32) * head_dim**-0.5).astype(BF16)
    keys = dot(normed, wk_ref[...]).astype(BF16)
    values = dot(normed, wv_ref[...]).astype(BF16)
    pair = PAIR * head_dim
    masks = halves(pair)
    step = rows // 2
    for first in range(0, width, pair):
        cols = slice(first, first + pair)
        values_ext = value_side(values[:, cols], masks)
        for row in range(0, rows, step):
            here = slice(row, row + step)
            sums, totals, top = pair_attend(q_ref[here, cols], keys[:, cols], values_ext, masks, None)
            sum_ref[here, cols] = sums
            total_ref[here, cols] = totals
            top_ref[here, cols] = top


def window_bias(rows, span, width, left_ok, right_ok, part):
    query = part * rows + lax.broadcasted_iota(jnp.int32, (rows, width), 0)
    key = part * rows + lax.broadcasted_iota(jnp.int32, (rows, width), 1)
    position = jnp.where(key < span, key - span, key)
    near = jnp.abs(position - query) <= HALF
    there = jnp.where(key < span, left_ok, right_ok) > 0
    return jnp.where(near & there, 0.0, MASKED).astype(F32)


def rest_kernel(
    head_dim, dests,
    place_ref, left_ref, right_ref, gain_ref, wk_ref, wv_ref, q_ref, sum_ref, total_ref, top_ref,
    x_ref, wout_ref, wdec_ref, near_ref, edge_ref,
    out_ref,
    normed_ref, bias_ref, proj_ref, high_ref, low_ref,
):
    group = pl.program_id(0)
    rows, width = q_ref.shape
    part_rows = rows // 2
    span = part_rows * 3

    @pl.when(group == 0)
    def _():
        normed_ref[:rows] = layer_norm(left_ref[...], gain_ref[...])
        normed_ref[rows:] = layer_norm(right_ref[...], gain_ref[...])
        for part in range(2):
            bias_ref[part] = window_bias(part_rows, rows, span, place_ref[0], place_ref[1], part)

    normed = normed_ref[...]
    keys = dot(normed, wk_ref[...]).astype(BF16)
    values = dot(normed, wv_ref[...]).astype(BF16)
    pair = PAIR * head_dim
    masks = halves(pair)
    context = [[], []]
    for first in range(0, width, pair):
        cols = slice(first, first + pair)
        for part in range(2):
            here = slice(part * part_rows, (part + 1) * part_rows)
            there = slice(part * part_rows, part * part_rows + span)
            sums, totals, top = pair_attend(
                q_ref[here, cols], keys[there, cols], value_side(values[there, cols], masks), masks, bias_ref[part]
            )
            own_top = top_ref[here, cols]
            best = jnp.maximum(top, own_top)
            scale, own_scale = jnp.exp(top - best), jnp.exp(own_top - best)
            sums = sums * scale + sum_ref[here, cols] * own_scale
            totals = totals * scale + total_ref[here, cols] * own_scale
            context[part].append((sums / totals).astype(BF16))
    context = jnp.concatenate([jnp.concatenate(c, axis=1) for c in context], axis=0)
    added = dot(context, wout_ref[...])

    @pl.when(group == 0)
    def _():
        proj_ref[...] = x_ref[...].astype(F32) + added

    @pl.when(group > 0)
    def _():
        proj_ref[...] += added

    points = near_ref.shape[1]
    token = lax.broadcasted_iota(jnp.int32, (rows, points), 0) + place_ref[2]
    matrix = jnp.zeros((rows, points), F32)
    for k in range(NEIGH):
        matrix += jnp.where(token == near_ref[k : k + 1], edge_ref[k : k + 1], 0.0)
    high = matrix.astype(BF16)
    high_ref[group] = high
    low_ref[group] = (matrix - high.astype(F32)).astype(BF16)

    @pl.when(group == pl.num_programs(0) - 1)
    def _():
        fields = dot_nt(wdec_ref[...], proj_ref[...].astype(BF16))
        tall = fields.shape[0]
        fields_high = fields.astype(BF16)
        fields_low = (fields - fields_high.astype(F32)).astype(BF16)
        both = jnp.concatenate([fields_high, fields_low], axis=0)
        variables, each = out_ref.shape[1:]
        for g in range(high_ref.shape[0]):
            product = dot(both, high_ref[g])
            decoded = product[:tall] + product[tall:] + dot(fields_high, low_ref[g])
            decoded = decoded.astype(BF16)
            for d in range(points // each):
                out_ref[g * (points // each) + d] = decoded[:variables, d * each : (d + 1) * each]


def score_kernel(members, coeff, fields_ref, truth_ref, out_ref):
    fields = [fields_ref[m].astype(F32) for m in range(members)]
    truth = truth_ref[...]
    skill = sum(jnp.abs(f - truth) for f in fields) / members
    spread = sum(jnp.abs(fields[j] - fields[k]) for j in range(members) for k in range(j))
    out_ref[...] = skill - (2.0 * coeff) * spread


def whole(shape):
    return pl.BlockSpec(shape, lambda g: (0,) * len(shape))


def columns(shape, offset=0):
    return pl.BlockSpec(shape, lambda g: (0, offset + g))


def one_member(tokens, left, right, ln_gain, w_qkv, w_out, near, edge_weights, w_dec, place, dests):
    rows, model = tokens.shape
    head_dim = model // HEADS
    width = model // GROUPS
    points = near.shape[1]
    tall = -(-w_dec.shape[0] // 16) * 16
    gain = ln_gain[None]
    wide = lambda dtype: jax.ShapeDtypeStruct((rows, model), dtype)
    block = columns((rows, width))
    weight = lambda k: columns((model, width), k * GROUPS)
    queries, sums, totals, tops = pl.pallas_call(
        functools.partial(own_kernel, head_dim),
        grid=(GROUPS,),
        in_specs=[whole((rows, model)), whole((1, model)), weight(0), weight(1), weight(2)],
        out_specs=[block] * 4,
        out_shape=[wide(BF16), wide(F32), wide(F32), wide(F32)],
        scratch_shapes=[pltpu.VMEM((rows, model), BF16)],
        compiler_params=pltpu.CompilerParams(vmem_limit_bytes=40 * MIB),
        cost_estimate=pl.CostEstimate(
            flops=2 * rows * model * 3 * model + 16 * rows * rows * model, bytes_accessed=14 * MIB, transcendentals=HEADS * rows * rows
        ),
        name="own_tokens",
    )(tokens, gain, w_qkv, w_qkv, w_qkv)
    per_step = points // GROUPS
    return pl.pallas_call(
        functools.partial(rest_kernel, head_dim, dests),
        grid=(GROUPS,),
        in_specs=[
            pl.BlockSpec(memory_space=pltpu.SMEM),
            whole((rows, model)), whole((rows, model)), whole((1, model)), weight(1), weight(2),
            block, block, block, block,
            whole((rows, model)),
            pl.BlockSpec((width, model), lambda g: (g, 0)),
            whole((tall, model)),
            columns((NEIGH, per_step)), columns((NEIGH, per_step)),
        ],
        out_specs=whole((dests, w_dec.shape[0], points // dests)),
        out_shape=jax.ShapeDtypeStruct((dests, w_dec.shape[0], points // dests), BF16),
        scratch_shapes=[
            pltpu.VMEM((2 * rows, model), BF16),
            pltpu.VMEM((2, rows // 2, rows // 2 * 3), F32),
            pltpu.VMEM((rows, model), F32),
            pltpu.VMEM((GROUPS, rows, per_step), BF16),
            pltpu.VMEM((GROUPS, rows, per_step), BF16),
        ],
        compiler_params=pltpu.CompilerParams(vmem_limit_bytes=56 * MIB),
        cost_estimate=pl.CostEstimate(
            flops=2 * rows * model * 5 * model + 24 * rows * rows * model, bytes_accessed=20 * MIB, transcendentals=2 * HEADS * rows * rows
        ),
        name="neighbour_tokens",
    )(
        place, left, right, gain, w_qkv, w_qkv, queries, sums, totals, tops, tokens, w_out,
        jnp.pad(w_dec, ((0, tall - w_dec.shape[0]), (0, 0))), near, edge_weights,
    )


def shards(tokens, ln_gain, w_qkv, w_out, neighbours, edge_weights, w_dec, truth):
    lanes = lax.axis_size("mp")
    lane = lax.axis_index("mp")
    dests = lax.axis_size("ens")
    up = [(i, i + 1) for i in range(lanes - 1)]
    down = [(j, i) for i, j in up]
    left = lax.ppermute(tokens, "mp", up)
    right = lax.ppermute(tokens, "mp", down)
    rows = tokens.shape[1]
    place = jnp.stack([lane > 0, lane < lanes - 1, lane * rows]).astype(jnp.int32)
    decoded = jnp.stack(
        [
            one_member(tokens[m], left[m], right[m], ln_gain, w_qkv, w_out, neighbours, edge_weights, w_dec, place, dests)
            for m in range(tokens.shape[0])
        ]
    )
    gathered = lax.all_to_all(decoded, "ens", split_axis=1, concat_axis=0, tiled=True)
    gathered = gathered.reshape((-1,) + gathered.shape[2:])
    members = gathered.shape[0]
    coeff = ALPHA / (2.0 * members * (members - 1)) + (1.0 - ALPHA) / (2.0 * members * members)
    return pl.pallas_call(
        functools.partial(score_kernel, members, coeff),
        out_shape=jax.ShapeDtypeStruct(truth.shape, F32),
        name="scores",
    )(gathered, truth)


def solution(mesh):
    in_specs = (
        P("ens", "mp", None),
        P(),
        P(),
        P(),
        P(None, "mp"),
        P(None, "mp"),
        P(),
        P(None, ("mp", "ens")),
    )
    out_specs = P(None, ("mp", "ens"))
    return jax.shard_map(shards, mesh=mesh, in_specs=in_specs, out_specs=out_specs, check_vma=False)
```

time: 287 us -> 75.2 us (0.26)
  the two profiles are of different devices: /device:TPU:1 before, /device:TPU:0 now
where the time goes in v1:
time: 75.2 us; the launch traced here: 74.1 us
  Pallas kernels  40.3 us (54%)
  blocking collectives  19.5 us (26%)
  local copies, waits for them, and re-layouts  9.95 us (13%)
  starting transfers between devices  3.71 us (5%)
    pallas_call x1, Pallas kernels, one_member(): pl.pallas_call(functools.partial(rest_kernel, head_dim, dests), grid=(GRO...  25.4 us
    all_to_all x1, blocking collectives, shards(): lax.all_to_all(decoded, 'ens', split_axis=1, concat_axis=0, tiled=True)  19.5 us
    pallas_call x1, Pallas kernels, one_member(): pl.pallas_call(functools.partial(own_kernel, head_dim), grid=(GROUPS,), i...  12.8 us
    unnamed x16, local copies, waits for them, and re-layouts  8.29 us
    ppermute x1, starting transfers between devices, shards(): left = lax.ppermute(tokens, 'mp', up)  2.41 us
    pallas_call x1, Pallas kernels, shards(): pl.pallas_call(functools.partial(score_kernel, members, coeff), out_shape...  2.08 us
    pad x1, local copies, waits for them, and re-layouts, one_member(): jnp.pad(w_dec, ((0, tall - w_dec.shape[0]), (0, 0)))  1.66 us
  transfers between devices with their start and end apart: 2, of which 0 were waited for; matrix products, arithmetic and copies ran while one was open for 3% of the time, Pallas kernels for 17%

profile of v1, /device:TPU:0, one launch (start us, length us, event | category | flops | bytes accessed | tf_op | source)
XLA Modules:
  0.0 74.1 jit_solution(14841308642873411325)
XLA Ops:
  0.0 2.4 %collective-permute-start = (bf16[1,512,1024]{2,1,0:T(8,128)(2,1)}, bf16[1,512,1024]{2,1,0:T(8,128)(2,1)S(1)}, u32[]{:S(2)}, u32[]{:S(2)}) collective-permute-start(bf16[1,512,1024]{2,1,0:T(8,128)(2,1)} %param.8), channel_id=1, source_target_pairs={{0,1},{1,2},{2,3},{4,5},{5,6},{6,7},{8,9},{9,10},{10,11},{12,13},{... | collective-permute-start | bytes 3145736 | tf_op jit(solution)/shard_map/ppermute | solution.py:257
  2.4 1.3 %collective-permute-start.1 = (bf16[1,512,1024]{2,1,0:T(8,128)(2,1)}, bf16[1,512,1024]{2,1,0:T(8,128)(2,1)S(1)}, u32[]{:S(2)}, u32[]{:S(2)}) collective-permute-start(bf16[1,512,1024]{2,1,0:T(8,128)(2,1)} %param.8), channel_id=1, source_target_pairs={{1,0},{2,1},{3,2},{5,4},{6,5},{7,6},{9,8},{10,9},{11,10},{13,12},{... | collective-permute-start | bytes 3145736 | tf_op jit(solution)/shard_map/ppermute | solution.py:258
  3.7 1.7 %pad.4.wdec_ref = bf16[112,1024]{1,0:T(8,128)(2,1)} pad(bf16[100,1024]{1,0:T(8,128)(2,1)} %param.14, bf16[]{:T(256)} %constant.11.clone.1), padding=0_12x0_0 | pad | bytes 434178 | tf_op jit(solution)/shard_map/jit(_pad)/pad | solution.py:247
  5.4 0.7 pad_add_fusion.place_ref
  6.1 0.0 copy-start
  6.1 1.2 %copy-done = bf16[1,512,1024]{2,1,0:T(8,128)(2,1)S(1)} copy-done((bf16[1,512,1024]{2,1,0:T(8,128)(2,1)S(1)}, bf16[1,512,1024]{2,1,0:T(8,128)(2,1)}, u32[]{:S(2)}) %copy-start) | copy-done | bytes 1048600
  7.3 0.0 copy-start.1
  7.3 0.7 copy-done.1
  8.0 12.8 %own_tokens.1 = (bf16[512,1024]{1,0:T(8,128)(2,1)S(1)}, f32[512,1024]{1,0:T(8,128)S(1)}, f32[512,1024]{1,0:T(8,128)S(1)}, f32[512,1024]{1,0:T(8,128)S(1)}) custom-call(bf16[512,1024]{1,0:T(8,128)(2,1)S(1)} %bitcast.12, f32[1,1024]{1,0:T(1,128)S(1)} %bitcast.14, bf16[1024,3072]{1,0:T(8,128)(2,1)} %wv_ref.3, bf16[1024,3072]{1,0:T(8,128)(2,1)} %wv_ref.3, ...), custom_call_target="tpu_custom_call" | custom-call | flops 7516192768 | bytes 14680064 | tf_op jit(solution)/shard_map/own_tokens/pallas_call | solution.py:205
  20.8 0.0 copy-start.2
  20.8 1.3 %copy-done.2 = f32[512,1024]{1,0:T(8,128)} copy-done((f32[512,1024]{1,0:T(8,128)}, f32[512,1024]{1,0:T(8,128)S(1)}, u32[]{:S(2)}) %copy-start.2) | copy-done | bytes 2097176
  22.1 0.0 copy-start.3
  22.1 1.3 %copy-done.3 = f32[512,1024]{1,0:T(8,128)} copy-done((f32[512,1024]{1,0:T(8,128)}, f32[512,1024]{1,0:T(8,128)S(1)}, u32[]{:S(2)}) %copy-start.3) | copy-done | bytes 2097176
  23.4 0.0 copy-start.4
  23.4 1.3 %copy-done.4 = f32[512,1024]{1,0:T(8,128)} copy-done((f32[512,1024]{1,0:T(8,128)}, f32[512,1024]{1,0:T(8,128)S(1)}, u32[]{:S(2)}) %copy-start.4) | copy-done | bytes 2097176
  24.8 0.0 copy-start.5
  24.8 1.1 %copy-done.5 = bf16[512,1024]{1,0:T(8,128)(2,1)} copy-done((bf16[512,1024]{1,0:T(8,128)(2,1)}, bf16[512,1024]{1,0:T(8,128)(2,1)S(1)}, u32[]{:S(2)}) %copy-start.5) | copy-done | bytes 1048600
  25.8 0.0 collective-permute-done
  25.8 0.0 copy-start.6
  25.8 0.0 collective-permute-done.1
  25.8 0.0 copy-start.7
  25.8 1.0 %copy-done.6 = bf16[1,512,1024]{2,1,0:T(8,128)(2,1)} copy-done((bf16[1,512,1024]{2,1,0:T(8,128)(2,1)}, bf16[1,512,1024]{2,1,0:T(8,128)(2,1)S(1)}, u32[]{:S(2)}) %copy-start.6) | copy-done | bytes 1048600
  26.8 0.3 copy-done.7
  27.2 25.4 %neighbour_tokens.1 = bf16[8,100,256]{2,1,0:T(8,128)(2,1)} custom-call(s32[3]{0:T(128)} %pad_add_fusion.place_ref, bf16[512,1024]{1,0:T(8,128)(2,1)} %bitcast.17, bf16[512,1024]{1,0:T(8,128)(2,1)} %bitcast.18, f32[1,1024]{1,0:T(1,128)} %bitcast.13, bf16[1024,3072]{1,0:T(8,128)(2,1)} %wv_ref.3, bf16[1024,3072]{1,0:T(8,128)(2,1)} %wv_ref.3, ...), custom_call_target="tpu_custom_call" | custom-call | flops 11811160064 | bytes 20971520 | tf_op jit(solution)/shard_map/neighbour_tokens/pallas_call | solution.py:219
  52.6 19.5 %all_to_all.4 = bf16[1,8,100,256]{3,2,0,1:T(8,128)(2,1)} all-to-all(bf16[1,8,100,256]{3,2,0,1:T(8,128)(2,1)} %bitcast.16), channel_id=1, replica_groups=mesh['ens'=8,'mp'=4] {'ens'}, dimensions={1} | all-to-all | bytes 819200 | tf_op jit(solution)/shard_map/all_to_all | solution.py:267
  72.1 2.1 %scores.1 = f32[100,256]{1,0:T(8,128)} custom-call(bf16[8,100,256]{2,1,0:T(8,128)(2,1)} %bitcast.15, f32[100,256]{1,0:T(8,128)} %truth_ref.1), custom_call_target="tpu_custom_call" | custom-call | tf_op jit(solution)/shard_map/scores/pallas_call | solution.py:271
Async XLA Ops:
  0.0 25.8 %collective-permute-start = (bf16[1,512,1024]{2,1,0:T(8,128)(2,1)}, bf16[1,512,1024]{2,1,0:T(8,128)(2,1)S(1)}, u32[]{:S(2)}, u32[]{:S(2)}) collective-permute-start(bf16[1,512,1024]{2,1,0:T(8,128)(2,1)} %param.8), channel_id=1, source_target_pairs={{0,1},{1,2},{2,3},{4,5},{5,6},{6,7},{8,9},{9,10},{10,11},{12,13},{... | collective-permute-start | bytes 3145736 | tf_op jit(solution)/shard_map/ppermute | solution.py:257
  2.4 23.4 %collective-permute-start.1 = (bf16[1,512,1024]{2,1,0:T(8,128)(2,1)}, bf16[1,512,1024]{2,1,0:T(8,128)(2,1)S(1)}, u32[]{:S(2)}, u32[]{:S(2)}) collective-permute-start(bf16[1,512,1024]{2,1,0:T(8,128)(2,1)} %param.8), channel_id=1, source_target_pairs={{1,0},{2,1},{3,2},{5,4},{6,5},{7,6},{9,8},{10,9},{11,10},{13,12},{... | collective-permute-start | bytes 3145736 | tf_op jit(solution)/shard_map/ppermute | solution.py:258
  6.1 1.2 %copy-start = (bf16[1,512,1024]{2,1,0:T(8,128)(2,1)S(1)}, bf16[1,512,1024]{2,1,0:T(8,128)(2,1)}, u32[]{:S(2)}) copy-start(bf16[1,512,1024]{2,1,0:T(8,128)(2,1)} %param.8) | copy-start | bytes 3145732
  7.3 0.7 copy-start.1
  20.8 1.3 %copy-start.2 = (f32[512,1024]{1,0:T(8,128)}, f32[512,1024]{1,0:T(8,128)S(1)}, u32[]{:S(2)}) copy-start(f32[512,1024]{1,0:T(8,128)S(1)} %get-tuple-element.10.sum_ref) | copy-start | bytes 6291460
  22.1 1.3 %copy-start.3 = (f32[512,1024]{1,0:T(8,128)}, f32[512,1024]{1,0:T(8,128)S(1)}, u32[]{:S(2)}) copy-start(f32[512,1024]{1,0:T(8,128)S(1)} %get-tuple-element.11.total_ref) | copy-start | bytes 6291460
  23.4 1.3 %copy-start.4 = (f32[512,1024]{1,0:T(8,128)}, f32[512,1024]{1,0:T(8,128)S(1)}, u32[]{:S(2)}) copy-start(f32[512,1024]{1,0:T(8,128)S(1)} %get-tuple-element.12.top_ref) | copy-start | bytes 6291460
  24.8 1.1 %copy-start.5 = (bf16[512,1024]{1,0:T(8,128)(2,1)}, bf16[512,1024]{1,0:T(8,128)(2,1)S(1)}, u32[]{:S(2)}) copy-start(bf16[512,1024]{1,0:T(8,128)(2,1)S(1)} %get-tuple-element.9.q_ref) | copy-start | bytes 3145732
  25.8 1.0 %copy-start.6 = (bf16[1,512,1024]{2,1,0:T(8,128)(2,1)}, bf16[1,512,1024]{2,1,0:T(8,128)(2,1)S(1)}, u32[]{:S(2)}) copy-start(bf16[1,512,1024]{2,1,0:T(8,128)(2,1)S(1)} %collective-permute-done) | copy-start | bytes 3145732
  25.8 1.3 %copy-start.7 = (bf16[1,512,1024]{2,1,0:T(8,128)(2,1)}, bf16[1,512,1024]{2,1,0:T(8,128)(2,1)S(1)}, u32[]{:S(2)}) copy-start(bf16[1,512,1024]{2,1,0:T(8,128)(2,1)S(1)} %collective-permute-done.1) | copy-start | bytes 3145732

commit v2 on v1

v2 whole, which is shorter than its diff:
```python
import functools

import jax
import jax.numpy as jnp
from jax import lax
from jax.experimental import pallas as pl
from jax.experimental.pallas import tpu as pltpu
from jax.sharding import PartitionSpec as P

HEADS = 16
NEIGH = 4
HALF = 512
ALPHA = 0.95
EPS = 1e-05
MASKED = -1e30
STEP_COLS = 512
STEP_PAIRS = 2
OWN_ROWS = 256
FAR_ROWS = 128
EDGE_ROWS = 256
EDGE_COLS = 512

BF16 = jnp.bfloat16
F32 = jnp.float32
MIB = 1024 * 1024


def dot(a, b):
    return lax.dot_general(a, b, (((1,), (0,)), ((), ())), preferred_element_type=F32)


def dot_nt(a, b):
    return lax.dot_general(a, b, (((1,), (1,)), ((), ())), preferred_element_type=F32)


def layer_norm(inputs, ln_gain):
    values = inputs.astype(F32)
    average = jnp.mean(values, axis=-1, keepdims=True)
    centred = values - average
    variance = jnp.mean(centred * centred, axis=-1, keepdims=True)
    return (centred * lax.rsqrt(variance + EPS) * ln_gain).astype(BF16)


def halves(width):
    lane = lax.broadcasted_iota(jnp.int32, (1, width), 1)
    first = (lane < width // 2).astype(F32)
    return first.astype(BF16), (1.0 - first).astype(BF16)


def value_sides(values, masks):
    return [jnp.concatenate([values * mask, jnp.broadcast_to(mask, values.shape)], axis=1) for mask in masks]


def pair_attend(queries, key_sides, values_ext, bias):
    width = queries.shape[1]
    count = key_sides.shape[0] // 2
    both_scores = dot_nt(queries, key_sides)
    tops, weights = [], []
    for side in range(2):
        scores = both_scores[:, side * count : (side + 1) * count]
        if bias is not None:
            scores = scores + bias
        top = jnp.max(scores, axis=-1, keepdims=True)
        weights.append(jnp.exp(scores - top).astype(BF16))
        tops.append(top)
    both = dot(jnp.concatenate(weights, axis=1), values_ext)
    lane = lax.broadcasted_iota(jnp.int32, (queries.shape[0], width), 1)
    top = jnp.where(lane < width // 2, tops[0], tops[1])
    return both[:, :width], both[:, width:], top


def project_kernel(head_dim, x_ref, gain_ref, w_ref, kv_out_ref, q_ref, kv_ref, normed_ref):
    step = pl.program_id(0)
    model = x_ref.shape[1]
    q_steps = model // STEP_COLS

    @pl.when(step == 0)
    def _():
        normed_ref[...] = layer_norm(x_ref[...], gain_ref[...])

    made = dot(normed_ref[...], w_ref[...])

    @pl.when(step < q_steps)
    def _():
        cols = pl.ds(pl.multiple_of(step * STEP_COLS, STEP_COLS), STEP_COLS)
        q_ref[:, cols] = (made.astype(BF16).astype(F32) * head_dim**-0.5).astype(BF16)

    @pl.when(step >= q_steps)
    def _():
        cols = pl.ds(pl.multiple_of((step - q_steps) * STEP_COLS, STEP_COLS), STEP_COLS)
        rounded = made.astype(BF16)
        kv_ref[:, cols] = rounded
        kv_out_ref[...] = rounded


def edge_matrix(near, edge, high_ref, low_ref, cols):
    rows = high_ref.shape[0]
    points = near.shape[1]
    totals = []
    for k in range(NEIGH):
        total = jnp.zeros((1, points), F32)
        for j in range(NEIGH):
            total += jnp.where(near[j : j + 1] == near[k : k + 1], edge[j : j + 1], 0.0)
        totals.append(total)
    highs = [t.astype(BF16) for t in totals]
    lows = [(t - h.astype(F32)).astype(BF16) for t, h in zip(totals, highs)]
    shape = (EDGE_ROWS, points)
    token = lax.broadcasted_iota(jnp.int32, shape, 0).astype(F32).astype(BF16)
    for first in range(0, rows, EDGE_ROWS):
        high = jnp.zeros(shape, BF16)
        low = jnp.zeros(shape, BF16)
        for k in range(NEIGH):
            row = near[k : k + 1] - first
            row = jnp.where((row >= 0) & (row < EDGE_ROWS), row, -1).astype(F32).astype(BF16)
            hit = token == row
            high = jnp.where(hit, highs[k], high)
            low = jnp.where(hit, lows[k], low)
        high_ref[first : first + EDGE_ROWS, cols] = high
        low_ref[first : first + EDGE_ROWS, cols] = low


def own_kernel(
    head_dim, q_ref, kv_ref, near_ref, edge_ref, x_hbm, w_hbm, wout_hbm,
    sum_ref, total_ref, top_ref, high_ref, low_ref, x_ref, wkv_ref, wout_ref,
    sems,
):
    rows, model = q_ref.shape
    copies = [
        pltpu.make_async_copy(w_hbm.at[:, pl.ds(model, 2 * model)], wkv_ref, sems.at[0]),
        pltpu.make_async_copy(wout_hbm, wout_ref, sems.at[1]),
        pltpu.make_async_copy(x_hbm, x_ref, sems.at[2]),
    ]
    for copy in copies:
        copy.start()
    base = lax.axis_index("mp") * rows
    pair = 2 * head_dim
    masks = halves(pair)

    @pl.loop(0, model // (pair * STEP_PAIRS))
    def _(step):
        for p in range(STEP_PAIRS):
            first = (step * STEP_PAIRS + p) * pair
            cols = pl.ds(pl.multiple_of(first, pair), pair)
            keys = kv_ref[:, cols]
            values = kv_ref[:, pl.ds(pl.multiple_of(model + first, pair), pair)]
            key_sides = jnp.concatenate([keys * mask for mask in masks], axis=0)
            values_ext = jnp.concatenate(value_sides(values, masks), axis=0)
            for row in range(0, rows, OWN_ROWS):
                here = slice(row, row + OWN_ROWS)
                sums, totals, top = pair_attend(q_ref[here, cols], key_sides, values_ext, None)
                sum_ref[here, cols] = sums
                total_ref[here, cols] = totals
                top_ref[here, cols] = top

    for first in range(0, near_ref.shape[1], EDGE_COLS):
        cols = slice(first, first + EDGE_COLS)
        edge_matrix(near_ref[:, cols] - base, edge_ref[:, cols], high_ref, low_ref, cols)
    for copy in copies:
        copy.wait()


def window_bias(count, rows, span, left_ok, right_ok, first):
    query = first + lax.broadcasted_iota(jnp.int32, (count, span), 0)
    key = first + lax.broadcasted_iota(jnp.int32, (count, span), 1)
    position = jnp.where(key < rows, key - rows, key)
    near = jnp.abs(position - query) <= HALF
    there = jnp.where(key < rows, left_ok, right_ok) > 0
    return jnp.where(near & there, 0.0, MASKED).astype(F32)


def far_kernel(
    head_dim, chip_kv_hbm, far_hbm, gain_ref, q_ref, sum_ref, total_ref, top_ref, high_ref, low_ref, x_ref,
    wkv_ref, wout_ref, wdec_ref,
    out_ref,
    far_ref, kv_ref, bias_ref, context_ref, sems,
):
    rows, model = q_ref.shape
    lane = lax.axis_index("mp")
    lanes = lax.axis_size("mp")
    odd = lane % 2
    chip_at = pl.ds(pl.multiple_of((1 - odd) * rows, rows), rows)
    far_at = pl.ds(pl.multiple_of(odd * rows, rows), rows)
    far_copy = pltpu.make_async_copy(far_hbm, far_ref, sems.at[0])
    chip_copy = pltpu.make_async_copy(chip_kv_hbm, kv_ref.at[chip_at], sems.at[1])
    far_copy.start()
    chip_copy.start()
    span = rows + FAR_ROWS
    left_ok = (lane > 0).astype(jnp.int32)
    right_ok = (lane < lanes - 1).astype(jnp.int32)
    for part in range(rows // FAR_ROWS):
        bias_ref[part] = window_bias(FAR_ROWS, rows, span, left_ok, right_ok, part * FAR_ROWS)
    far_copy.wait()
    far_ref[...] = layer_norm(far_ref[...], gain_ref[...])
    normed = far_ref[...]
    for first in range(0, 2 * model, model):
        kv_ref[far_at, first : first + model] = dot(normed, wkv_ref[:, first : first + model]).astype(BF16)
    chip_copy.wait()
    pair = 2 * head_dim
    masks = halves(pair)

    @pl.loop(0, model // (pair * STEP_PAIRS))
    def _(step):
        for p in range(STEP_PAIRS):
            first = (step * STEP_PAIRS + p) * pair
            cols = pl.ds(pl.multiple_of(first, pair), pair)
            keys = kv_ref[:, cols]
            values = kv_ref[:, pl.ds(pl.multiple_of(model + first, pair), pair)]
            keys = [keys * mask for mask in masks]
            values = value_sides(values, masks)
            for part in range(rows // FAR_ROWS):
                here = slice(part * FAR_ROWS, (part + 1) * FAR_ROWS)
                there = slice(part * FAR_ROWS, part * FAR_ROWS + span)
                sums, totals, top = pair_attend(
                    q_ref[here, cols],
                    jnp.concatenate([k[there] for k in keys], axis=0),
                    jnp.concatenate([v[there] for v in values], axis=0),
                    bias_ref[part],
                )
                own_top = top_ref[here, cols]
                best = jnp.maximum(top, own_top)
                scale, own_scale = jnp.exp(top - best), jnp.exp(own_top - best)
                sums = sums * scale + sum_ref[here, cols] * own_scale
                totals = totals * scale + total_ref[here, cols] * own_scale
                context_ref[here, cols] = (sums / totals).astype(BF16)

    processed = (x_ref[...].astype(F32) + dot(context_ref[...], wout_ref[...])).astype(BF16)
    fields = dot_nt(wdec_ref[...], processed)
    variables, each = out_ref.shape[1:]
    tall = -(-variables // 16) * 16
    fields = jnp.concatenate([fields, jnp.zeros((tall - variables, rows), F32)], axis=0)
    fields_high = fields.astype(BF16)
    fields_low = (fields - fields_high.astype(F32)).astype(BF16)
    both = jnp.concatenate([fields_high, fields_low], axis=0)
    for d in range(out_ref.shape[0]):
        cols = slice(d * each, (d + 1) * each)
        product = dot(both, high_ref[:, cols])
        decoded = product[:tall] + product[tall:] + dot(fields_high, low_ref[:, cols])
        out_ref[d] = decoded[:variables].astype(BF16)


def score_kernel(members, coeff, fields_ref, truth_ref, out_ref):
    fields = [fields_ref[m].astype(F32) for m in range(members)]
    truth = truth_ref[...]
    skill = sum(jnp.abs(f - truth) for f in fields) / members
    spread = sum(jnp.abs(fields[j] - fields[k]) for j in range(members) for k in range(j))
    out_ref[...] = skill - (2.0 * coeff) * spread


IN_VMEM = pl.BlockSpec(memory_space=pltpu.VMEM)
ANYWHERE = pl.BlockSpec(memory_space=pl.ANY)


def held(value):
    return pltpu.with_memory_space_constraint(value, pltpu.VMEM)


def exchange(value, first, lanes):
    partner = list(range(lanes))
    for i in range(first, lanes - 1, 2):
        partner[i], partner[i + 1] = i + 1, i
    return lax.ppermute(value, "mp", list(enumerate(partner)))


def one_member(tokens, far, ln_gain, w_qkv, w_out, near, edge_weights, w_dec):
    rows, model = tokens.shape
    head_dim = model // HEADS
    points = near.shape[1]
    lanes = lax.axis_size("mp")
    dests = lax.axis_size("ens")
    gain = ln_gain[None]
    q_steps = model // STEP_COLS
    kv_out, queries, kv = pl.pallas_call(
        functools.partial(project_kernel, head_dim),
        grid=(3 * q_steps,),
        in_specs=[
            pl.BlockSpec((rows, model), lambda s: (0, 0)),
            pl.BlockSpec((1, model), lambda s: (0, 0)),
            pl.BlockSpec((model, STEP_COLS), lambda s: (0, s)),
        ],
        out_specs=[pl.BlockSpec((rows, STEP_COLS), lambda s: (0, jnp.maximum(s - q_steps, 0))), IN_VMEM, IN_VMEM],
        out_shape=[
            jax.ShapeDtypeStruct((rows, 2 * model), BF16),
            pltpu.VMEM((rows, model), BF16),
            pltpu.VMEM((rows, 2 * model), BF16),
        ],
        scratch_shapes=[pltpu.VMEM((rows, model), BF16)],
        compiler_params=pltpu.CompilerParams(vmem_limit_bytes=32 * MIB),
        cost_estimate=pl.CostEstimate(flops=6 * rows * model * model, bytes_accessed=10 * MIB, transcendentals=0),
        name="project",
    )(tokens, gain, w_qkv)
    chip_kv = exchange(kv_out, 0, lanes)
    wide = pltpu.VMEM((rows, model), F32)
    edges = pltpu.VMEM((rows, points), BF16)
    sums, totals, tops, high, low, x, wkv, wout = pl.pallas_call(
        functools.partial(own_kernel, head_dim),
        in_specs=[IN_VMEM] * 4 + [ANYWHERE] * 3,
        out_specs=[IN_VMEM] * 8,
        out_shape=[
            wide, wide, wide, edges, edges,
            pltpu.VMEM((rows, model), BF16), pltpu.VMEM((model, 2 * model), BF16), pltpu.VMEM((model, model), BF16),
        ],
        scratch_shapes=[pltpu.SemaphoreType.DMA((3,))],
        compiler_params=pltpu.CompilerParams(vmem_limit_bytes=24 * MIB),
        cost_estimate=pl.CostEstimate(
            flops=16 * rows * rows * model, bytes_accessed=10 * MIB, transcendentals=HEADS * rows * rows
        ),
        name="own_tokens",
    )(held(queries), held(kv), near, edge_weights, tokens, w_qkv, w_out)
    span = rows + FAR_ROWS
    return pl.pallas_call(
        functools.partial(far_kernel, head_dim),
        in_specs=[ANYWHERE] * 2 + [IN_VMEM] * 11,
        out_specs=IN_VMEM,
        out_shape=jax.ShapeDtypeStruct((dests, w_dec.shape[0], points // dests), BF16),
        scratch_shapes=[
            pltpu.VMEM((rows, model), BF16),
            pltpu.VMEM((2 * rows, 2 * model), BF16),
            pltpu.VMEM((rows // FAR_ROWS, FAR_ROWS, span), F32),
            pltpu.VMEM((rows, model), BF16),
            pltpu.SemaphoreType.DMA((2,)),
        ],
        compiler_params=pltpu.CompilerParams(vmem_limit_bytes=32 * MIB),
        cost_estimate=pl.CostEstimate(
            flops=2 * rows * model * 3 * model + 20 * rows * rows * model, bytes_accessed=8 * MIB, transcendentals=HEADS * rows * span
        ),
        name="neighbour_tokens",
    )(
        chip_kv, far, gain, held(queries), held(sums), held(totals), held(tops), held(high), held(low), held(x),
        held(wkv), held(wout), w_dec,
    )


def shards(tokens, ln_gain, w_qkv, w_out, neighbours, edge_weights, w_dec, truth):
    lanes = lax.axis_size("mp")
    far = exchange(tokens, 1, lanes)
    decoded = jnp.stack(
        [
            one_member(tokens[m], far[m], ln_gain, w_qkv, w_out, neighbours, edge_weights, w_dec)
            for m in range(tokens.shape[0])
        ]
    )
    gathered = lax.all_to_all(decoded, "ens", split_axis=1, concat_axis=0, tiled=True)
    gathered = gathered.reshape((-1,) + gathered.shape[2:])
    members = gathered.shape[0]
    coeff = ALPHA / (2.0 * members * (members - 1)) + (1.0 - ALPHA) / (2.0 * members * members)
    return pl.pallas_call(
        functools.partial(score_kernel, members, coeff),
        out_shape=jax.ShapeDtypeStruct(truth.shape, F32),
        name="scores",
    )(gathered, truth)


def solution(mesh):
    in_specs = (
        P("ens", "mp", None),
        P(),
        P(),
        P(),
        P(None, "mp"),
        P(None, "mp"),
        P(),
        P(None, ("mp", "ens")),
    )
    out_specs = P(None, ("mp", "ens"))
    return jax.shard_map(shards, mesh=mesh, in_specs=in_specs, out_specs=out_specs, check_vma=False)
```

time: 75.2 us -> 87.8 us (1.17)
  local copies, waits for them, and re-layouts: 9.95 us -> 30.9 us
  Pallas kernels: 40.3 us -> 33.7 us
  starting transfers between devices: 3.71 us -> 2.32 us
    unnamed x16 -> x56, local copies, waits for them, and re-layouts: 8.29 us -> 30.9 us
    pallas_call x2 -> x3, Pallas kernels: 38.2 us -> 31.6 us  [the longest x1 14.8 us: one_member(): pl.pallas_call(functools.partial(far_kernel, head_dim), in_specs=[ANYWHER...]
    pad x1 -> x0, local copies, waits for them, and re-layouts: 1.66 us -> none  [one_member(): jnp.pad(w_dec, ((0, tall - w_dec.shape[0]), (0, 0)))]
    ppermute x2, starting transfers between devices: 3.71 us -> 2.32 us  [exchange(): return lax.ppermute(value, 'mp', list(enumerate(partner)))]
  transfers between devices with their start and end apart: 2 -> 2, of which waited for: 0 -> 0; matrix products, arithmetic and copies ran while one was open for 3% -> 0% of each run, Pallas kernels for 17% -> 10%
where the time goes in v2:
time: 87.8 us; the launch traced here: 87.2 us
  Pallas kernels  33.7 us (38%)
  local copies, waits for them, and re-layouts  30.9 us (35%)
  blocking collectives  20.2 us (23%)
  starting transfers between devices  2.32 us (3%)
    unnamed x56, local copies, waits for them, and re-layouts  30.9 us
    all_to_all x1, blocking collectives, shards(): lax.all_to_all(decoded, 'ens', split_axis=1, concat_axis=0, tiled=True)  20.2 us
    pallas_call x1, Pallas kernels, one_member(): pl.pallas_call(functools.partial(far_kernel, head_dim), in_specs=[ANYWHER...  14.8 us
    pallas_call x1, Pallas kernels, one_member(): pl.pallas_call(functools.partial(own_kernel, head_dim), in_specs=[IN_VMEM...  8.7 us
    pallas_call x1, Pallas kernels, one_member(): pl.pallas_call(functools.partial(project_kernel, head_dim), grid=(3 * q_s...  8.15 us
    ppermute x2, starting transfers between devices, exchange(): return lax.ppermute(value, 'mp', list(enumerate(partner)))  2.32 us
    pallas_call x1, Pallas kernels, shards(): pl.pallas_call(functools.partial(score_kernel, members, coeff), out_shape...  2.08 us
  transfers between devices with their start and end apart: 2, of which 0 were waited for; matrix products, arithmetic and copies ran while one was open for 0% of the time, Pallas kernels for 10%

profile of v2, /device:TPU:0, one launch (start us, length us, event | category | flops | bytes accessed | tf_op | source)
XLA Modules:
  0.0 87.2 jit_solution(15733900790591516080)
XLA Ops:
  0.0 0.0 copy-start
  0.0 2.8 %copy-done = bf16[1024,3072]{1,0:T(8,128)(2,1)S(1)} copy-done((bf16[1024,3072]{1,0:T(8,128)(2,1)S(1)}, bf16[1024,3072]{1,0:T(8,128)(2,1)}, u32[]{:S(2)}) %copy-start) | copy-done | bytes 6291480
  2.8 0.0 copy-start.8
  2.8 0.7 copy-done.8
  3.5 0.0 copy-start.1
  3.5 0.0 copy-start.2
  3.5 0.0 copy-start.6
  3.5 0.0 copy-start.7
  3.5 8.2 %project.1 = (bf16[512,2048]{1,0:T(8,128)(2,1)}, bf16[512,1024]{1,0:T(8,128)(2,1)S(1)}, bf16[512,2048]{1,0:T(8,128)(2,1)S(1)}) custom-call(bf16[512,1024]{1,0:T(8,128)(2,1)} %bitcast.x_ref.x_hbm, f32[1,1024]{1,0:T(1,128)S(1)} %bitcast.9, bf16[1024,3072]{1,0:T(8,128)(2,1)S(1)} %copy-done), custom_call_target="tpu_custom_call" | custom-call | flops 3221225472 | bytes 10485760 | tf_op jit(solution)/shard_map/project/pallas_call | solution.py:272
  11.6 0.0 copy-start.12
  11.6 1.3 %copy-done.12 = bf16[512,2048]{1,0:T(8,128)(2,1)} copy-done((bf16[512,2048]{1,0:T(8,128)(2,1)}, bf16[512,2048]{1,0:T(8,128)(2,1)S(1)}, u32[]{:S(2)}) %copy-start.12) | copy-done | bytes 2097176
  13.0 0.0 copy-start.24
  13.0 0.5 collective-permute-start
  13.4 1.9 %collective-permute-start.1 = (bf16[1,512,1024]{2,1,0:T(8,128)(2,1)}, bf16[1,512,1024]{2,1,0:T(8,128)(2,1)S(1)}, u32[]{:S(2)}, u32[]{:S(2)}) collective-permute-start(bf16[1,512,1024]{2,1,0:T(8,128)(2,1)} %param.8), channel_id=1, source_target_pairs={{0,0},{1,2},{2,1},{3,3},{4,4},{5,6},{6,5},{7,7},{8,8},{9,10},{10,9... | collective-permute-start | bytes 3145736 | tf_op jit(solution)/shard_map/ppermute | solution.py:261
  15.3 0.0 copy-done.1
  15.3 0.0 copy-done.2
  15.3 0.0 copy-done.6
  15.3 0.0 copy-done.7
  15.3 0.0 copy-start.13
  15.3 1.6 %copy-done.13 = bf16[512,2048]{1,0:T(8,128)(2,1)S(1)} copy-done((bf16[512,2048]{1,0:T(8,128)(2,1)S(1)}, bf16[512,2048]{1,0:T(8,128)(2,1)}, u32[]{:S(2)}) %copy-start.13) | copy-done | bytes 2097176
  16.9 8.7 %own_tokens.1 = (f32[512,1024]{1,0:T(8,128)S(1)}, f32[512,1024]{1,0:T(8,128)S(1)}, f32[512,1024]{1,0:T(8,128)S(1)}, bf16[512,2048]{1,0:T(8,128)(2,1)S(1)}, bf16[...) custom-call(bf16[512,1024]{1,0:T(8,128)(2,1)S(1)} %get-tuple-element, ...), custom_call_target="tpu_custom_call" | custom-call | flops 4294967296 | bytes 10485760 | tf_op jit(solution)/shard_map/own_tokens/pallas_call | solution.py:294
  25.6 0.0 copy-done.24
  25.6 0.0 copy-start.10
  25.6 2.0 %copy-done.10 = bf16[1024,2048]{1,0:T(8,128)(2,1)} copy-done((bf16[1024,2048]{1,0:T(8,128)(2,1)}, bf16[1024,2048]{1,0:T(8,128)(2,1)S(1)}, u32[]{:S(2)}) %copy-start.10) | copy-done | bytes 4194328
  27.6 1.4 %copy-done.14 = f32[512,1024]{1,0:T(8,128)} copy-done((f32[512,1024]{1,0:T(8,128)}, f32[512,1024]{1,0:T(8,128)S(1)}, u32[]{:S(2)}) %copy-start.14) | copy-done | bytes 2097176
  29.0 1.4 %copy-done.16 = f32[512,1024]{1,0:T(8,128)} copy-done((f32[512,1024]{1,0:T(8,128)}, f32[512,1024]{1,0:T(8,128)S(1)}, u32[]{:S(2)}) %copy-start.16) | copy-done | bytes 2097176
  30.4 1.3 %copy-done.18 = f32[512,1024]{1,0:T(8,128)} copy-done((f32[512,1024]{1,0:T(8,128)}, f32[512,1024]{1,0:T(8,128)S(1)}, u32[]{:S(2)}) %copy-start.18) | copy-done | bytes 2097176
  31.7 1.3 %copy-done.20 = bf16[512,2048]{1,0:T(8,128)(2,1)} copy-done((bf16[512,2048]{1,0:T(8,128)(2,1)}, bf16[512,2048]{1,0:T(8,128)(2,1)S(1)}, u32[]{:S(2)}) %copy-start.20) | copy-done | bytes 2097176
  33.0 1.3 %copy-done.22 = bf16[512,2048]{1,0:T(8,128)(2,1)} copy-done((bf16[512,2048]{1,0:T(8,128)(2,1)}, bf16[512,2048]{1,0:T(8,128)(2,1)S(1)}, u32[]{:S(2)}) %copy-start.22) | copy-done | bytes 2097176
  34.3 1.0 %copy-done.26 = bf16[512,1024]{1,0:T(8,128)(2,1)} copy-done((bf16[512,1024]{1,0:T(8,128)(2,1)}, bf16[512,1024]{1,0:T(8,128)(2,1)S(1)}, u32[]{:S(2)}) %copy-start.26) | copy-done | bytes 1048600
  35.3 0.0 collective-permute-done.1
  35.3 1.0 %copy-done.3 = bf16[1,512,1024]{2,1,0:T(8,128)(2,1)} copy-done((bf16[1,512,1024]{2,1,0:T(8,128)(2,1)}, bf16[1,512,1024]{2,1,0:T(8,128)(2,1)S(1)}, u32[]{:S(2)}) %copy-start.3) | copy-done | bytes 1048600
  36.3 0.0 collective-permute-done.chip_kv_hbm
  36.3 0.0 copy-done.5
  36.3 0.0 copy-done.9
  36.3 0.0 copy-start.4
  36.3 1.2 %copy-done.4 = bf16[1,512,1024]{2,1,0:T(8,128)(2,1)S(1)} copy-done((bf16[1,512,1024]{2,1,0:T(8,128)(2,1)S(1)}, bf16[1,512,1024]{2,1,0:T(8,128)(2,1)}, u32[]{:S(2)}) %copy-start.4) | copy-done | bytes 1048600
  37.6 2.2 %copy-done.11 = bf16[1024,2048]{1,0:T(8,128)(2,1)S(1)} copy-done((bf16[1024,2048]{1,0:T(8,128)(2,1)S(1)}, bf16[1024,2048]{1,0:T(8,128)(2,1)}, u32[]{:S(2)}) %copy-start.11) | copy-done | bytes 4194328
  39.7 1.6 %copy-done.15 = f32[512,1024]{1,0:T(8,128)S(1)} copy-done((f32[512,1024]{1,0:T(8,128)S(1)}, f32[512,1024]{1,0:T(8,128)}, u32[]{:S(2)}) %copy-start.15) | copy-done | bytes 2097176
  41.3 1.6 %copy-done.17 = f32[512,1024]{1,0:T(8,128)S(1)} copy-done((f32[512,1024]{1,0:T(8,128)S(1)}, f32[512,1024]{1,0:T(8,128)}, u32[]{:S(2)}) %copy-start.17) | copy-done | bytes 2097176
  42.9 1.6 %copy-done.19 = f32[512,1024]{1,0:T(8,128)S(1)} copy-done((f32[512,1024]{1,0:T(8,128)S(1)}, f32[512,1024]{1,0:T(8,128)}, u32[]{:S(2)}) %copy-start.19) | copy-done | bytes 2097176
  44.5 1.6 %copy-done.21 = bf16[512,2048]{1,0:T(8,128)(2,1)S(1)} copy-done((bf16[512,2048]{1,0:T(8,128)(2,1)S(1)}, bf16[512,2048]{1,0:T(8,128)(2,1)}, u32[]{:S(2)}) %copy-start.21) | copy-done | bytes 2097176
  46.1 1.6 %copy-done.23 = bf16[512,2048]{1,0:T(8,128)(2,1)S(1)} copy-done((bf16[512,2048]{1,0:T(8,128)(2,1)S(1)}, bf16[512,2048]{1,0:T(8,128)(2,1)}, u32[]{:S(2)}) %copy-start.23) | copy-done | bytes 2097176
  47.7 1.2 %copy-done.25 = bf16[512,1024]{1,0:T(8,128)(2,1)S(1)} copy-done((bf16[512,1024]{1,0:T(8,128)(2,1)S(1)}, bf16[512,1024]{1,0:T(8,128)(2,1)}, u32[]{:S(2)}) %copy-start.25) | copy-done | bytes 1048600
  48.9 1.2 %copy-done.27 = bf16[512,1024]{1,0:T(8,128)(2,1)S(1)} copy-done((bf16[512,1024]{1,0:T(8,128)(2,1)S(1)}, bf16[512,1024]{1,0:T(8,128)(2,1)}, u32[]{:S(2)}) %copy-start.27) | copy-done | bytes 1048600
  50.1 14.8 %neighbour_tokens.1 = bf16[8,100,256]{2,1,0:T(8,128)(2,1)S(1)} custom-call(bf16[512,2048]{1,0:T(8,128)(2,1)S(1)} %collective-permute-done.chip_kv_hbm, bf16[512,1024]{1,0:T(8,128)(2,1)S(1)} %bitcast.8, f32[1,1024]{1,0:T(1,128)S(1)} %bitcast.10, bf16[512,1024]{1,0:T(8,128)(2,1)S(1)} %copy-done.25, f32[512,1024]{1,0:T(8,128)S(1)} %copy-done.15, ...), custom_call_target="tpu_custom_call" | custom-call | flops 8589934592 | bytes 8388608 | tf_op jit(solution)/shard_map/neighbour_tokens/pallas_call | solution.py:310
  64.9 20.2 %all_to_all.4 = bf16[1,8,100,256]{3,2,0,1:T(8,128)(2,1)} all-to-all(bf16[1,8,100,256]{3,2,0,1:T(8,128)(2,1)S(1)} %bitcast.7), channel_id=1, replica_groups=mesh['ens'=8,'mp'=4] {'ens'}, dimensions={1} | all-to-all | bytes 819200 | tf_op jit(solution)/shard_map/all_to_all | solution.py:342
  85.1 2.1 %scores.1 = f32[100,256]{1,0:T(8,128)} custom-call(bf16[8,100,256]{2,1,0:T(8,128)(2,1)} %bitcast.11, f32[100,256]{1,0:T(8,128)} %truth_ref.1), custom_call_target="tpu_custom_call" | custom-call | tf_op jit(solution)/shard_map/scores/pallas_call | solution.py:346
  (17 shorter events, 0.0 us)
Async XLA Ops:
  0.0 2.8 %copy-start = (bf16[1024,3072]{1,0:T(8,128)(2,1)S(1)}, bf16[1024,3072]{1,0:T(8,128)(2,1)}, u32[]{:S(2)}) copy-start(bf16[1024,3072]{1,0:T(8,128)(2,1)} %w_hbm.1) | copy-start | bytes 18874372
  2.8 0.7 copy-start.8
  3.5 11.8 %copy-start.1 = (bf16[1024,3072]{1,0:T(8,128)(2,1)S(1)}, bf16[1024,3072]{1,0:T(8,128)(2,1)}, u32[]{:S(2)}) copy-start(bf16[1024,3072]{1,0:T(8,128)(2,1)} %w_hbm.1) | copy-start | bytes 18874372
  3.5 11.8 %copy-start.2 = (bf16[1024,1024]{1,0:T(8,128)(2,1)S(1)}, bf16[1024,1024]{1,0:T(8,128)(2,1)}, u32[]{:S(2)}) copy-start(bf16[1024,1024]{1,0:T(8,128)(2,1)} %wout_hbm.1) | copy-start | bytes 6291460
  3.5 11.8 %copy-start.6 = (s32[4,2048]{1,0:T(4,128)S(1)}, s32[4,2048]{1,0:T(4,128)}, u32[]{:S(2)}) copy-start(s32[4,2048]{1,0:T(4,128)} %near_ref.1) | copy-start | bytes 98308
  3.5 11.8 %copy-start.7 = (f32[4,2048]{1,0:T(4,128)S(1)}, f32[4,2048]{1,0:T(4,128)}, u32[]{:S(2)}) copy-start(f32[4,2048]{1,0:T(4,128)} %edge_ref.1) | copy-start | bytes 98308
  11.6 1.3 %copy-start.12 = (bf16[512,2048]{1,0:T(8,128)(2,1)}, bf16[512,2048]{1,0:T(8,128)(2,1)S(1)}, u32[]{:S(2)}) copy-start(bf16[512,2048]{1,0:T(8,128)(2,1)S(1)} %get-tuple-element.18.kv_ref) | copy-start | bytes 6291460
  13.0 12.6 %copy-start.24 = (bf16[512,1024]{1,0:T(8,128)(2,1)}, bf16[512,1024]{1,0:T(8,128)(2,1)S(1)}, u32[]{:S(2)}) copy-start(bf16[512,1024]{1,0:T(8,128)(2,1)S(1)} %get-tuple-element.17.q_ref) | copy-start | bytes 3145732
  13.0 23.3 %collective-permute-start = (bf16[512,2048]{1,0:T(8,128)(2,1)}, bf16[512,2048]{1,0:T(8,128)(2,1)S(1)}, u32[]{:S(2)}, u32[]{:S(2)}) collective-permute-start(bf16[512,2048]{1,0:T(8,128)(2,1)} %get-tuple-element.16), channel_id=1, source_target_pairs={{0,1},{1,0},{2,3},{3,2},{4,5},{5,4},{6,7},{7,6},{8,9},{9,8},{10,11... | collective-permute-start | bytes 6291464 | tf_op jit(solution)/shard_map/ppermute | solution.py:261
  13.4 21.9 %collective-permute-start.1 = (bf16[1,512,1024]{2,1,0:T(8,128)(2,1)}, bf16[1,512,1024]{2,1,0:T(8,128)(2,1)S(1)}, u32[]{:S(2)}, u32[]{:S(2)}) collective-permute-start(bf16[1,512,1024]{2,1,0:T(8,128)(2,1)} %param.8), channel_id=1, source_target_pairs={{0,0},{1,2},{2,1},{3,3},{4,4},{5,6},{6,5},{7,7},{8,8},{9,10},{10,9... | collective-permute-start | bytes 3145736 | tf_op jit(solution)/shard_map/ppermute | solution.py:261
  15.3 1.6 %copy-start.13 = (bf16[512,2048]{1,0:T(8,128)(2,1)S(1)}, bf16[512,2048]{1,0:T(8,128)(2,1)}, u32[]{:S(2)}) copy-start(bf16[512,2048]{1,0:T(8,128)(2,1)} %copy-done.12) | copy-start | bytes 6291460
  16.9 19.4 %copy-start.5 = (bf16[100,1024]{1,0:T(8,128)(2,1)S(1)}, bf16[100,1024]{1,0:T(8,128)(2,1)}, u32[]{:S(2)}) copy-start(bf16[100,1024]{1,0:T(8,128)(2,1)} %wdec_ref.1) | copy-start | bytes 614404
  16.9 19.4 %copy-start.9 = (f32[1024]{0:T(1024)S(1)}, f32[1024]{0:T(1024)}, u32[]{:S(2)}) copy-start(f32[1024]{0:T(1024)} %param.9) | copy-start | bytes 12292
  25.6 2.0 %copy-start.10 = (bf16[1024,2048]{1,0:T(8,128)(2,1)}, bf16[1024,2048]{1,0:T(8,128)(2,1)S(1)}, u32[]{:S(2)}) copy-start(bf16[1024,2048]{1,0:T(8,128)(2,1)S(1)} %get-tuple-element.25.wkv_ref) | copy-start | bytes 12582916
  27.6 1.4 %copy-start.14 = (f32[512,1024]{1,0:T(8,128)}, f32[512,1024]{1,0:T(8,128)S(1)}, u32[]{:S(2)}) copy-start(f32[512,1024]{1,0:T(8,128)S(1)} %get-tuple-element.19.sum_ref) | copy-start | bytes 6291460
  29.0 1.4 %copy-start.16 = (f32[512,1024]{1,0:T(8,128)}, f32[512,1024]{1,0:T(8,128)S(1)}, u32[]{:S(2)}) copy-start(f32[512,1024]{1,0:T(8,128)S(1)} %get-tuple-element.20.total_ref) | copy-start | bytes 6291460
  30.4 1.4 %copy-start.18 = (f32[512,1024]{1,0:T(8,128)}, f32[512,1024]{1,0:T(8,128)S(1)}, u32[]{:S(2)}) copy-start(f32[512,1024]{1,0:T(8,128)S(1)} %get-tuple-element.21.top_ref) | copy-start | bytes 6291460
  31.7 1.3 %copy-start.20 = (bf16[512,2048]{1,0:T(8,128)(2,1)}, bf16[512,2048]{1,0:T(8,128)(2,1)S(1)}, u32[]{:S(2)}) copy-start(bf16[512,2048]{1,0:T(8,128)(2,1)S(1)} %get-tuple-element.22.high_ref) | copy-start | bytes 6291460
  33.0 1.3 %copy-start.22 = (bf16[512,2048]{1,0:T(8,128)(2,1)}, bf16[512,2048]{1,0:T(8,128)(2,1)S(1)}, u32[]{:S(2)}) copy-start(bf16[512,2048]{1,0:T(8,128)(2,1)S(1)} %get-tuple-element.23.low_ref) | copy-start | bytes 6291460
  34.3 1.0 %copy-start.26 = (bf16[512,1024]{1,0:T(8,128)(2,1)}, bf16[512,1024]{1,0:T(8,128)(2,1)S(1)}, u32[]{:S(2)}) copy-start(bf16[512,1024]{1,0:T(8,128)(2,1)S(1)} %get-tuple-element.24.x_ref) | copy-start | bytes 3145732
  35.3 1.0 %copy-start.3 = (bf16[1,512,1024]{2,1,0:T(8,128)(2,1)}, bf16[1,512,1024]{2,1,0:T(8,128)(2,1)S(1)}, u32[]{:S(2)}) copy-start(bf16[1,512,1024]{2,1,0:T(8,128)(2,1)S(1)} %collective-permute-done.1) | copy-start | bytes 3145732
  36.3 1.2 %copy-start.4 = (bf16[1,512,1024]{2,1,0:T(8,128)(2,1)S(1)}, bf16[1,512,1024]{2,1,0:T(8,128)(2,1)}, u32[]{:S(2)}) copy-start(bf16[1,512,1024]{2,1,0:T(8,128)(2,1)} %copy-done.3) | copy-start | bytes 3145732
  37.5 2.2 %copy-start.11 = (bf16[1024,2048]{1,0:T(8,128)(2,1)S(1)}, bf16[1024,2048]{1,0:T(8,128)(2,1)}, u32[]{:S(2)}) copy-start(bf16[1024,2048]{1,0:T(8,128)(2,1)} %copy-done.10) | copy-start | bytes 12582916
  39.7 1.6 %copy-start.15 = (f32[512,1024]{1,0:T(8,128)S(1)}, f32[512,1024]{1,0:T(8,128)}, u32[]{:S(2)}) copy-start(f32[512,1024]{1,0:T(8,128)} %copy-done.14) | copy-start | bytes 6291460
  41.3 1.6 %copy-start.17 = (f32[512,1024]{1,0:T(8,128)S(1)}, f32[512,1024]{1,0:T(8,128)}, u32[]{:S(2)}) copy-start(f32[512,1024]{1,0:T(8,128)} %copy-done.16) | copy-start | bytes 6291460
  42.9 1.6 %copy-start.19 = (f32[512,1024]{1,0:T(8,128)S(1)}, f32[512,1024]{1,0:T(8,128)}, u32[]{:S(2)}) copy-start(f32[512,1024]{1,0:T(8,128)} %copy-done.18) | copy-start | bytes 6291460
  44.5 1.6 %copy-start.21 = (bf16[512,2048]{1,0:T(8,128)(2,1)S(1)}, bf16[512,2048]{1,0:T(8,128)(2,1)}, u32[]{:S(2)}) copy-start(bf16[512,2048]{1,0:T(8,128)(2,1)} %copy-done.20) | copy-start | bytes 6291460
  46.1 1.6 %copy-start.23 = (bf16[512,2048]{1,0:T(8,128)(2,1)S(1)}, bf16[512,2048]{1,0:T(8,128)(2,1)}, u32[]{:S(2)}) copy-start(bf16[512,2048]{1,0:T(8,128)(2,1)} %copy-done.22) | copy-start | bytes 6291460
  47.7 1.2 %copy-start.25 = (bf16[512,1024]{1,0:T(8,128)(2,1)S(1)}, bf16[512,1024]{1,0:T(8,128)(2,1)}, u32[]{:S(2)}) copy-start(bf16[512,1024]{1,0:T(8,128)(2,1)} %copy-done.24) | copy-start | bytes 3145732
  48.9 1.2 %copy-start.27 = (bf16[512,1024]{1,0:T(8,128)(2,1)S(1)}, bf16[512,1024]{1,0:T(8,128)(2,1)}, u32[]{:S(2)}) copy-start(bf16[512,1024]{1,0:T(8,128)(2,1)} %copy-done.26) | copy-start | bytes 3145732

commit v3 on v2

v3 whole, which is shorter than its diff:
```python
import functools

import jax
import jax.numpy as jnp
from jax import lax
from jax.experimental import pallas as pl
from jax.experimental.pallas import tpu as pltpu
from jax.sharding import PartitionSpec as P

HEADS = 16
NEIGH = 4
HALF = 512
ALPHA = 0.95
EPS = 1e-05
MASKED = -1e30
STEP_COLS = 1024
LN_ROWS = 128
STEP_PAIRS = 4
FULL_STEPS = 1
OWN_ROWS = 256
AHEAD = 1
LAG = 0
FAR_ROWS = 128
EDGE_ROWS = 256
EDGE_COLS = 512

BF16 = jnp.bfloat16
F32 = jnp.float32
MIB = 1024 * 1024
VMEM_LIMIT = 63 * MIB
LONG = pl.CostEstimate(flops=MIB * MIB, bytes_accessed=MIB, transcendentals=0)


def dot(a, b):
    return lax.dot_general(a, b, (((1,), (0,)), ((), ())), preferred_element_type=F32)


def dot_nt(a, b):
    return lax.dot_general(a, b, (((1,), (1,)), ((), ())), preferred_element_type=F32)


def layer_norm(inputs, ln_gain):
    values = inputs.astype(F32)
    average = jnp.mean(values, axis=-1, keepdims=True)
    centred = values - average
    variance = jnp.mean(centred * centred, axis=-1, keepdims=True)
    return (centred * lax.rsqrt(variance + EPS) * ln_gain).astype(BF16)


def halves(width):
    lane = lax.broadcasted_iota(jnp.int32, (1, width), 1)
    first = (lane < width // 2).astype(F32)
    return first.astype(BF16), (1.0 - first).astype(BF16)


def value_sides(values, masks):
    return [jnp.concatenate([values * mask, jnp.broadcast_to(mask, values.shape)], axis=1) for mask in masks]


def pair_weigh(scores, bias):
    count = scores.shape[1] // 2
    tops, weights = [], []
    for side in range(2):
        kept = scores[:, side * count : (side + 1) * count]
        if bias is not None:
            kept = kept + bias
        top = jnp.max(kept, axis=-1, keepdims=True)
        weights.append(jnp.exp(kept - top).astype(BF16))
        tops.append(top)
    return jnp.concatenate(weights, axis=1), tops


def pair_sums(weights, tops, values_ext):
    both = dot(weights, values_ext)
    width = both.shape[1] // 2
    lane = lax.broadcasted_iota(jnp.int32, (both.shape[0], width), 1)
    return both[:, :width], both[:, width:], jnp.where(lane < width // 2, tops[0], tops[1])


def in_turn(items, score, weigh, finish):
    scored, weighed = [], []
    for i in range(len(items) + AHEAD + LAG):
        if i < len(items):
            scored.append(score(items[i]))
        if AHEAD <= i < len(items) + AHEAD:
            weighed.append(weigh(items[i - AHEAD], scored[i - AHEAD]))
        if i >= AHEAD + LAG:
            finish(items[i - AHEAD - LAG], weighed[i - AHEAD - LAG])


def project_kernel(head_dim, x_hbm, w_hbm, gain_ref, q_hbm, kv_hbm, x_ref, w_ref, made_ref, x_sem, w_sems, out_sems):
    steps, rows, width = made_ref.shape
    model = x_ref.shape[1]
    q_steps = model // width
    x_copy = pltpu.make_async_copy(x_hbm, x_ref, x_sem)
    x_copy.start()
    ins, outs = [], []
    for step in range(steps):
        cols = pl.ds(step * width, width)
        target = q_hbm.at[:, cols] if step < q_steps else kv_hbm.at[:, pl.ds((step - q_steps) * width, width)]
        ins.append(pltpu.make_async_copy(w_hbm.at[:, cols], w_ref.at[step], w_sems.at[step]))
        outs.append(pltpu.make_async_copy(made_ref.at[step], target, out_sems.at[step]))
    for copy in ins:
        copy.start()
    x_copy.wait()
    for first in range(0, rows, LN_ROWS):
        here = slice(first, first + LN_ROWS)
        x_ref[here] = layer_norm(x_ref[here], gain_ref[...])
    for step in range(steps):
        ins[step].wait()
        made = dot(x_ref[...], w_ref[step]).astype(BF16)
        if step < q_steps:
            made = (made.astype(F32) * head_dim**-0.5).astype(BF16)
        made_ref[step] = made
        outs[step].start()
    for copy in outs:
        copy.wait()


def edge_matrix(near, edge, high_ref, low_ref):
    rows = high_ref.shape[0]
    points = near.shape[1]
    totals = []
    for k in range(NEIGH):
        total = jnp.zeros((1, points), F32)
        for j in range(NEIGH):
            total += jnp.where(near[j : j + 1] == near[k : k + 1], edge[j : j + 1], 0.0)
        totals.append(total)
    highs = [t.astype(BF16) for t in totals]
    lows = [(t - h.astype(F32)).astype(BF16) for t, h in zip(totals, highs)]
    shape = (EDGE_ROWS, points)
    token = lax.broadcasted_iota(jnp.int32, shape, 0).astype(F32).astype(BF16)
    for first in range(0, rows, EDGE_ROWS):
        high = jnp.zeros(shape, BF16)
        low = jnp.zeros(shape, BF16)
        for k in range(NEIGH):
            row = near[k : k + 1] - first
            row = jnp.where((row >= 0) & (row < EDGE_ROWS), row, -1).astype(F32).astype(BF16)
            hit = token == row
            high = jnp.where(hit, highs[k], high)
            low = jnp.where(hit, lows[k], low)
        high_ref[first : first + EDGE_ROWS] = high
        low_ref[first : first + EDGE_ROWS] = low


def own_kernel(head_dim, q_hbm, kv_hbm, *refs):
    out_hbms, (q_ref, k_ref, v_ref), out_refs, (in_sems, out_sems) = refs[:3], refs[3:6], refs[6:9], refs[9:]
    pairs, rows, width = q_ref.shape
    model = q_hbm.shape[1]
    skipped = model - pairs * width
    ins, outs = [], []
    for p in range(pairs):
        here, there = pl.ds(p * width, width), pl.ds(skipped + p * width, width)
        sources = (q_hbm.at[:, there], kv_hbm.at[:, there], kv_hbm.at[:, pl.ds(model + skipped + p * width, width)])
        ins.append(
            [
                pltpu.make_async_copy(source, target.at[p], in_sems.at[p, i])
                for i, (source, target) in enumerate(zip(sources, (q_ref, k_ref, v_ref)))
            ]
        )
        outs.append(
            [
                pltpu.make_async_copy(source.at[p], target.at[:, here], out_sems.at[p, i])
                for i, (source, target) in enumerate(zip(out_refs, out_hbms))
            ]
        )
    for group in ins:
        for copy in group:
            copy.start()
    masks = halves(width)
    sides = {}

    def score(item):
        p, row = item
        if row == 0:
            for copy in ins[p]:
                copy.wait()
            sides[p] = (
                jnp.concatenate([k_ref[p] * mask for mask in masks], axis=0),
                jnp.concatenate(value_sides(v_ref[p], masks), axis=0),
            )
        return dot_nt(q_ref[p, row : row + OWN_ROWS], sides[p][0])

    def finish(item, weighed):
        p, row = item
        for out_ref, made in zip(out_refs, pair_sums(*weighed, sides[p][1])):
            out_ref[p, row : row + OWN_ROWS] = made
        if row + OWN_ROWS == rows:
            for copy in outs[p]:
                copy.start()

    in_turn([(p, row) for p in range(pairs) for row in range(0, rows, OWN_ROWS)], score, lambda _, s: pair_weigh(s, None), finish)
    for group in outs:
        for copy in group:
            copy.wait()


def window_bias(count, rows, span, left_ok, right_ok, first):
    query = first + lax.broadcasted_iota(jnp.int32, (count, span), 0)
    key = first + lax.broadcasted_iota(jnp.int32, (count, span), 1)
    position = jnp.where(key < rows, key - rows, key)
    near = jnp.abs(position - query) <= HALF
    there = jnp.where(key < rows, left_ok, right_ok) > 0
    return jnp.where(near & there, 0.0, MASKED).astype(F32)


def far_kernel(
    head_dim, far_hbm, w_hbm, chip_kv_hbm, own_kv_hbm, q_hbm, sum_hbm, total_hbm, top_hbm, wout_hbm, x_hbm,
    gain_ref, wdec_ref, near_ref, edge_ref,
    out_ref,
    far_ref, w_ref, kv_ref, q_ref, sum_ref, total_ref, top_ref, wout_ref, x_ref, high_ref, low_ref,
    bias_ref, context_ref, sems, step_sems,
):
    rows, model = q_ref.shape
    lane = lax.axis_index("mp")
    lanes = lax.axis_size("mp")
    odd = lane % 2
    chip_at = pl.ds(pl.multiple_of((1 - odd) * 2 * rows, rows), rows)
    far_at = pl.ds(pl.multiple_of(odd * 2 * rows, rows), rows)
    own_at = pl.ds(rows, rows)
    pair = 2 * head_dim
    width = pair * STEP_PAIRS
    steps = model // width
    far_copy = pltpu.make_async_copy(far_hbm, far_ref, sems.at[0])
    last_copies = [
        pltpu.make_async_copy(wout_hbm, wout_ref, sems.at[1]),
        pltpu.make_async_copy(x_hbm, x_ref, sems.at[2]),
    ]
    weight_copies, step_copies = [], []
    for step in range(steps):
        cols = pl.ds(step * width, width)
        sides = [cols, pl.ds(model + step * width, width)]
        weights = [(w_hbm.at[:, pl.ds(model + s.start, width)], w_ref.at[:, s]) for s in sides]
        moves = [(chip_kv_hbm.at[:, s], kv_ref.at[chip_at, s]) for s in sides] + [(q_hbm.at[:, cols], q_ref.at[:, cols])]
        if step < FULL_STEPS:
            moves += [(own_kv_hbm.at[:, s], kv_ref.at[own_at, s]) for s in sides]
        else:
            kept = pl.ds((step - FULL_STEPS) * width, width)
            moves += [
                (a.at[:, kept], b.at[:, kept])
                for a, b in ((sum_hbm, sum_ref), (total_hbm, total_ref), (top_hbm, top_ref))
            ]
        made = [pltpu.make_async_copy(a, b, step_sems.at[step, i]) for i, (a, b) in enumerate(weights + moves)]
        weight_copies.append(made[:2])
        step_copies.append(made[2:])

    far_copy.start()
    for copy in weight_copies[0] + step_copies[0]:
        copy.start()
    span = rows + FAR_ROWS
    left_ok = (lane > 0).astype(jnp.int32)
    right_ok = (lane < lanes - 1).astype(jnp.int32)
    parts = rows // FAR_ROWS
    for part in range(parts):
        bias_ref[part] = window_bias(FAR_ROWS, rows, span, left_ok, right_ok, part * FAR_ROWS)
    for first in range(0, near_ref.shape[1], EDGE_COLS):
        cols = slice(first, first + EDGE_COLS)
        edge_matrix(near_ref[:, cols] - lane * rows, edge_ref[:, cols], high_ref.at[:, cols], low_ref.at[:, cols])
    far_copy.wait()
    for first in range(0, rows, LN_ROWS):
        here = slice(first, first + LN_ROWS)
        far_ref[here] = layer_norm(far_ref[here], gain_ref[...])

    masks = halves(pair)
    for step in range(steps):
        later = weight_copies[step + 1] + step_copies[step + 1] if step + 1 < steps else last_copies
        for side, copy in enumerate(weight_copies[step]):
            cols = slice(side * model + step * width, side * model + (step + 1) * width)
            copy.wait()
            kv_ref[far_at, cols] = dot(far_ref[...], w_ref[:, cols]).astype(BF16)
        for copy in step_copies[step]:
            copy.wait()
        for copy in later:
            copy.start()
        full = step < FULL_STEPS
        sides = {}

        def window(part, full=full):
            left, right = slice(part * FAR_ROWS, rows), slice(2 * rows, 2 * rows + (part + 1) * FAR_ROWS)
            return [slice(left.start, right.stop)] if full else [left, right]

        def score(item, sides=sides, window=window):
            first, part = item
            cols = slice(first, first + pair)
            if part == 0:
                sides[first] = (
                    [kv_ref[:, cols] * mask for mask in masks],
                    value_sides(kv_ref[:, model + first : model + first + pair], masks),
                )
            keys = [k[w] for k in sides[first][0] for w in window(part)]
            return dot_nt(q_ref[part * FAR_ROWS : (part + 1) * FAR_ROWS, cols], jnp.concatenate(keys, axis=0))

        def weigh(item, scores, full=full):
            part = item[1]
            bias = bias_ref[part]
            if full:
                reach = rows - part * FAR_ROWS
                bias = jnp.concatenate([bias[:, :reach], jnp.zeros((FAR_ROWS, rows), F32), bias[:, reach:]], axis=1)
            return pair_weigh(scores, bias)

        def finish(item, weighed, sides=sides, window=window, full=full):
            first, part = item
            here = slice(part * FAR_ROWS, (part + 1) * FAR_ROWS)
            values = [v[w] for v in sides[first][1] for w in window(part)]
            sums, totals, top = pair_sums(*weighed, jnp.concatenate(values, axis=0))
            if not full:
                kept = slice(first - FULL_STEPS * width, first - FULL_STEPS * width + pair)
                own_top = top_ref[here, kept]
                best = jnp.maximum(top, own_top)
                scale, own_scale = jnp.exp(top - best), jnp.exp(own_top - best)
                sums = sums * scale + sum_ref[here, kept] * own_scale
                totals = totals * scale + total_ref[here, kept] * own_scale
            context_ref[here, first : first + pair] = (sums / totals).astype(BF16)

        firsts = range(step * width, (step + 1) * width, pair)
        in_turn([(first, part) for first in firsts for part in range(parts)], score, weigh, finish)

    for copy in last_copies:
        copy.wait()
    processed = (x_ref[...].astype(F32) + dot(context_ref[...], wout_ref[...])).astype(BF16)
    fields = dot_nt(wdec_ref[...], processed)
    variables, each = out_ref.shape[1:]
    tall = -(-variables // 16) * 16
    fields = jnp.concatenate([fields, jnp.zeros((tall - variables, rows), F32)], axis=0)
    fields_high = fields.astype(BF16)
    fields_low = (fields - fields_high.astype(F32)).astype(BF16)
    both = jnp.concatenate([fields_high, fields_low], axis=0)
    for d in range(out_ref.shape[0]):
        cols = slice(d * each, (d + 1) * each)
        product = dot(both, high_ref[:, cols])
        decoded = product[:tall] + product[tall:] + dot(fields_high, low_ref[:, cols])
        out_ref[d] = decoded[:variables].astype(BF16)


def score_kernel(members, coeff, fields_ref, truth_ref, out_ref):
    fields = [fields_ref[m].astype(F32) for m in range(members)]
    truth = truth_ref[...]
    skill = sum(jnp.abs(f - truth) for f in fields) / members
    spread = sum(jnp.abs(fields[j] - fields[k]) for j in range(members) for k in range(j))
    out_ref[...] = skill - (2.0 * coeff) * spread


IN_VMEM = pl.BlockSpec(memory_space=pltpu.VMEM)
ANYWHERE = pl.BlockSpec(memory_space=pl.ANY)
IN_HBM = pl.BlockSpec(memory_space=pltpu.HBM)


def exchange(value, first, lanes):
    pairs = [(i, i + 1) for i in range(first, lanes - 1, 2)]
    return lax.ppermute(value, "mp", pairs + [(j, i) for i, j in pairs])


def project(tokens, gain, w_qkv):
    rows, model = tokens.shape
    steps = 3 * model // STEP_COLS
    return pl.pallas_call(
        functools.partial(project_kernel, model // HEADS),
        in_specs=[IN_HBM, IN_HBM, IN_VMEM],
        out_specs=[IN_HBM, IN_HBM],
        out_shape=[jax.ShapeDtypeStruct((rows, model), BF16), jax.ShapeDtypeStruct((rows, 2 * model), BF16)],
        scratch_shapes=[
            pltpu.VMEM((rows, model), BF16),
            pltpu.VMEM((steps, model, STEP_COLS), BF16),
            pltpu.VMEM((steps, rows, STEP_COLS), BF16),
            pltpu.SemaphoreType.DMA,
            pltpu.SemaphoreType.DMA((steps,)),
            pltpu.SemaphoreType.DMA((steps,)),
        ],
        compiler_params=pltpu.CompilerParams(vmem_limit_bytes=VMEM_LIMIT),
        cost_estimate=LONG,
        name="project",
    )(tokens, w_qkv, gain)


def own_attention(queries, kv):
    rows, model = queries.shape
    pair = 2 * model // HEADS
    pairs = HEADS // 2 - FULL_STEPS * STEP_PAIRS
    held = lambda dtype: pltpu.VMEM((pairs, rows, pair), dtype)
    return pl.pallas_call(
        functools.partial(own_kernel, model // HEADS),
        in_specs=[IN_HBM] * 2,
        out_specs=[IN_HBM] * 3,
        out_shape=[jax.ShapeDtypeStruct((rows, pairs * pair), F32)] * 3,
        scratch_shapes=[held(BF16)] * 3
        + [held(F32)] * 3
        + [pltpu.SemaphoreType.DMA((pairs, 3)), pltpu.SemaphoreType.DMA((pairs, 3))],
        compiler_params=pltpu.CompilerParams(vmem_limit_bytes=VMEM_LIMIT),
        cost_estimate=LONG,
        name="own_tokens",
    )(queries, kv)


def far_attention(
    far, w_qkv, chip_kv, own_kv, queries, sums, totals, tops, w_out, tokens, gain, w_dec, near, edge_weights, dests
):
    rows, model = tokens.shape
    points = near.shape[1]
    span = rows + FAR_ROWS
    steps = HEADS // (2 * STEP_PAIRS)
    held = lambda dtype, cols=model: pltpu.VMEM((rows, cols), dtype)
    return pl.pallas_call(
        functools.partial(far_kernel, model // HEADS),
        in_specs=[IN_HBM] * 10 + [IN_VMEM] * 4,
        out_specs=IN_VMEM,
        out_shape=jax.ShapeDtypeStruct((dests, w_dec.shape[0], points // dests), BF16),
        scratch_shapes=[
            held(BF16), pltpu.VMEM((model, 2 * model), BF16), pltpu.VMEM((3 * rows, 2 * model), BF16), held(BF16),
            held(F32, sums.shape[1]), held(F32, sums.shape[1]), held(F32, sums.shape[1]),
            pltpu.VMEM((model, model), BF16), held(BF16),
            held(BF16, points), held(BF16, points),
            pltpu.VMEM((rows // FAR_ROWS, FAR_ROWS, span), F32), held(BF16), pltpu.SemaphoreType.DMA((3,)),
            pltpu.SemaphoreType.DMA((steps, 8)),
        ],
        compiler_params=pltpu.CompilerParams(vmem_limit_bytes=VMEM_LIMIT),
        cost_estimate=LONG,
        name="neighbour_tokens",
    )(far, w_qkv, chip_kv, own_kv, queries, sums, totals, tops, w_out, tokens, gain, w_dec, near, edge_weights)


def one_member(tokens, far, ln_gain, w_qkv, w_out, near, edge_weights, w_dec):
    gain = ln_gain[None]
    queries, kv = project(tokens, gain, w_qkv)
    chip_kv = exchange(kv, 0, lax.axis_size("mp"))
    state = own_attention(queries, kv)
    return far_attention(
        far, w_qkv, chip_kv, kv, queries, *state, w_out, tokens, gain, w_dec, near, edge_weights, lax.axis_size("ens")
    )


def shards(tokens, ln_gain, w_qkv, w_out, neighbours, edge_weights, w_dec, truth):
    far = exchange(tokens, 1, lax.axis_size("mp"))
    decoded = jnp.stack(
        [
            one_member(tokens[m], far[m], ln_gain, w_qkv, w_out, neighbours, edge_weights, w_dec)
            for m in range(tokens.shape[0])
        ]
    )
    gathered = lax.all_to_all(decoded, "ens", split_axis=1, concat_axis=0, tiled=True)
    gathered = gathered.reshape((-1,) + gathered.shape[2:])
    members = gathered.shape[0]
    coeff = ALPHA / (2.0 * members * (members - 1)) + (1.0 - ALPHA) / (2.0 * members * members)
    return pl.pallas_call(
        functools.partial(score_kernel, members, coeff),
        out_shape=jax.ShapeDtypeStruct(truth.shape, F32),
        name="scores",
    )(gathered, truth)


def solution(mesh):
    in_specs = (
        P("ens", "mp", None),
        P(),
        P(),
        P(),
        P(None, "mp"),
        P(None, "mp"),
        P(),
        P(None, ("mp", "ens")),
    )
    out_specs = P(None, ("mp", "ens"))
    return jax.shard_map(shards, mesh=mesh, in_specs=in_specs, out_specs=out_specs, check_vma=False)
```

time: 87.8 us -> 60.6 us (0.69)
  local copies, waits for them, and re-layouts: 30.9 us -> 0 us
  Pallas kernels: 33.7 us -> 36.5 us
  starting transfers between devices: 2.32 us -> 5.03 us
  blocking collectives: 20.2 us -> 18.7 us
    unnamed x56 -> x0, local copies, waits for them, and re-layouts: 30.9 us -> none
    pallas_call x3, Pallas kernels: 31.6 us -> 34.4 us  [the longest x1 20.1 us: far_attention(): pl.pallas_call(functools.partial(far_kernel, model // HEADS), in_specs=[I...]
    ppermute x2, starting transfers between devices: 2.32 us -> 5.03 us  [exchange(): return lax.ppermute(value, 'mp', pairs + [(j, i) for i, j in pairs])]
    all_to_all x1, blocking collectives: 20.2 us -> 18.7 us  [shards(): lax.all_to_all(decoded, 'ens', split_axis=1, concat_axis=0, tiled=True)]
  transfers between devices with their start and end apart: 2 -> 2, of which waited for: 0 -> 0; matrix products, arithmetic and copies ran while one was open for 0% -> 0% of each run, Pallas kernels for 10% -> 24%
where the time goes in v3:
time: 60.6 us; the launch traced here: 60.3 us
  Pallas kernels  36.5 us (60%)
  blocking collectives  18.7 us (31%)
  starting transfers between devices  5.03 us (8%)
    pallas_call x1, Pallas kernels, far_attention(): pl.pallas_call(functools.partial(far_kernel, model // HEADS), in_specs=[I...  20.1 us
    all_to_all x1, blocking collectives, shards(): lax.all_to_all(decoded, 'ens', split_axis=1, concat_axis=0, tiled=True)  18.7 us
    pallas_call x1, Pallas kernels, project(): pl.pallas_call(functools.partial(project_kernel, model // HEADS), in_spec...  8.63 us
    pallas_call x1, Pallas kernels, own_attention(): pl.pallas_call(functools.partial(own_kernel, model // HEADS), in_specs=[I...  5.68 us
    ppermute x2, starting transfers between devices, exchange(): return lax.ppermute(value, 'mp', pairs + [(j, i) for i, j in pairs])  5.03 us
    pallas_call x1, Pallas kernels, shards(): pl.pallas_call(functools.partial(score_kernel, members, coeff), out_shape...  2.08 us
  transfers between devices with their start and end apart: 2, of which 0 were waited for; matrix products, arithmetic and copies ran while one was open for 0% of the time, Pallas kernels for 24%

profile of v3, /device:TPU:0, one launch (start us, length us, event | category | flops | bytes accessed | tf_op | source)
XLA Modules:
  0.0 60.3 jit_solution(6854183507425336133)
XLA Ops:
  0.0 1.6 %collective-permute-start = (bf16[1,512,1024]{2,1,0:T(8,128)(2,1)}, bf16[1,512,1024]{2,1,0:T(8,128)(2,1)}, u32[]{:S(2)}, u32[]{:S(2)}) collective-permute-start(bf16[1,512,1024]{2,1,0:T(8,128)(2,1)} %param.8), channel_id=1, source_target_pairs={{1,2},{2,1},{5,6},{6,5},{9,10},{10,9},{13,14},{14,13},{17,18},{18,... | collective-permute-start | bytes 3145736 | tf_op jit(solution)/shard_map/ppermute | solution.py:350
  1.6 8.6 %project.1 = (bf16[512,1024]{1,0:T(8,128)(2,1)}, bf16[512,2048]{1,0:T(8,128)(2,1)}) custom-call(bf16[512,1024]{1,0:T(8,128)(2,1)} %bitcast.9, bf16[1024,3072]{1,0:T(8,128)(2,1)} %w_hbm.3, f32[1,1024]{1,0:T(1,128)} %bitcast.11), custom_call_target="tpu_custom_call" | custom-call | flops 1099511627776 | bytes 1048576 | tf_op jit(solution)/shard_map/project/pallas_call | solution.py:356
  10.3 3.4 %collective-permute-start.1 = (bf16[512,2048]{1,0:T(8,128)(2,1)}, bf16[512,2048]{1,0:T(8,128)(2,1)}, u32[]{:S(2)}, u32[]{:S(2)}) collective-permute-start(bf16[512,2048]{1,0:T(8,128)(2,1)} %get-tuple-element.10.kv_hbm.own_kv_hbm), channel_id=1, source_target_pairs={{0,1},{2,3},{1,0},{3,2},{4,5},{6,7},{5,4},{7,6},{8,9},{10,11},{9,8... | collective-permute-start | bytes 6291464 | tf_op jit(solution)/shard_map/ppermute | solution.py:350
  13.7 5.7 %own_tokens.1 = (f32[512,512]{1,0:T(8,128)}, f32[512,512]{1,0:T(8,128)}, f32[512,512]{1,0:T(8,128)}) custom-call(bf16[512,1024]{1,0:T(8,128)(2,1)} %get-tuple-element.11.q_hbm, bf16[512,2048]{1,0:T(8,128)(2,1)} %get-tuple-element.10.kv_hbm.own_kv_hbm), custom_call_target="tpu_custom_call" | custom-call | flops 1099511627776 | bytes 1048576 | tf_op jit(solution)/shard_map/own_tokens/pallas_call | solution.py:380
  19.4 0.0 collective-permute-done
  19.4 0.0 collective-permute-done.1.chip_kv_hbm
  19.4 20.1 %neighbour_tokens.1 = bf16[8,100,256]{2,1,0:T(8,128)(2,1)} custom-call(bf16[512,1024]{1,0:T(8,128)(2,1)} %bitcast.far_hbm, bf16[1024,3072]{1,0:T(8,128)(2,1)} %w_hbm.3, bf16[512,2048]{1,0:T(8,128)(2,1)} %collective-permute-done.1.chip_kv_hbm, bf16[512,2048]{1,0:T(8,128)(2,1)} %get-tuple-element.10.kv_hbm.own_kv_hbm, ...), custom_call_target="tpu_custom_call" | custom-call | flops 1099511627776 | bytes 1048576 | tf_op jit(solution)/shard_map/neighbour_tokens/pallas_call | solution.py:402
  39.5 18.7 %all_to_all.4 = bf16[1,8,100,256]{3,2,0,1:T(8,128)(2,1)} all-to-all(bf16[1,8,100,256]{3,2,0,1:T(8,128)(2,1)} %bitcast.8), channel_id=1, replica_groups=mesh['ens'=8,'mp'=4] {'ens'}, dimensions={1} | all-to-all | bytes 819200 | tf_op jit(solution)/shard_map/all_to_all | solution.py:439
  58.3 2.1 %scores.1 = f32[100,256]{1,0:T(8,128)} custom-call(bf16[8,100,256]{2,1,0:T(8,128)(2,1)} %bitcast.7, f32[100,256]{1,0:T(8,128)} %truth_ref.1), custom_call_target="tpu_custom_call" | custom-call | tf_op jit(solution)/shard_map/scores/pallas_call | solution.py:443
Async XLA Ops:
  0.0 19.4 %collective-permute-start = (bf16[1,512,1024]{2,1,0:T(8,128)(2,1)}, bf16[1,512,1024]{2,1,0:T(8,128)(2,1)}, u32[]{:S(2)}, u32[]{:S(2)}) collective-permute-start(bf16[1,512,1024]{2,1,0:T(8,128)(2,1)} %param.8), channel_id=1, source_target_pairs={{1,2},{2,1},{5,6},{6,5},{9,10},{10,9},{13,14},{14,13},{17,18},{18,... | collective-permute-start | bytes 3145736 | tf_op jit(solution)/shard_map/ppermute | solution.py:350
  10.3 9.1 %collective-permute-start.1 = (bf16[512,2048]{1,0:T(8,128)(2,1)}, bf16[512,2048]{1,0:T(8,128)(2,1)}, u32[]{:S(2)}, u32[]{:S(2)}) collective-permute-start(bf16[512,2048]{1,0:T(8,128)(2,1)} %get-tuple-element.10.kv_hbm.own_kv_hbm), channel_id=1, source_target_pairs={{0,1},{2,3},{1,0},{3,2},{4,5},{6,7},{5,4},{7,6},{8,9},{10,11},{9,8... | collective-permute-start | bytes 6291464 | tf_op jit(solution)/shard_map/ppermute | solution.py:350

commit v4 on v3

--- a/solution.py
+++ b/solution.py
@@ -14,12 +14,13 @@
 EPS = 1e-05
 MASKED = -1e30
 STEP_COLS = 1024
-LN_ROWS = 128
+LN_ROWS = 256
 STEP_PAIRS = 4
 FULL_STEPS = 1
-OWN_ROWS = 256
+OWN_ROWS = 128
 AHEAD = 1
-LAG = 0
+OWN_LAG = 1
+FAR_LAG = 0
 FAR_ROWS = 128
 EDGE_ROWS = 256
 EDGE_COLS = 512
@@ -57,15 +58,21 @@
     return [jnp.concatenate([values * mask, jnp.broadcast_to(mask, values.shape)], axis=1) for mask in masks]
 
 
-def pair_weigh(scores, bias):
+def pair_weigh(scores, biases):
     count = scores.shape[1] // 2
     tops, weights = [], []
     for side in range(2):
-        kept = scores[:, side * count : (side + 1) * count]
-        if bias is not None:
-            kept = kept + bias
-        top = jnp.max(kept, axis=-1, keepdims=True)
-        weights.append(jnp.exp(kept - top).astype(BF16))
+        pieces, done = [], side * count
+        for first, bias in biases:
+            first += side * count
+            if first > done:
+                pieces.append(scores[:, done:first])
+            done = first + bias.shape[1]
+            pieces.append(scores[:, first:done] + bias)
+        if done < (side + 1) * count:
+            pieces.append(scores[:, done : (side + 1) * count])
+        top = functools.reduce(jnp.maximum, [jnp.max(piece, axis=-1, keepdims=True) for piece in pieces])
+        weights += [jnp.exp(piece - top).astype(BF16) for piece in pieces]
         tops.append(top)
     return jnp.concatenate(weights, axis=1), tops
 
@@ -77,22 +84,26 @@
     return both[:, :width], both[:, width:], jnp.where(lane < width // 2, tops[0], tops[1])
 
 
-def in_turn(items, score, weigh, finish):
+def in_turn(items, lag, score, weigh, finish):
     scored, weighed = [], []
-    for i in range(len(items) + AHEAD + LAG):
+    for i in range(len(items) + AHEAD + lag):
         if i < len(items):
             scored.append(score(items[i]))
         if AHEAD <= i < len(items) + AHEAD:
             weighed.append(weigh(items[i - AHEAD], scored[i - AHEAD]))
-        if i >= AHEAD + LAG:
-            finish(items[i - AHEAD - LAG], weighed[i - AHEAD - LAG])
-
-
-def project_kernel(head_dim, x_hbm, w_hbm, gain_ref, q_hbm, kv_hbm, x_ref, w_ref, made_ref, x_sem, w_sems, out_sems):
+        if i >= AHEAD + lag:
+            finish(items[i - AHEAD - lag], weighed[i - AHEAD - lag])
+
+
+def project_kernel(
+    head_dim, x_hbm, w_hbm, gain_hbm, q_hbm, kv_hbm, x_ref, gain_ref, w_ref, made_ref, x_sem, gain_sem, w_sems, out_sems
+):
     steps, rows, width = made_ref.shape
     model = x_ref.shape[1]
     q_steps = model // width
     x_copy = pltpu.make_async_copy(x_hbm, x_ref, x_sem)
+    gain_copy = pltpu.make_async_copy(gain_hbm, gain_ref, gain_sem)
+    gain_copy.start()
     x_copy.start()
     ins, outs = [], []
     for step in range(steps):
@@ -102,16 +113,19 @@
         outs.append(pltpu.make_async_copy(made_ref.at[step], target, out_sems.at[step]))
     for copy in ins:
         copy.start()
+    gain_copy.wait()
     x_copy.wait()
-    for first in range(0, rows, LN_ROWS):
-        here = slice(first, first + LN_ROWS)
-        x_ref[here] = layer_norm(x_ref[here], gain_ref[...])
     for step in range(steps):
         ins[step].wait()
-        made = dot(x_ref[...], w_ref[step]).astype(BF16)
-        if step < q_steps:
-            made = (made.astype(F32) * head_dim**-0.5).astype(BF16)
-        made_ref[step] = made
+        part = LN_ROWS if step == 0 else rows
+        for first in range(0, rows, part):
+            here = slice(first, first + part)
+            if step == 0:
+                x_ref[here] = layer_norm(x_ref[here], gain_ref[...])
+            made = dot(x_ref[here], w_ref[step]).astype(BF16)
+            if step < q_steps:
+                made = (made.astype(F32) * head_dim**-0.5).astype(BF16)
+            made_ref[step, here] = made
         outs[step].start()
     for copy in outs:
         copy.wait()
@@ -189,7 +203,8 @@
             for copy in outs[p]:
                 copy.start()
 
-    in_turn([(p, row) for p in range(pairs) for row in range(0, rows, OWN_ROWS)], score, lambda _, s: pair_weigh(s, None), finish)
+    items = [(p, row) for p in range(pairs) for row in range(0, rows, OWN_ROWS)]
+    in_turn(items, OWN_LAG, score, lambda _, s: pair_weigh(s, []), finish)
     for group in outs:
         for copy in group:
             copy.wait()
@@ -206,8 +221,9 @@
 
 def far_kernel(
     head_dim, far_hbm, w_hbm, chip_kv_hbm, own_kv_hbm, q_hbm, sum_hbm, total_hbm, top_hbm, wout_hbm, x_hbm,
+    gain_hbm, wdec_hbm, near_hbm, edge_hbm,
+    out_ref,
     gain_ref, wdec_ref, near_ref, edge_ref,
-    out_ref,
     far_ref, w_ref, kv_ref, q_ref, sum_ref, total_ref, top_ref, wout_ref, x_ref, high_ref, low_ref,
     bias_ref, context_ref, sems, step_sems,
 ):
@@ -225,6 +241,12 @@
     last_copies = [
         pltpu.make_async_copy(wout_hbm, wout_ref, sems.at[1]),
         pltpu.make_async_copy(x_hbm, x_ref, sems.at[2]),
+        pltpu.make_async_copy(wdec_hbm, wdec_ref, sems.at[3]),
+    ]
+    gain_copy = pltpu.make_async_copy(gain_hbm, gain_ref, sems.at[4])
+    edge_copies = [
+        pltpu.make_async_copy(near_hbm, near_ref, sems.at[5]),
+        pltpu.make_async_copy(edge_hbm, edge_ref, sems.at[6]),
     ]
     weight_copies, step_copies = [], []
     for step in range(steps):
@@ -244,8 +266,7 @@
         weight_copies.append(made[:2])
         step_copies.append(made[2:])
 
-    far_copy.start()
-    for copy in weight_copies[0] + step_copies[0]:
+    for copy in edge_copies + [gain_copy, far_copy] + weight_copies[0] + step_copies[0]:
         copy.start()
     span = rows + FAR_ROWS
     left_ok = (lane > 0).astype(jnp.int32)
@@ -253,9 +274,12 @@
     parts = rows // FAR_ROWS
     for part in range(parts):
         bias_ref[part] = window_bias(FAR_ROWS, rows, span, left_ok, right_ok, part * FAR_ROWS)
+    for copy in edge_copies:
+        copy.wait()
     for first in range(0, near_ref.shape[1], EDGE_COLS):
         cols = slice(first, first + EDGE_COLS)
         edge_matrix(near_ref[:, cols] - lane * rows, edge_ref[:, cols], high_ref.at[:, cols], low_ref.at[:, cols])
+    gain_copy.wait()
     far_copy.wait()
     for first in range(0, rows, LN_ROWS):
         here = slice(first, first + LN_ROWS)
@@ -295,8 +319,8 @@
             bias = bias_ref[part]
             if full:
                 reach = rows - part * FAR_ROWS
-                bias = jnp.concatenate([bias[:, :reach], jnp.zeros((FAR_ROWS, rows), F32), bias[:, reach:]], axis=1)
-            return pair_weigh(scores, bias)
+                return pair_weigh(scores, [(0, jnp.concatenate([bias[:, :reach], jnp.zeros((FAR_ROWS, rows), F32), bias[:, reach:]], axis=1))])
+            return pair_weigh(scores, [(0, bias)])
 
         def finish(item, weighed, sides=sides, window=window, full=full):
             first, part = item
@@ -313,7 +337,7 @@
             context_ref[here, first : first + pair] = (sums / totals).astype(BF16)
 
         firsts = range(step * width, (step + 1) * width, pair)
-        in_turn([(first, part) for first in firsts for part in range(parts)], score, weigh, finish)
+        in_turn([(first, part) for first in firsts for part in range(parts)], FAR_LAG, score, weigh, finish)
 
     for copy in last_copies:
         copy.wait()
@@ -355,13 +379,15 @@
     steps = 3 * model // STEP_COLS
     return pl.pallas_call(
         functools.partial(project_kernel, model // HEADS),
-        in_specs=[IN_HBM, IN_HBM, IN_VMEM],
+        in_specs=[IN_HBM] * 3,
         out_specs=[IN_HBM, IN_HBM],
         out_shape=[jax.ShapeDtypeStruct((rows, model), BF16), jax.ShapeDtypeStruct((rows, 2 * model), BF16)],
         scratch_shapes=[
             pltpu.VMEM((rows, model), BF16),
+            pltpu.VMEM((1, model), F32),
             pltpu.VMEM((steps, model, STEP_COLS), BF16),
             pltpu.VMEM((steps, rows, STEP_COLS), BF16),
+            pltpu.SemaphoreType.DMA,
             pltpu.SemaphoreType.DMA,
             pltpu.SemaphoreType.DMA((steps,)),
             pltpu.SemaphoreType.DMA((steps,)),
@@ -401,15 +427,17 @@
     held = lambda dtype, cols=model: pltpu.VMEM((rows, cols), dtype)
     return pl.pallas_call(
         functools.partial(far_kernel, model // HEADS),
-        in_specs=[IN_HBM] * 10 + [IN_VMEM] * 4,
+        in_specs=[IN_HBM] * 14,
         out_specs=IN_VMEM,
         out_shape=jax.ShapeDtypeStruct((dests, w_dec.shape[0], points // dests), BF16),
         scratch_shapes=[
+            pltpu.VMEM((1, model), F32), pltpu.VMEM(w_dec.shape, BF16),
+            pltpu.VMEM(near.shape, jnp.int32), pltpu.VMEM(near.shape, F32),
             held(BF16), pltpu.VMEM((model, 2 * model), BF16), pltpu.VMEM((3 * rows, 2 * model), BF16), held(BF16),
             held(F32, sums.shape[1]), held(F32, sums.shape[1]), held(F32, sums.shape[1]),
             pltpu.VMEM((model, model), BF16), held(BF16),
             held(BF16, points), held(BF16, points),
-            pltpu.VMEM((rows // FAR_ROWS, FAR_ROWS, span), F32), held(BF16), pltpu.SemaphoreType.DMA((3,)),
+            pltpu.VMEM((rows // FAR_ROWS, FAR_ROWS, span), F32), held(BF16), pltpu.SemaphoreType.DMA((7,)),
             pltpu.SemaphoreType.DMA((steps, 8)),
         ],
         compiler_params=pltpu.CompilerParams(vmem_limit_bytes=VMEM_LIMIT),

time: 60.6 us -> 59.5 us (0.982)
  Pallas kernels: 36.5 us -> 35.4 us
    pallas_call x1, Pallas kernels: 8.63 us -> 7.67 us  [project(): pl.pallas_call(functools.partial(project_kernel, model // HEADS), in_spec...]
  transfers between devices with their start and end apart: 2 -> 2, of which waited for: 0 -> 0; matrix products, arithmetic and copies ran while one was open for 0% -> 0% of each run, Pallas kernels for 24% -> 22%
where the time goes in v4:
time: 59.5 us; the launch traced here: 59.3 us
  Pallas kernels  35.4 us (59%)
  blocking collectives  18.8 us (32%)
  starting transfers between devices  5.03 us (8%)
    pallas_call x1, Pallas kernels, far_attention(): pl.pallas_call(functools.partial(far_kernel, model // HEADS), in_specs=[I...  20.2 us
    all_to_all x1, blocking collectives, shards(): lax.all_to_all(decoded, 'ens', split_axis=1, concat_axis=0, tiled=True)  18.8 us
    pallas_call x1, Pallas kernels, project(): pl.pallas_call(functools.partial(project_kernel, model // HEADS), in_spec...  7.67 us
    pallas_call x1, Pallas kernels, own_attention(): pl.pallas_call(functools.partial(own_kernel, model // HEADS), in_specs=[I...  5.46 us
    ppermute x2, starting transfers between devices, exchange(): return lax.ppermute(value, 'mp', pairs + [(j, i) for i, j in pairs])  5.03 us
    pallas_call x1, Pallas kernels, shards(): pl.pallas_call(functools.partial(score_kernel, members, coeff), out_shape...  2.08 us
  transfers between devices with their start and end apart: 2, of which 0 were waited for; matrix products, arithmetic and copies ran while one was open for 0% of the time, Pallas kernels for 22%

profile of v4, /device:TPU:0, one launch (start us, length us, event | category | flops | bytes accessed | tf_op | source)
XLA Modules:
  0.0 59.3 jit_solution(3061620046806997642)
XLA Ops:
  0.0 1.6 %collective-permute-start = (bf16[1,512,1024]{2,1,0:T(8,128)(2,1)}, bf16[1,512,1024]{2,1,0:T(8,128)(2,1)}, u32[]{:S(2)}, u32[]{:S(2)}) collective-permute-start(bf16[1,512,1024]{2,1,0:T(8,128)(2,1)} %param.8), channel_id=1, source_target_pairs={{1,2},{2,1},{5,6},{6,5},{9,10},{10,9},{13,14},{14,13},{17,18},{18,... | collective-permute-start | bytes 3145736 | tf_op jit(solution)/shard_map/ppermute | solution.py:374
  1.6 7.7 %project.1 = (bf16[512,1024]{1,0:T(8,128)(2,1)}, bf16[512,2048]{1,0:T(8,128)(2,1)}) custom-call(bf16[512,1024]{1,0:T(8,128)(2,1)} %bitcast.9, bf16[1024,3072]{1,0:T(8,128)(2,1)} %w_hbm.3, f32[1,1024]{1,0:T(1,128)} %bitcast.11), custom_call_target="tpu_custom_call" | custom-call | flops 1099511627776 | bytes 1048576 | tf_op jit(solution)/shard_map/project/pallas_call | solution.py:380
  9.3 3.4 %collective-permute-start.1 = (bf16[512,2048]{1,0:T(8,128)(2,1)}, bf16[512,2048]{1,0:T(8,128)(2,1)}, u32[]{:S(2)}, u32[]{:S(2)}) collective-permute-start(bf16[512,2048]{1,0:T(8,128)(2,1)} %get-tuple-element.10.kv_hbm.own_kv_hbm), channel_id=1, source_target_pairs={{0,1},{2,3},{1,0},{3,2},{4,5},{6,7},{5,4},{7,6},{8,9},{10,11},{9,8... | collective-permute-start | bytes 6291464 | tf_op jit(solution)/shard_map/ppermute | solution.py:374
  12.7 5.5 %own_tokens.1 = (f32[512,512]{1,0:T(8,128)}, f32[512,512]{1,0:T(8,128)}, f32[512,512]{1,0:T(8,128)}) custom-call(bf16[512,1024]{1,0:T(8,128)(2,1)} %get-tuple-element.11.q_hbm, bf16[512,2048]{1,0:T(8,128)(2,1)} %get-tuple-element.10.kv_hbm.own_kv_hbm), custom_call_target="tpu_custom_call" | custom-call | flops 1099511627776 | bytes 1048576 | tf_op jit(solution)/shard_map/own_tokens/pallas_call | solution.py:406
  18.2 0.0 collective-permute-done
  18.2 0.0 collective-permute-done.1.chip_kv_hbm
  18.2 20.2 %neighbour_tokens.1 = bf16[8,100,256]{2,1,0:T(8,128)(2,1)} custom-call(bf16[512,1024]{1,0:T(8,128)(2,1)} %bitcast.far_hbm, bf16[1024,3072]{1,0:T(8,128)(2,1)} %w_hbm.3, bf16[512,2048]{1,0:T(8,128)(2,1)} %collective-permute-done.1.chip_kv_hbm, bf16[512,2048]{1,0:T(8,128)(2,1)} %get-tuple-element.10.kv_hbm.own_kv_hbm, ...), custom_call_target="tpu_custom_call" | custom-call | flops 1099511627776 | bytes 1048576 | tf_op jit(solution)/shard_map/neighbour_tokens/pallas_call | solution.py:428
  38.4 18.8 %all_to_all.4 = bf16[1,8,100,256]{3,2,0,1:T(8,128)(2,1)} all-to-all(bf16[1,8,100,256]{3,2,0,1:T(8,128)(2,1)} %bitcast.8), channel_id=1, replica_groups=mesh['ens'=8,'mp'=4] {'ens'}, dimensions={1} | all-to-all | bytes 819200 | tf_op jit(solution)/shard_map/all_to_all | solution.py:467
  57.2 2.1 %scores.1 = f32[100,256]{1,0:T(8,128)} custom-call(bf16[8,100,256]{2,1,0:T(8,128)(2,1)} %bitcast.7, f32[100,256]{1,0:T(8,128)} %truth_ref.1), custom_call_target="tpu_custom_call" | custom-call | tf_op jit(solution)/shard_map/scores/pallas_call | solution.py:471
Async XLA Ops:
  0.0 18.2 %collective-permute-start = (bf16[1,512,1024]{2,1,0:T(8,128)(2,1)}, bf16[1,512,1024]{2,1,0:T(8,128)(2,1)}, u32[]{:S(2)}, u32[]{:S(2)}) collective-permute-start(bf16[1,512,1024]{2,1,0:T(8,128)(2,1)} %param.8), channel_id=1, source_target_pairs={{1,2},{2,1},{5,6},{6,5},{9,10},{10,9},{13,14},{14,13},{17,18},{18,... | collective-permute-start | bytes 3145736 | tf_op jit(solution)/shard_map/ppermute | solution.py:374
  9.3 8.9 %collective-permute-start.1 = (bf16[512,2048]{1,0:T(8,128)(2,1)}, bf16[512,2048]{1,0:T(8,128)(2,1)}, u32[]{:S(2)}, u32[]{:S(2)}) collective-permute-start(bf16[512,2048]{1,0:T(8,128)(2,1)} %get-tuple-element.10.kv_hbm.own_kv_hbm), channel_id=1, source_target_pairs={{0,1},{2,3},{1,0},{3,2},{4,5},{6,7},{5,4},{7,6},{8,9},{10,11},{9,8... | collective-permute-start | bytes 6291464 | tf_op jit(solution)/shard_map/ppermute | solution.py:374

commit v5 on v4

--- a/solution.py
+++ b/solution.py
@@ -15,20 +15,25 @@
 MASKED = -1e30
 STEP_COLS = 1024
 LN_ROWS = 256
+NORM_ROWS = 32
 STEP_PAIRS = 4
+LOOP_PAIRS = 2
 FULL_STEPS = 1
 OWN_ROWS = 128
 AHEAD = 1
 OWN_LAG = 1
-FAR_LAG = 0
+FAR_LAG = 1
 FAR_ROWS = 128
 EDGE_ROWS = 256
 EDGE_COLS = 512
+EDGE_PART = 32
+SCORE_ROWS = 16
 
 BF16 = jnp.bfloat16
 F32 = jnp.float32
 MIB = 1024 * 1024
 VMEM_LIMIT = 63 * MIB
+SHARED_LIMIT = VMEM_LIMIT - 9 * MIB - MIB // 2
 LONG = pl.CostEstimate(flops=MIB * MIB, bytes_accessed=MIB, transcendentals=0)
 
 
@@ -46,6 +51,12 @@
     centred = values - average
     variance = jnp.mean(centred * centred, axis=-1, keepdims=True)
     return (centred * lax.rsqrt(variance + EPS) * ln_gain).astype(BF16)
+
+
+def normalise(ref, here, ln_gain):
+    for first in range(here.start, here.stop, NORM_ROWS):
+        part = slice(first, first + NORM_ROWS)
+        ref[part] = layer_norm(ref[part], ln_gain)
 
 
 def halves(width):
@@ -121,7 +132,7 @@
         for first in range(0, rows, part):
             here = slice(first, first + part)
             if step == 0:
-                x_ref[here] = layer_norm(x_ref[here], gain_ref[...])
+                normalise(x_ref, here, gain_ref[...])
             made = dot(x_ref[here], w_ref[step]).astype(BF16)
             if step < q_steps:
                 made = (made.astype(F32) * head_dim**-0.5).astype(BF16)
@@ -142,19 +153,22 @@
         totals.append(total)
     highs = [t.astype(BF16) for t in totals]
     lows = [(t - h.astype(F32)).astype(BF16) for t, h in zip(totals, highs)]
-    shape = (EDGE_ROWS, points)
-    token = lax.broadcasted_iota(jnp.int32, shape, 0).astype(F32).astype(BF16)
+    shape = (EDGE_PART, points)
     for first in range(0, rows, EDGE_ROWS):
-        high = jnp.zeros(shape, BF16)
-        low = jnp.zeros(shape, BF16)
+        near_rows = []
         for k in range(NEIGH):
             row = near[k : k + 1] - first
-            row = jnp.where((row >= 0) & (row < EDGE_ROWS), row, -1).astype(F32).astype(BF16)
-            hit = token == row
-            high = jnp.where(hit, highs[k], high)
-            low = jnp.where(hit, lows[k], low)
-        high_ref[first : first + EDGE_ROWS] = high
-        low_ref[first : first + EDGE_ROWS] = low
+            near_rows.append(jnp.where((row >= 0) & (row < EDGE_ROWS), row, -1).astype(F32).astype(BF16))
+        for part in range(0, EDGE_ROWS, EDGE_PART):
+            token = (part + lax.broadcasted_iota(jnp.int32, shape, 0)).astype(F32).astype(BF16)
+            high = jnp.zeros(shape, BF16)
+            low = jnp.zeros(shape, BF16)
+            for k in range(NEIGH):
+                hit = token == near_rows[k]
+                high = jnp.where(hit, highs[k], high)
+                low = jnp.where(hit, lows[k], low)
+            high_ref[first + part : first + part + EDGE_PART] = high
+            low_ref[first + part : first + part + EDGE_PART] = low
 
 
 def own_kernel(head_dim, q_hbm, kv_hbm, *refs):
@@ -220,12 +234,11 @@
 
 
 def far_kernel(
-    head_dim, far_hbm, w_hbm, chip_kv_hbm, own_kv_hbm, q_hbm, sum_hbm, total_hbm, top_hbm, wout_hbm, x_hbm,
-    gain_hbm, wdec_hbm, near_hbm, edge_hbm,
+    head_dim, far_hbm, chip_kv_hbm, own_kv_hbm, q_hbm, sum_hbm, total_hbm, top_hbm,
+    w_ref, wout_ref, x_ref, gain_ref, wdec_ref, near_ref, edge_ref,
     out_ref,
-    gain_ref, wdec_ref, near_ref, edge_ref,
-    far_ref, w_ref, kv_ref, q_ref, sum_ref, total_ref, top_ref, wout_ref, x_ref, high_ref, low_ref,
-    bias_ref, context_ref, sems, step_sems,
+    far_ref, kv_ref, q_ref, sum_ref, total_ref, top_ref, high_ref, low_ref,
+    bias_ref, context_ref, far_sem, step_sems,
 ):
     rows, model = q_ref.shape
     lane = lax.axis_index("mp")
@@ -237,22 +250,11 @@
     pair = 2 * head_dim
     width = pair * STEP_PAIRS
     steps = model // width
-    far_copy = pltpu.make_async_copy(far_hbm, far_ref, sems.at[0])
-    last_copies = [
-        pltpu.make_async_copy(wout_hbm, wout_ref, sems.at[1]),
-        pltpu.make_async_copy(x_hbm, x_ref, sems.at[2]),
-        pltpu.make_async_copy(wdec_hbm, wdec_ref, sems.at[3]),
-    ]
-    gain_copy = pltpu.make_async_copy(gain_hbm, gain_ref, sems.at[4])
-    edge_copies = [
-        pltpu.make_async_copy(near_hbm, near_ref, sems.at[5]),
-        pltpu.make_async_copy(edge_hbm, edge_ref, sems.at[6]),
-    ]
-    weight_copies, step_copies = [], []
+    far_copy = pltpu.make_async_copy(far_hbm, far_ref, far_sem)
+    step_copies = []
     for step in range(steps):
         cols = pl.ds(step * width, width)
         sides = [cols, pl.ds(model + step * width, width)]
-        weights = [(w_hbm.at[:, pl.ds(model + s.start, width)], w_ref.at[:, s]) for s in sides]
         moves = [(chip_kv_hbm.at[:, s], kv_ref.at[chip_at, s]) for s in sides] + [(q_hbm.at[:, cols], q_ref.at[:, cols])]
         if step < FULL_STEPS:
             moves += [(own_kv_hbm.at[:, s], kv_ref.at[own_at, s]) for s in sides]
@@ -262,11 +264,9 @@
                 (a.at[:, kept], b.at[:, kept])
                 for a, b in ((sum_hbm, sum_ref), (total_hbm, total_ref), (top_hbm, top_ref))
             ]
-        made = [pltpu.make_async_copy(a, b, step_sems.at[step, i]) for i, (a, b) in enumerate(weights + moves)]
-        weight_copies.append(made[:2])
-        step_copies.append(made[2:])
-
-    for copy in edge_copies + [gain_copy, far_copy] + weight_copies[0] + step_copies[0]:
+        step_copies.append([pltpu.make_async_copy(a, b, step_sems.at[step, i]) for i, (a, b) in enumerate(moves)])
+
+    for copy in [far_copy] + step_copies[0]:
         copy.start()
     span = rows + FAR_ROWS
     left_ok = (lane > 0).astype(jnp.int32)
@@ -274,73 +274,72 @@
     parts = rows // FAR_ROWS
     for part in range(parts):
         bias_ref[part] = window_bias(FAR_ROWS, rows, span, left_ok, right_ok, part * FAR_ROWS)
-    for copy in edge_copies:
-        copy.wait()
     for first in range(0, near_ref.shape[1], EDGE_COLS):
         cols = slice(first, first + EDGE_COLS)
         edge_matrix(near_ref[:, cols] - lane * rows, edge_ref[:, cols], high_ref.at[:, cols], low_ref.at[:, cols])
-    gain_copy.wait()
     far_copy.wait()
     for first in range(0, rows, LN_ROWS):
         here = slice(first, first + LN_ROWS)
-        far_ref[here] = layer_norm(far_ref[here], gain_ref[...])
+        normalise(far_ref, here, gain_ref[...])
 
     masks = halves(pair)
     for step in range(steps):
-        later = weight_copies[step + 1] + step_copies[step + 1] if step + 1 < steps else last_copies
-        for side, copy in enumerate(weight_copies[step]):
+        later = step_copies[step + 1] if step + 1 < steps else []
+        for side in range(2):
             cols = slice(side * model + step * width, side * model + (step + 1) * width)
-            copy.wait()
-            kv_ref[far_at, cols] = dot(far_ref[...], w_ref[:, cols]).astype(BF16)
+            kv_ref[far_at, cols] = dot(far_ref[...], w_ref[:, model + cols.start : model + cols.stop]).astype(BF16)
         for copy in step_copies[step]:
             copy.wait()
         for copy in later:
             copy.start()
         full = step < FULL_STEPS
-        sides = {}
-
-        def window(part, full=full):
-            left, right = slice(part * FAR_ROWS, rows), slice(2 * rows, 2 * rows + (part + 1) * FAR_ROWS)
-            return [slice(left.start, right.stop)] if full else [left, right]
-
-        def score(item, sides=sides, window=window):
-            first, part = item
-            cols = slice(first, first + pair)
-            if part == 0:
-                sides[first] = (
-                    [kv_ref[:, cols] * mask for mask in masks],
-                    value_sides(kv_ref[:, model + first : model + first + pair], masks),
-                )
-            keys = [k[w] for k in sides[first][0] for w in window(part)]
-            return dot_nt(q_ref[part * FAR_ROWS : (part + 1) * FAR_ROWS, cols], jnp.concatenate(keys, axis=0))
-
-        def weigh(item, scores, full=full):
-            part = item[1]
-            bias = bias_ref[part]
-            if full:
-                reach = rows - part * FAR_ROWS
-                return pair_weigh(scores, [(0, jnp.concatenate([bias[:, :reach], jnp.zeros((FAR_ROWS, rows), F32), bias[:, reach:]], axis=1))])
-            return pair_weigh(scores, [(0, bias)])
-
-        def finish(item, weighed, sides=sides, window=window, full=full):
-            first, part = item
-            here = slice(part * FAR_ROWS, (part + 1) * FAR_ROWS)
-            values = [v[w] for v in sides[first][1] for w in window(part)]
-            sums, totals, top = pair_sums(*weighed, jnp.concatenate(values, axis=0))
-            if not full:
-                kept = slice(first - FULL_STEPS * width, first - FULL_STEPS * width + pair)
-                own_top = top_ref[here, kept]
-                best = jnp.maximum(top, own_top)
-                scale, own_scale = jnp.exp(top - best), jnp.exp(own_top - best)
-                sums = sums * scale + sum_ref[here, kept] * own_scale
-                totals = totals * scale + total_ref[here, kept] * own_scale
-            context_ref[here, first : first + pair] = (sums / totals).astype(BF16)
-
-        firsts = range(step * width, (step + 1) * width, pair)
-        in_turn([(first, part) for first in firsts for part in range(parts)], FAR_LAG, score, weigh, finish)
-
-    for copy in last_copies:
-        copy.wait()
+
+        @pl.loop(0, STEP_PAIRS // LOOP_PAIRS)
+        def _(turn, step=step, full=full):
+            sides = {}
+
+            def window(part):
+                left, right = slice(part * FAR_ROWS, rows), slice(2 * rows, 2 * rows + (part + 1) * FAR_ROWS)
+                return [slice(left.start, right.stop)] if full else [left, right]
+
+            def columns(p, offset=0):
+                first = offset + step * width + (turn * LOOP_PAIRS + p) * pair
+                return pl.ds(pl.multiple_of(first, pair), pair)
+
+            def score(item):
+                p, part = item
+                if part == 0:
+                    sides[p] = (
+                        [kv_ref[:, columns(p)] * mask for mask in masks],
+                        value_sides(kv_ref[:, columns(p, model)], masks),
+                    )
+                keys = [k[w] for k in sides[p][0] for w in window(part)]
+                queries = q_ref[part * FAR_ROWS : (part + 1) * FAR_ROWS, columns(p)]
+                return dot_nt(queries, jnp.concatenate(keys, axis=0))
+
+            def weigh(item, scores):
+                bias = bias_ref[item[1]]
+                if full:
+                    reach = rows - item[1] * FAR_ROWS
+                    bias = jnp.concatenate([bias[:, :reach], jnp.zeros((FAR_ROWS, rows), F32), bias[:, reach:]], axis=1)
+                return pair_weigh(scores, [(0, bias)])
+
+            def finish(item, weighed):
+                p, part = item
+                here = slice(part * FAR_ROWS, (part + 1) * FAR_ROWS)
+                values = [v[w] for v in sides[p][1] for w in window(part)]
+                sums, totals, top = pair_sums(*weighed, jnp.concatenate(values, axis=0))
+                if not full:
+                    kept = columns(p, -FULL_STEPS * width)
+                    own_top = top_ref[here, kept]
+                    best = jnp.maximum(top, own_top)
+                    scale, own_scale = jnp.exp(top - best), jnp.exp(own_top - best)
+                    sums = sums * scale + sum_ref[here, kept] * own_scale
+                    totals = totals * scale + total_ref[here, kept] * own_scale
+                context_ref[here, columns(p)] = (sums / totals).astype(BF16)
+
+            in_turn([(p, part) for p in range(LOOP_PAIRS) for part in range(parts)], FAR_LAG, score, weigh, finish)
+
     processed = (x_ref[...].astype(F32) + dot(context_ref[...], wout_ref[...])).astype(BF16)
     fields = dot_nt(wdec_ref[...], processed)
     variables, each = out_ref.shape[1:]
@@ -357,16 +356,23 @@
 
 
 def score_kernel(members, coeff, fields_ref, truth_ref, out_ref):
-    fields = [fields_ref[m].astype(F32) for m in range(members)]
-    truth = truth_ref[...]
-    skill = sum(jnp.abs(f - truth) for f in fields) / members
-    spread = sum(jnp.abs(fields[j] - fields[k]) for j in range(members) for k in range(j))
-    out_ref[...] = skill - (2.0 * coeff) * spread
+    rows = out_ref.shape[0]
+    for first in range(0, rows, SCORE_ROWS):
+        here = slice(first, min(first + SCORE_ROWS, rows))
+        fields = [fields_ref[m, here].astype(F32) for m in range(members)]
+        truth = truth_ref[here]
+        skill = sum(jnp.abs(f - truth) for f in fields) / members
+        spread = sum(jnp.abs(fields[j] - fields[k]) for j in range(members) for k in range(j))
+        out_ref[here] = skill - (2.0 * coeff) * spread
 
 
 IN_VMEM = pl.BlockSpec(memory_space=pltpu.VMEM)
 ANYWHERE = pl.BlockSpec(memory_space=pl.ANY)
 IN_HBM = pl.BlockSpec(memory_space=pltpu.HBM)
+
+
+def near_by(value):
+    return pltpu.with_memory_space_constraint(value, pltpu.VMEM)
 
 
 def exchange(value, first, lanes):
@@ -411,7 +417,7 @@
         scratch_shapes=[held(BF16)] * 3
         + [held(F32)] * 3
         + [pltpu.SemaphoreType.DMA((pairs, 3)), pltpu.SemaphoreType.DMA((pairs, 3))],
-        compiler_params=pltpu.CompilerParams(vmem_limit_bytes=VMEM_LIMIT),
+        compiler_params=pltpu.CompilerParams(vmem_limit_bytes=SHARED_LIMIT),
         cost_estimate=LONG,
         name="own_tokens",
     )(queries, kv)
@@ -427,23 +433,23 @@
     held = lambda dtype, cols=model: pltpu.VMEM((rows, cols), dtype)
     return pl.pallas_call(
         functools.partial(far_kernel, model // HEADS),
-        in_specs=[IN_HBM] * 14,
+        in_specs=[IN_HBM] * 7 + [IN_VMEM] * 7,
         out_specs=IN_VMEM,
         out_shape=jax.ShapeDtypeStruct((dests, w_dec.shape[0], points // dests), BF16),
         scratch_shapes=[
-            pltpu.VMEM((1, model), F32), pltpu.VMEM(w_dec.shape, BF16),
-            pltpu.VMEM(near.shape, jnp.int32), pltpu.VMEM(near.shape, F32),
-            held(BF16), pltpu.VMEM((model, 2 * model), BF16), pltpu.VMEM((3 * rows, 2 * model), BF16), held(BF16),
+            held(BF16), pltpu.VMEM((3 * rows, 2 * model), BF16), held(BF16),
             held(F32, sums.shape[1]), held(F32, sums.shape[1]), held(F32, sums.shape[1]),
-            pltpu.VMEM((model, model), BF16), held(BF16),
             held(BF16, points), held(BF16, points),
-            pltpu.VMEM((rows // FAR_ROWS, FAR_ROWS, span), F32), held(BF16), pltpu.SemaphoreType.DMA((7,)),
-            pltpu.SemaphoreType.DMA((steps, 8)),
+            pltpu.VMEM((rows // FAR_ROWS, FAR_ROWS, span), F32), held(BF16), pltpu.SemaphoreType.DMA,
+            pltpu.SemaphoreType.DMA((steps, 6)),
         ],
-        compiler_params=pltpu.CompilerParams(vmem_limit_bytes=VMEM_LIMIT),
+        compiler_params=pltpu.CompilerParams(vmem_limit_bytes=SHARED_LIMIT),
         cost_estimate=LONG,
         name="neighbour_tokens",
-    )(far, w_qkv, chip_kv, own_kv, queries, sums, totals, tops, w_out, tokens, gain, w_dec, near, edge_weights)
+    )(
+        far, chip_kv, own_kv, queries, sums, totals, tops,
+        *[near_by(a) for a in (w_qkv, w_out, tokens, gain, w_dec, near, edge_weights)],
+    )
 
 
 def one_member(tokens, far, ln_gain, w_qkv, w_out, near, edge_weights, w_dec):

time: 59.5 us -> 58.8 us (0.988)
  Pallas kernels: 35.4 us -> 34.6 us
    pallas_call x1, Pallas kernels: 20.2 us -> 19.2 us  [far_attention(): pl.pallas_call(functools.partial(far_kernel, model // HEADS), in_specs=[I...]
  transfers between devices with their start and end apart: 2 -> 2, of which waited for: 0 -> 0; matrix products, arithmetic and copies ran while one was open for 0% -> 0% of each run, Pallas kernels for 22% -> 23%
where the time goes in v5:
time: 58.8 us; the launch traced here: 58.6 us
  Pallas kernels  34.6 us (59%)
  blocking collectives  18.8 us (32%)
  starting transfers between devices  5.03 us (9%)
    pallas_call x1, Pallas kernels, far_attention(): pl.pallas_call(functools.partial(far_kernel, model // HEADS), in_specs=[I...  19.2 us
    all_to_all x1, blocking collectives, shards(): lax.all_to_all(decoded, 'ens', split_axis=1, concat_axis=0, tiled=True)  18.8 us
    pallas_call x1, Pallas kernels, project(): pl.pallas_call(functools.partial(project_kernel, model // HEADS), in_spec...  7.67 us
    pallas_call x1, Pallas kernels, own_attention(): pl.pallas_call(functools.partial(own_kernel, model // HEADS), in_specs=[I...  5.59 us
    ppermute x2, starting transfers between devices, exchange(): return lax.ppermute(value, 'mp', pairs + [(j, i) for i, j in pairs])  5.03 us
    pallas_call x1, Pallas kernels, shards(): pl.pallas_call(functools.partial(score_kernel, members, coeff), out_shape...  2.08 us
  transfers between devices with their start and end apart: 2, of which 0 were waited for; matrix products, arithmetic and copies ran while one was open for 0% of the time, Pallas kernels for 23%

profile of v5, /device:TPU:0, one launch (start us, length us, event | category | flops | bytes accessed | tf_op | source)
XLA Modules:
  0.0 58.6 jit_solution(6254270169800258313)
XLA Ops:
  0.0 1.6 %collective-permute-start = (bf16[1,512,1024]{2,1,0:T(8,128)(2,1)}, bf16[1,512,1024]{2,1,0:T(8,128)(2,1)}, u32[]{:S(2)}, u32[]{:S(2)}) collective-permute-start(bf16[1,512,1024]{2,1,0:T(8,128)(2,1)} %param.8), channel_id=1, source_target_pairs={{1,2},{2,1},{5,6},{6,5},{9,10},{10,9},{13,14},{14,13},{17,18},{18,... | collective-permute-start | bytes 3145736 | tf_op jit(solution)/shard_map/ppermute | solution.py:380
  1.6 7.7 %project.1 = (bf16[512,1024]{1,0:T(8,128)(2,1)}, bf16[512,2048]{1,0:T(8,128)(2,1)}) custom-call(bf16[512,1024]{1,0:T(8,128)(2,1)} %bitcast.7, bf16[1024,3072]{1,0:T(8,128)(2,1)} %w_ref.1, f32[1,1024]{1,0:T(1,128)} %bitcast.9), custom_call_target="tpu_custom_call" | custom-call | flops 1099511627776 | bytes 1048576 | tf_op jit(solution)/shard_map/project/pallas_call | solution.py:386
  9.3 3.4 %collective-permute-start.1 = (bf16[512,2048]{1,0:T(8,128)(2,1)}, bf16[512,2048]{1,0:T(8,128)(2,1)}, u32[]{:S(2)}, u32[]{:S(2)}) collective-permute-start(bf16[512,2048]{1,0:T(8,128)(2,1)} %get-tuple-element.10.kv_hbm.own_kv_hbm), channel_id=1, source_target_pairs={{0,1},{2,3},{1,0},{3,2},{4,5},{6,7},{5,4},{7,6},{8,9},{10,11},{9,8... | collective-permute-start | bytes 6291464 | tf_op jit(solution)/shard_map/ppermute | solution.py:380
  12.7 0.0 copy-start
  12.7 0.0 copy-start.1
  12.7 0.0 copy-start.2
  12.7 0.0 copy-start.3
  12.7 0.0 copy-start.4
  12.7 0.0 copy-start.5
  12.7 0.0 copy-start.6
  12.8 5.6 %own_tokens.1 = (f32[512,512]{1,0:T(8,128)}, f32[512,512]{1,0:T(8,128)}, f32[512,512]{1,0:T(8,128)}) custom-call(bf16[512,1024]{1,0:T(8,128)(2,1)} %get-tuple-element.11.q_hbm, bf16[512,2048]{1,0:T(8,128)(2,1)} %get-tuple-element.10.kv_hbm.own_kv_hbm), custom_call_target="tpu_custom_call" | custom-call | flops 1099511627776 | bytes 1048576 | tf_op jit(solution)/shard_map/own_tokens/pallas_call | solution.py:412
  18.4 0.0 collective-permute-done
  18.4 0.0 collective-permute-done.1.chip_kv_hbm
  18.4 0.0 copy-done
  18.4 0.0 copy-done.1
  18.4 0.0 copy-done.2
  18.4 0.0 copy-done.3
  18.4 0.0 copy-done.4
  18.4 0.0 copy-done.5
  18.4 0.0 copy-done.6
  18.4 19.2 %neighbour_tokens.1 = bf16[8,100,256]{2,1,0:T(8,128)(2,1)} custom-call(bf16[512,1024]{1,0:T(8,128)(2,1)} %bitcast.far_hbm, bf16[512,2048]{1,0:T(8,128)(2,1)} %collective-permute-done.1.chip_kv_hbm, bf16[512,2048]{1,0:T(8,128)(2,1)} %get-tuple-element.10.kv_hbm.own_kv_hbm, bf16[512,1024]{1,0:T(8,128)(2,1)} %get-tuple-element.11.q_hbm, ...), custom_call_target="tpu_custom_call" | custom-call | flops 1099511627776 | bytes 1048576 | tf_op jit(solution)/shard_map/neighbour_tokens/pallas_call | solution.py:434
  37.7 18.8 %all_to_all.4 = bf16[1,8,100,256]{3,2,0,1:T(8,128)(2,1)} all-to-all(bf16[1,8,100,256]{3,2,0,1:T(8,128)(2,1)} %bitcast.12), channel_id=1, replica_groups=mesh['ens'=8,'mp'=4] {'ens'}, dimensions={1} | all-to-all | bytes 819200 | tf_op jit(solution)/shard_map/all_to_all | solution.py:473
  56.5 2.1 %scores.1 = f32[100,256]{1,0:T(8,128)} custom-call(bf16[8,100,256]{2,1,0:T(8,128)(2,1)} %bitcast.11, f32[100,256]{1,0:T(8,128)} %truth_ref.1), custom_call_target="tpu_custom_call" | custom-call | tf_op jit(solution)/shard_map/scores/pallas_call | solution.py:477
Async XLA Ops:
  0.0 18.4 %collective-permute-start = (bf16[1,512,1024]{2,1,0:T(8,128)(2,1)}, bf16[1,512,1024]{2,1,0:T(8,128)(2,1)}, u32[]{:S(2)}, u32[]{:S(2)}) collective-permute-start(bf16[1,512,1024]{2,1,0:T(8,128)(2,1)} %param.8), channel_id=1, source_target_pairs={{1,2},{2,1},{5,6},{6,5},{9,10},{10,9},{13,14},{14,13},{17,18},{18,... | collective-permute-start | bytes 3145736 | tf_op jit(solution)/shard_map/ppermute | solution.py:380
  9.3 9.1 %collective-permute-start.1 = (bf16[512,2048]{1,0:T(8,128)(2,1)}, bf16[512,2048]{1,0:T(8,128)(2,1)}, u32[]{:S(2)}, u32[]{:S(2)}) collective-permute-start(bf16[512,2048]{1,0:T(8,128)(2,1)} %get-tuple-element.10.kv_hbm.own_kv_hbm), channel_id=1, source_target_pairs={{0,1},{2,3},{1,0},{3,2},{4,5},{6,7},{5,4},{7,6},{8,9},{10,11},{9,8... | collective-permute-start | bytes 6291464 | tf_op jit(solution)/shard_map/ppermute | solution.py:380
  12.7 5.7 %copy-start = (bf16[1024,3072]{1,0:T(8,128)(2,1)S(1)}, bf16[1024,3072]{1,0:T(8,128)(2,1)}, u32[]{:S(2)}) copy-start(bf16[1024,3072]{1,0:T(8,128)(2,1)} %w_ref.1) | copy-start | bytes 18874372
  12.7 5.7 %copy-start.1 = (bf16[1024,1024]{1,0:T(8,128)(2,1)S(1)}, bf16[1024,1024]{1,0:T(8,128)(2,1)}, u32[]{:S(2)}) copy-start(bf16[1024,1024]{1,0:T(8,128)(2,1)} %wout_ref.1) | copy-start | bytes 6291460
  12.7 5.7 %copy-start.2 = (bf16[1,512,1024]{2,1,0:T(8,128)(2,1)S(1)}, bf16[1,512,1024]{2,1,0:T(8,128)(2,1)}, u32[]{:S(2)}) copy-start(bf16[1,512,1024]{2,1,0:T(8,128)(2,1)} %param.8) | copy-start | bytes 3145732
  12.7 5.7 %copy-start.3 = (bf16[100,1024]{1,0:T(8,128)(2,1)S(1)}, bf16[100,1024]{1,0:T(8,128)(2,1)}, u32[]{:S(2)}) copy-start(bf16[100,1024]{1,0:T(8,128)(2,1)} %wdec_ref.1) | copy-start | bytes 614404
  12.7 5.7 %copy-start.4 = (s32[4,2048]{1,0:T(4,128)S(1)}, s32[4,2048]{1,0:T(4,128)}, u32[]{:S(2)}) copy-start(s32[4,2048]{1,0:T(4,128)} %near_ref.1) | copy-start | bytes 98308
  12.7 5.7 %copy-start.5 = (f32[4,2048]{1,0:T(4,128)S(1)}, f32[4,2048]{1,0:T(4,128)}, u32[]{:S(2)}) copy-start(f32[4,2048]{1,0:T(4,128)} %edge_ref.1) | copy-start | bytes 98308
  12.7 5.7 %copy-start.6 = (f32[1024]{0:T(1024)S(1)}, f32[1024]{0:T(1024)}, u32[]{:S(2)}) copy-start(f32[1024]{0:T(1024)} %param.9) | copy-start | bytes 12292

commit v6 on v5

--- a/solution.py
+++ b/solution.py
@@ -14,15 +14,19 @@
 EPS = 1e-05
 MASKED = -1e30
 STEP_COLS = 1024
+FAR_COLS = 1024
+DECODE_COLS = 1024
 LN_ROWS = 256
 NORM_ROWS = 32
 STEP_PAIRS = 4
-LOOP_PAIRS = 2
+LOOP_PAIRS = 4
 FULL_STEPS = 1
 OWN_ROWS = 128
 AHEAD = 1
 OWN_LAG = 1
-FAR_LAG = 1
+FAR_AHEAD = 2
+ONES_ROWS = 16
+FAR_LAG = 3
 FAR_ROWS = 128
 EDGE_ROWS = 256
 EDGE_COLS = 512
@@ -95,15 +99,37 @@
     return both[:, :width], both[:, width:], jnp.where(lane < width // 2, tops[0], tops[1])
 
 
-def in_turn(items, lag, score, weigh, finish):
+def tall_weigh(scores, biases):
+    pieces, done = [], 0
+    for first, bias in biases:
+        if first > done:
+            pieces.append(scores[done:first])
+        done = first + bias.shape[0]
+        pieces.append(scores[first:done] + bias)
+    if done < scores.shape[0]:
+        pieces.append(scores[done:])
+    top = functools.reduce(jnp.maximum, [jnp.max(piece, axis=0, keepdims=True) for piece in pieces])
+    return jnp.concatenate([jnp.exp(piece - top).astype(BF16) for piece in pieces], axis=0), top
+
+
+def tall_sums(weights, top, values):
+    width, count = values.shape[0], weights.shape[1] // 2
+    ones = jnp.ones((ONES_ROWS, values.shape[1]), BF16)
+    both = dot(jnp.concatenate([values, ones], axis=0), weights)
+    both, total = both[:width], both[width : width + 1]
+    first = lax.broadcasted_iota(jnp.int32, (width, count), 0) < width // 2
+    return [jnp.where(first, a[:, :count], a[:, count:]) for a in (both, total, top)]
+
+
+def in_turn(items, ahead, lag, score, weigh, finish):
     scored, weighed = [], []
-    for i in range(len(items) + AHEAD + lag):
+    for i in range(len(items) + ahead + lag):
         if i < len(items):
             scored.append(score(items[i]))
-        if AHEAD <= i < len(items) + AHEAD:
-            weighed.append(weigh(items[i - AHEAD], scored[i - AHEAD]))
-        if i >= AHEAD + lag:
-            finish(items[i - AHEAD - lag], weighed[i - AHEAD - lag])
+        if ahead <= i < len(items) + ahead:
+            weighed.append(weigh(items[i - ahead], scored[i - ahead]))
+        if i >= ahead + lag:
+            finish(items[i - ahead - lag], weighed[i - ahead - lag])
 
 
 def project_kernel(
@@ -218,15 +244,15 @@
                 copy.start()
 
     items = [(p, row) for p in range(pairs) for row in range(0, rows, OWN_ROWS)]
-    in_turn(items, OWN_LAG, score, lambda _, s: pair_weigh(s, []), finish)
+    in_turn(items, AHEAD, OWN_LAG, score, lambda _, s: pair_weigh(s, []), finish)
     for group in outs:
         for copy in group:
             copy.wait()
 
 
 def window_bias(count, rows, span, left_ok, right_ok, first):
-    query = first + lax.broadcasted_iota(jnp.int32, (count, span), 0)
-    key = first + lax.broadcasted_iota(jnp.int32, (count, span), 1)
+    key = first + lax.broadcasted_iota(jnp.int32, (span, 2 * count), 0)
+    query = first + lax.broadcasted_iota(jnp.int32, (span, 2 * count), 1) % count
     position = jnp.where(key < rows, key - rows, key)
     near = jnp.abs(position - query) <= HALF
     there = jnp.where(key < rows, left_ok, right_ok) > 0
@@ -282,12 +308,13 @@
         here = slice(first, first + LN_ROWS)
         normalise(far_ref, here, gain_ref[...])
 
+    for first in range(0, 2 * model, FAR_COLS):
+        cols = slice(first, first + FAR_COLS)
+        kv_ref[far_at, cols] = dot(far_ref[...], w_ref[:, model + cols.start : model + cols.stop]).astype(BF16)
+
     masks = halves(pair)
     for step in range(steps):
         later = step_copies[step + 1] if step + 1 < steps else []
-        for side in range(2):
-            cols = slice(side * model + step * width, side * model + (step + 1) * width)
-            kv_ref[far_at, cols] = dot(far_ref[...], w_ref[:, model + cols.start : model + cols.stop]).astype(BF16)
         for copy in step_copies[step]:
             copy.wait()
         for copy in later:
@@ -296,7 +323,7 @@
 
         @pl.loop(0, STEP_PAIRS // LOOP_PAIRS)
         def _(turn, step=step, full=full):
-            sides = {}
+            values = {}
 
             def window(part):
                 left, right = slice(part * FAR_ROWS, rows), slice(2 * rows, 2 * rows + (part + 1) * FAR_ROWS)
@@ -309,36 +336,36 @@
             def score(item):
                 p, part = item
                 if part == 0:
-                    sides[p] = (
-                        [kv_ref[:, columns(p)] * mask for mask in masks],
-                        value_sides(kv_ref[:, columns(p, model)], masks),
-                    )
-                keys = [k[w] for k in sides[p][0] for w in window(part)]
+                    values[p] = kv_ref[:, columns(p, model)].T
+                keys = jnp.concatenate([kv_ref[w, columns(p)] for w in window(part)], axis=0)
                 queries = q_ref[part * FAR_ROWS : (part + 1) * FAR_ROWS, columns(p)]
-                return dot_nt(queries, jnp.concatenate(keys, axis=0))
+                return dot_nt(keys, jnp.concatenate([queries * mask for mask in masks], axis=0))
 
             def weigh(item, scores):
                 bias = bias_ref[item[1]]
                 if full:
                     reach = rows - item[1] * FAR_ROWS
-                    bias = jnp.concatenate([bias[:, :reach], jnp.zeros((FAR_ROWS, rows), F32), bias[:, reach:]], axis=1)
-                return pair_weigh(scores, [(0, bias)])
+                    return tall_weigh(scores, [(0, bias[:reach]), (reach + rows, bias[reach:])])
+                return tall_weigh(scores, [(0, bias)])
 
             def finish(item, weighed):
                 p, part = item
                 here = slice(part * FAR_ROWS, (part + 1) * FAR_ROWS)
-                values = [v[w] for v in sides[p][1] for w in window(part)]
-                sums, totals, top = pair_sums(*weighed, jnp.concatenate(values, axis=0))
-                if not full:
-                    kept = columns(p, -FULL_STEPS * width)
-                    own_top = top_ref[here, kept]
-                    best = jnp.maximum(top, own_top)
-                    scale, own_scale = jnp.exp(top - best), jnp.exp(own_top - best)
-                    sums = sums * scale + sum_ref[here, kept] * own_scale
-                    totals = totals * scale + total_ref[here, kept] * own_scale
+                there = jnp.concatenate([values[p][:, w] for w in window(part)], axis=1)
+                sums, totals, top = tall_sums(*weighed, there)
+                if full:
+                    context_ref[here, columns(p)] = (sums / totals).T.astype(BF16)
+                    return
+                sums, totals, top = sums.T, totals.T, top.T
+                kept = columns(p, -FULL_STEPS * width)
+                own_top = top_ref[here, kept]
+                best = jnp.maximum(top, own_top)
+                scale, own_scale = jnp.exp(top - best), jnp.exp(own_top - best)
+                sums = sums * scale + sum_ref[here, kept] * own_scale
+                totals = totals * scale + total_ref[here, kept] * own_scale
                 context_ref[here, columns(p)] = (sums / totals).astype(BF16)
 
-            in_turn([(p, part) for p in range(LOOP_PAIRS) for part in range(parts)], FAR_LAG, score, weigh, finish)
+            in_turn([(p, part) for p in range(LOOP_PAIRS) for part in range(parts)], FAR_AHEAD, FAR_LAG, score, weigh, finish)
 
     processed = (x_ref[...].astype(F32) + dot(context_ref[...], wout_ref[...])).astype(BF16)
     fields = dot_nt(wdec_ref[...], processed)
@@ -348,11 +375,14 @@
     fields_high = fields.astype(BF16)
     fields_low = (fields - fields_high.astype(F32)).astype(BF16)
     both = jnp.concatenate([fields_high, fields_low], axis=0)
-    for d in range(out_ref.shape[0]):
-        cols = slice(d * each, (d + 1) * each)
+    points = high_ref.shape[1]
+    for first in range(0, points, DECODE_COLS):
+        cols = slice(first, first + DECODE_COLS)
         product = dot(both, high_ref[:, cols])
         decoded = product[:tall] + product[tall:] + dot(fields_high, low_ref[:, cols])
-        out_ref[d] = decoded[:variables].astype(BF16)
+        decoded = decoded[:variables].astype(BF16)
+        for at in range(0, DECODE_COLS, each):
+            out_ref[(first + at) // each] = decoded[:, at : at + each]
 
 
 def score_kernel(members, coeff, fields_ref, truth_ref, out_ref):
@@ -440,7 +470,7 @@
             held(BF16), pltpu.VMEM((3 * rows, 2 * model), BF16), held(BF16),
             held(F32, sums.shape[1]), held(F32, sums.shape[1]), held(F32, sums.shape[1]),
             held(BF16, points), held(BF16, points),
-            pltpu.VMEM((rows // FAR_ROWS, FAR_ROWS, span), F32), held(BF16), pltpu.SemaphoreType.DMA,
+            pltpu.VMEM((rows // FAR_ROWS, span, 2 * FAR_ROWS), F32), held(BF16), pltpu.SemaphoreType.DMA,
             pltpu.SemaphoreType.DMA((steps, 6)),
         ],
         compiler_params=pltpu.CompilerParams(vmem_limit_bytes=SHARED_LIMIT),

time: 58.8 us -> 58.6 us (level)
  no operation moved by 1% of the time
where the time goes in v6:
time: 58.6 us; the launch traced here: 58.4 us
  Pallas kernels  34.4 us (59%)
  blocking collectives  18.8 us (32%)
  starting transfers between devices  5.03 us (9%)
    pallas_call x1, Pallas kernels, far_attention(): pl.pallas_call(functools.partial(far_kernel, model // HEADS), in_specs=[I...  19.1 us
    all_to_all x1, blocking collectives, shards(): lax.all_to_all(decoded, 'ens', split_axis=1, concat_axis=0, tiled=True)  18.8 us
    pallas_call x1, Pallas kernels, project(): pl.pallas_call(functools.partial(project_kernel, model // HEADS), in_spec...  7.67 us
    pallas_call x1, Pallas kernels, own_attention(): pl.pallas_call(functools.partial(own_kernel, model // HEADS), in_specs=[I...  5.59 us
    ppermute x2, starting transfers between devices, exchange(): return lax.ppermute(value, 'mp', pairs + [(j, i) for i, j in pairs])  5.03 us
    pallas_call x1, Pallas kernels, shards(): pl.pallas_call(functools.partial(score_kernel, members, coeff), out_shape...  2.08 us
  transfers between devices with their start and end apart: 2, of which 0 were waited for; matrix products, arithmetic and copies ran while one was open for 0% of the time, Pallas kernels for 23%

profile of v6, /device:TPU:0, one launch (start us, length us, event | category | flops | bytes accessed | tf_op | source)
XLA Modules:
  0.0 58.4 jit_solution(13415928048295308762)
XLA Ops:
  0.0 1.6 %collective-permute-start = (bf16[1,512,1024]{2,1,0:T(8,128)(2,1)}, bf16[1,512,1024]{2,1,0:T(8,128)(2,1)}, u32[]{:S(2)}, u32[]{:S(2)}) collective-permute-start(bf16[1,512,1024]{2,1,0:T(8,128)(2,1)} %param.8), channel_id=1, source_target_pairs={{1,2},{2,1},{5,6},{6,5},{9,10},{10,9},{13,14},{14,13},{17,18},{18,... | collective-permute-start | bytes 3145736 | tf_op jit(solution)/shard_map/ppermute | solution.py:410
  1.6 7.7 %project.1 = (bf16[512,1024]{1,0:T(8,128)(2,1)}, bf16[512,2048]{1,0:T(8,128)(2,1)}) custom-call(bf16[512,1024]{1,0:T(8,128)(2,1)} %bitcast.7, bf16[1024,3072]{1,0:T(8,128)(2,1)} %w_ref.1, f32[1,1024]{1,0:T(1,128)} %bitcast.9), custom_call_target="tpu_custom_call" | custom-call | flops 1099511627776 | bytes 1048576 | tf_op jit(solution)/shard_map/project/pallas_call | solution.py:416
  9.3 3.4 %collective-permute-start.1 = (bf16[512,2048]{1,0:T(8,128)(2,1)}, bf16[512,2048]{1,0:T(8,128)(2,1)}, u32[]{:S(2)}, u32[]{:S(2)}) collective-permute-start(bf16[512,2048]{1,0:T(8,128)(2,1)} %get-tuple-element.10.kv_hbm.own_kv_hbm), channel_id=1, source_target_pairs={{0,1},{2,3},{1,0},{3,2},{4,5},{6,7},{5,4},{7,6},{8,9},{10,11},{9,8... | collective-permute-start | bytes 6291464 | tf_op jit(solution)/shard_map/ppermute | solution.py:410
  12.7 0.0 copy-start
  12.7 0.0 copy-start.1
  12.7 0.0 copy-start.2
  12.7 0.0 copy-start.3
  12.7 0.0 copy-start.4
  12.7 0.0 copy-start.5
  12.7 0.0 copy-start.6
  12.8 5.6 %own_tokens.1 = (f32[512,512]{1,0:T(8,128)}, f32[512,512]{1,0:T(8,128)}, f32[512,512]{1,0:T(8,128)}) custom-call(bf16[512,1024]{1,0:T(8,128)(2,1)} %get-tuple-element.11.q_hbm, bf16[512,2048]{1,0:T(8,128)(2,1)} %get-tuple-element.10.kv_hbm.own_kv_hbm), custom_call_target="tpu_custom_call" | custom-call | flops 1099511627776 | bytes 1048576 | tf_op jit(solution)/shard_map/own_tokens/pallas_call | solution.py:442
  18.4 0.0 collective-permute-done
  18.4 0.0 collective-permute-done.1.chip_kv_hbm
  18.4 0.0 copy-done
  18.4 0.0 copy-done.1
  18.4 0.0 copy-done.2
  18.4 0.0 copy-done.3
  18.4 0.0 copy-done.4
  18.4 0.0 copy-done.5
  18.4 0.0 copy-done.6
  18.4 19.1 %neighbour_tokens.1 = bf16[8,100,256]{2,1,0:T(8,128)(2,1)} custom-call(bf16[512,1024]{1,0:T(8,128)(2,1)} %bitcast.far_hbm, bf16[512,2048]{1,0:T(8,128)(2,1)} %collective-permute-done.1.chip_kv_hbm, bf16[512,2048]{1,0:T(8,128)(2,1)} %get-tuple-element.10.kv_hbm.own_kv_hbm, bf16[512,1024]{1,0:T(8,128)(2,1)} %get-tuple-element.11.q_hbm, ...), custom_call_target="tpu_custom_call" | custom-call | flops 1099511627776 | bytes 1048576 | tf_op jit(solution)/shard_map/neighbour_tokens/pallas_call | solution.py:464
  37.5 18.8 %all_to_all.4 = bf16[1,8,100,256]{3,2,0,1:T(8,128)(2,1)} all-to-all(bf16[1,8,100,256]{3,2,0,1:T(8,128)(2,1)} %bitcast.12), channel_id=1, replica_groups=mesh['ens'=8,'mp'=4] {'ens'}, dimensions={1} | all-to-all | bytes 819200 | tf_op jit(solution)/shard_map/all_to_all | solution.py:503
  56.3 2.1 %scores.1 = f32[100,256]{1,0:T(8,128)} custom-call(bf16[8,100,256]{2,1,0:T(8,128)(2,1)} %bitcast.11, f32[100,256]{1,0:T(8,128)} %truth_ref.1), custom_call_target="tpu_custom_call" | custom-call | tf_op jit(solution)/shard_map/scores/pallas_call | solution.py:507
Async XLA Ops:
  0.0 18.4 %collective-permute-start = (bf16[1,512,1024]{2,1,0:T(8,128)(2,1)}, bf16[1,512,1024]{2,1,0:T(8,128)(2,1)}, u32[]{:S(2)}, u32[]{:S(2)}) collective-permute-start(bf16[1,512,1024]{2,1,0:T(8,128)(2,1)} %param.8), channel_id=1, source_target_pairs={{1,2},{2,1},{5,6},{6,5},{9,10},{10,9},{13,14},{14,13},{17,18},{18,... | collective-permute-start | bytes 3145736 | tf_op jit(solution)/shard_map/ppermute | solution.py:410
  9.3 9.1 %collective-permute-start.1 = (bf16[512,2048]{1,0:T(8,128)(2,1)}, bf16[512,2048]{1,0:T(8,128)(2,1)}, u32[]{:S(2)}, u32[]{:S(2)}) collective-permute-start(bf16[512,2048]{1,0:T(8,128)(2,1)} %get-tuple-element.10.kv_hbm.own_kv_hbm), channel_id=1, source_target_pairs={{0,1},{2,3},{1,0},{3,2},{4,5},{6,7},{5,4},{7,6},{8,9},{10,11},{9,8... | collective-permute-start | bytes 6291464 | tf_op jit(solution)/shard_map/ppermute | solution.py:410
  12.7 5.7 %copy-start = (bf16[1024,3072]{1,0:T(8,128)(2,1)S(1)}, bf16[1024,3072]{1,0:T(8,128)(2,1)}, u32[]{:S(2)}) copy-start(bf16[1024,3072]{1,0:T(8,128)(2,1)} %w_ref.1) | copy-start | bytes 18874372
  12.7 5.7 %copy-start.1 = (bf16[1024,1024]{1,0:T(8,128)(2,1)S(1)}, bf16[1024,1024]{1,0:T(8,128)(2,1)}, u32[]{:S(2)}) copy-start(bf16[1024,1024]{1,0:T(8,128)(2,1)} %wout_ref.1) | copy-start | bytes 6291460
  12.7 5.7 %copy-start.2 = (bf16[1,512,1024]{2,1,0:T(8,128)(2,1)S(1)}, bf16[1,512,1024]{2,1,0:T(8,128)(2,1)}, u32[]{:S(2)}) copy-start(bf16[1,512,1024]{2,1,0:T(8,128)(2,1)} %param.8) | copy-start | bytes 3145732
  12.7 5.7 %copy-start.3 = (bf16[100,1024]{1,0:T(8,128)(2,1)S(1)}, bf16[100,1024]{1,0:T(8,128)(2,1)}, u32[]{:S(2)}) copy-start(bf16[100,1024]{1,0:T(8,128)(2,1)} %wdec_ref.1) | copy-start | bytes 614404
  12.7 5.7 %copy-start.4 = (s32[4,2048]{1,0:T(4,128)S(1)}, s32[4,2048]{1,0:T(4,128)}, u32[]{:S(2)}) copy-start(s32[4,2048]{1,0:T(4,128)} %near_ref.1) | copy-start | bytes 98308
  12.7 5.7 %copy-start.5 = (f32[4,2048]{1,0:T(4,128)S(1)}, f32[4,2048]{1,0:T(4,128)}, u32[]{:S(2)}) copy-start(f32[4,2048]{1,0:T(4,128)} %edge_ref.1) | copy-start | bytes 98308
  12.7 5.7 %copy-start.6 = (f32[1024]{0:T(1024)S(1)}, f32[1024]{0:T(1024)}, u32[]{:S(2)}) copy-start(f32[1024]{0:T(1024)} %param.9) | copy-start | bytes 12292

commit v7 on v6

--- a/solution.py
+++ b/solution.py
@@ -507,6 +507,7 @@
     return pl.pallas_call(
         functools.partial(score_kernel, members, coeff),
         out_shape=jax.ShapeDtypeStruct(truth.shape, F32),
+        compiler_params=pltpu.CompilerParams(vmem_limit_bytes=16 * MIB),
         name="scores",
     )(gathered, truth)
 

time: 58.6 us -> 57.5 us (0.981)
  Pallas kernels: 34.4 us -> 33.4 us
    pallas_call x1, Pallas kernels: 2.08 us -> 1.06 us  [shards(): pl.pallas_call(functools.partial(score_kernel, members, coeff), out_shape...]
where the time goes in v7:
time: 57.5 us; the launch traced here: 57.3 us
  Pallas kernels  33.4 us (58%)
  blocking collectives  18.7 us (33%)
  starting transfers between devices  5.03 us (9%)
    pallas_call x1, Pallas kernels, far_attention(): pl.pallas_call(functools.partial(far_kernel, model // HEADS), in_specs=[I...  19.1 us
    all_to_all x1, blocking collectives, shards(): lax.all_to_all(decoded, 'ens', split_axis=1, concat_axis=0, tiled=True)  18.7 us
    pallas_call x1, Pallas kernels, project(): pl.pallas_call(functools.partial(project_kernel, model // HEADS), in_spec...  7.67 us
    pallas_call x1, Pallas kernels, own_attention(): pl.pallas_call(functools.partial(own_kernel, model // HEADS), in_specs=[I...  5.59 us
    ppermute x2, starting transfers between devices, exchange(): return lax.ppermute(value, 'mp', pairs + [(j, i) for i, j in pairs])  5.03 us
  transfers between devices with their start and end apart: 2, of which 0 were waited for; matrix products, arithmetic and copies ran while one was open for 0% of the time, Pallas kernels for 23%

profile of v7, /device:TPU:0, one launch (start us, length us, event | category | flops | bytes accessed | tf_op | source)
XLA Modules:
  0.0 57.3 jit_solution(8991787965696174022)
XLA Ops:
  0.0 1.6 %collective-permute-start = (bf16[1,512,1024]{2,1,0:T(8,128)(2,1)}, bf16[1,512,1024]{2,1,0:T(8,128)(2,1)}, u32[]{:S(2)}, u32[]{:S(2)}) collective-permute-start(bf16[1,512,1024]{2,1,0:T(8,128)(2,1)} %param.8), channel_id=1, source_target_pairs={{1,2},{2,1},{5,6},{6,5},{9,10},{10,9},{13,14},{14,13},{17,18},{18,... | collective-permute-start | bytes 3145736 | tf_op jit(solution)/shard_map/ppermute | solution.py:410
  1.6 7.7 %project.1 = (bf16[512,1024]{1,0:T(8,128)(2,1)}, bf16[512,2048]{1,0:T(8,128)(2,1)}) custom-call(bf16[512,1024]{1,0:T(8,128)(2,1)} %bitcast.8, bf16[1024,3072]{1,0:T(8,128)(2,1)} %w_ref.1, f32[1,1024]{1,0:T(1,128)} %bitcast.10), custom_call_target="tpu_custom_call" | custom-call | flops 1099511627776 | bytes 1048576 | tf_op jit(solution)/shard_map/project/pallas_call | solution.py:416
  9.3 3.4 %collective-permute-start.1 = (bf16[512,2048]{1,0:T(8,128)(2,1)}, bf16[512,2048]{1,0:T(8,128)(2,1)}, u32[]{:S(2)}, u32[]{:S(2)}) collective-permute-start(bf16[512,2048]{1,0:T(8,128)(2,1)} %get-tuple-element.10.kv_hbm.own_kv_hbm), channel_id=1, source_target_pairs={{0,1},{2,3},{1,0},{3,2},{4,5},{6,7},{5,4},{7,6},{8,9},{10,11},{9,8... | collective-permute-start | bytes 6291464 | tf_op jit(solution)/shard_map/ppermute | solution.py:410
  12.7 0.0 copy-start.1
  12.7 0.0 copy-start.2
  12.7 0.0 copy-start.3
  12.7 0.0 copy-start.4
  12.7 0.0 copy-start.5
  12.7 0.0 copy-start.6
  12.7 0.0 copy-start.7
  12.8 5.6 %own_tokens.1 = (f32[512,512]{1,0:T(8,128)}, f32[512,512]{1,0:T(8,128)}, f32[512,512]{1,0:T(8,128)}) custom-call(bf16[512,1024]{1,0:T(8,128)(2,1)} %get-tuple-element.11.q_hbm, bf16[512,2048]{1,0:T(8,128)(2,1)} %get-tuple-element.10.kv_hbm.own_kv_hbm), custom_call_target="tpu_custom_call" | custom-call | flops 1099511627776 | bytes 1048576 | tf_op jit(solution)/shard_map/own_tokens/pallas_call | solution.py:442
  18.4 0.0 collective-permute-done
  18.4 0.0 collective-permute-done.1.chip_kv_hbm
  18.4 0.0 copy-done.1
  18.4 0.0 copy-done.2
  18.4 0.0 copy-done.3
  18.4 0.0 copy-done.4
  18.4 0.0 copy-done.5
  18.4 0.0 copy-done.6
  18.4 0.0 copy-done.7
  18.5 0.0 copy-start
  18.5 19.1 %neighbour_tokens.1 = bf16[8,100,256]{2,1,0:T(8,128)(2,1)} custom-call(bf16[512,1024]{1,0:T(8,128)(2,1)} %bitcast.far_hbm, bf16[512,2048]{1,0:T(8,128)(2,1)} %collective-permute-done.1.chip_kv_hbm, bf16[512,2048]{1,0:T(8,128)(2,1)} %get-tuple-element.10.kv_hbm.own_kv_hbm, bf16[512,1024]{1,0:T(8,128)(2,1)} %get-tuple-element.11.q_hbm, ...), custom_call_target="tpu_custom_call" | custom-call | flops 1099511627776 | bytes 1048576 | tf_op jit(solution)/shard_map/neighbour_tokens/pallas_call | solution.py:464
  37.5 18.7 %all_to_all.4 = bf16[1,8,100,256]{3,2,0,1:T(8,128)(2,1)S(1)} all-to-all(bf16[1,8,100,256]{3,2,0,1:T(8,128)(2,1)} %bitcast.12), channel_id=1, replica_groups=mesh['ens'=8,'mp'=4] {'ens'}, dimensions={1} | all-to-all | bytes 819200 | tf_op jit(solution)/shard_map/all_to_all | solution.py:503
  56.2 0.0 copy-done
  56.2 1.1 %scores.1 = f32[100,256]{1,0:T(8,128)} custom-call(bf16[8,100,256]{2,1,0:T(8,128)(2,1)S(1)} %bitcast.7, f32[100,256]{1,0:T(8,128)S(1)} %copy-done), custom_call_target="tpu_custom_call" | custom-call | tf_op jit(solution)/shard_map/scores/pallas_call | solution.py:507
Async XLA Ops:
  0.0 18.4 %collective-permute-start = (bf16[1,512,1024]{2,1,0:T(8,128)(2,1)}, bf16[1,512,1024]{2,1,0:T(8,128)(2,1)}, u32[]{:S(2)}, u32[]{:S(2)}) collective-permute-start(bf16[1,512,1024]{2,1,0:T(8,128)(2,1)} %param.8), channel_id=1, source_target_pairs={{1,2},{2,1},{5,6},{6,5},{9,10},{10,9},{13,14},{14,13},{17,18},{18,... | collective-permute-start | bytes 3145736 | tf_op jit(solution)/shard_map/ppermute | solution.py:410
  9.3 9.1 %collective-permute-start.1 = (bf16[512,2048]{1,0:T(8,128)(2,1)}, bf16[512,2048]{1,0:T(8,128)(2,1)}, u32[]{:S(2)}, u32[]{:S(2)}) collective-permute-start(bf16[512,2048]{1,0:T(8,128)(2,1)} %get-tuple-element.10.kv_hbm.own_kv_hbm), channel_id=1, source_target_pairs={{0,1},{2,3},{1,0},{3,2},{4,5},{6,7},{5,4},{7,6},{8,9},{10,11},{9,8... | collective-permute-start | bytes 6291464 | tf_op jit(solution)/shard_map/ppermute | solution.py:410
  12.7 5.7 %copy-start.1 = (bf16[1024,3072]{1,0:T(8,128)(2,1)S(1)}, bf16[1024,3072]{1,0:T(8,128)(2,1)}, u32[]{:S(2)}) copy-start(bf16[1024,3072]{1,0:T(8,128)(2,1)} %w_ref.1) | copy-start | bytes 18874372
  12.7 5.7 %copy-start.2 = (bf16[1024,1024]{1,0:T(8,128)(2,1)S(1)}, bf16[1024,1024]{1,0:T(8,128)(2,1)}, u32[]{:S(2)}) copy-start(bf16[1024,1024]{1,0:T(8,128)(2,1)} %wout_ref.1) | copy-start | bytes 6291460
  12.7 5.7 %copy-start.3 = (bf16[1,512,1024]{2,1,0:T(8,128)(2,1)S(1)}, bf16[1,512,1024]{2,1,0:T(8,128)(2,1)}, u32[]{:S(2)}) copy-start(bf16[1,512,1024]{2,1,0:T(8,128)(2,1)} %param.8) | copy-start | bytes 3145732
  12.7 5.7 %copy-start.4 = (bf16[100,1024]{1,0:T(8,128)(2,1)S(1)}, bf16[100,1024]{1,0:T(8,128)(2,1)}, u32[]{:S(2)}) copy-start(bf16[100,1024]{1,0:T(8,128)(2,1)} %wdec_ref.1) | copy-start | bytes 614404
  12.7 5.7 %copy-start.5 = (s32[4,2048]{1,0:T(4,128)S(1)}, s32[4,2048]{1,0:T(4,128)}, u32[]{:S(2)}) copy-start(s32[4,2048]{1,0:T(4,128)} %near_ref.1) | copy-start | bytes 98308
  12.7 5.7 %copy-start.6 = (f32[4,2048]{1,0:T(4,128)S(1)}, f32[4,2048]{1,0:T(4,128)}, u32[]{:S(2)}) copy-start(f32[4,2048]{1,0:T(4,128)} %edge_ref.1) | copy-start | bytes 98308
  12.7 5.7 %copy-start.7 = (f32[1024]{0:T(1024)S(1)}, f32[1024]{0:T(1024)}, u32[]{:S(2)}) copy-start(f32[1024]{0:T(1024)} %param.9) | copy-start | bytes 12292
  18.5 37.8 %copy-start = (f32[100,256]{1,0:T(8,128)S(1)}, f32[100,256]{1,0:T(8,128)}, u32[]{:S(2)}) copy-start(f32[100,256]{1,0:T(8,128)} %truth_ref.1) | copy-start | bytes 307204
